TPU v7x, 32 devices: a whole 2x2x4 slice. The times are simulated.
32 devices in a mesh: batch: 16 (over z, y, core), seq: 2 (over x).
Axes of the slice: x: 2, y: 2, z: 4, core: 2. Of those that a mesh axis runs over, the one named last changes fastest.
Arguments:
- tokens: bfloat16 [16, 1664, 1152], P('batch', 'seq'), may hold values from -6 to 6
- skip_parts: bfloat16 [2, 16, 1664, 1152], P('seq', 'batch'), may hold values from -4 to 4
- lengths: int32 [16, 4], P('batch'), may hold values from 0 to 1026, as said below
- cotangent: bfloat16 [16, 1664, 1152], P('batch', 'seq'), may hold values from -6 to 6
- skip_w: bfloat16 [2304, 1152], P('batch'), may hold values from -0.125 to 0.125
- qkv_w: bfloat16 [1152, 3456], P('batch'), may hold values from -0.1875 to 0.1875
- proj_w: bfloat16 [1152, 1152], P('batch'), may hold values from -0.75 to 0.75
- fc1_w: bfloat16 [1152, 4608], P('batch'), may hold values from -0.1875 to 0.1875
- fc2_w: bfloat16 [4608, 1152], P('batch'), may hold values from -0.125 to 0.125
- skip_bias: float32 [1152], replicated, may hold values from -2 to 2
- ln1_gain: float32 [1152], replicated, may hold values from 0.25 to 1.75
- ln1_bias: float32 [1152], replicated, may hold values from -2 to 2
- proj_bias: float32 [1152], replicated, may hold values from -2 to 2
- ln2_gain: float32 [1152], replicated, may hold values from 0.25 to 1.75
- ln2_bias: float32 [1152], replicated, may hold values from -2 to 2
- fc1_bias: float32 [4608], replicated, may hold values from -2 to 2
- fc2_bias: float32 [1152], replicated, may hold values from -2 to 2
Outputs:
- output: bfloat16 [16, 1664, 1152], P('batch', 'seq')
- d_tokens: float32 [16, 1664, 1152], P('batch', 'seq')
- d_skip: float32 [16, 1664, 1152], P('batch', 'seq')
- d_skip_w: float32 [2304, 1152], P('batch')
- d_qkv_w: float32 [1152, 3456], P('batch')
- d_proj_w: float32 [1152, 1152], P('batch')
- d_fc1_w: float32 [1152, 4608], P('batch')
- d_fc2_w: float32 [4608, 1152], P('batch')
- d_skip_bias: float32 [1152], replicated
- d_ln1_gain: float32 [1152], replicated
- d_ln1_bias: float32 [1152], replicated
- d_proj_bias: float32 [1152], replicated
- d_ln2_gain: float32 [1152], replicated
- d_ln2_bias: float32 [1152], replicated
- d_fc1_bias: float32 [4608], replicated
- d_fc2_bias: float32 [1152], replicated
Inputs may be any that keep to these rules, and one draw needn't show every extreme that they name: `lengths`: each row holds in order an item of 258 tokens, an item of 1026 tokens, another of 258 tokens, and an item of 122 tokens in exactly half of the rows (rounded down) or an empty one (0) in the others; the rest of the row is padding.
All inputs are finite; a program needn't handle non-finite values.
Results may differ from a plain program's by a relative error of at most 0.03.
Values may be sent and summed in bfloat16 or wider, within the bound.
No kernel may reach another device: no remote copies, remote signals or barrier semaphores. Data moves between devices by JAX's collectives and lax.ppermute only.
A program may use at most 320 MiB of HBM per device.

v0:
```python
import math

import jax
import jax.numpy as jnp
from jax import lax
from jax.sharding import PartitionSpec as P

HEADS = 16
HD = 72


EPS = 1e-05


def layer_norm(hidden, gain, shift):
    centred = hidden - jnp.mean(hidden, axis=-1, keepdims=True)
    spread = jnp.mean(centred * centred, axis=-1, keepdims=True)
    return centred * lax.rsqrt(spread + EPS) * gain + shift


def exact_gelu(value):
    return jax.nn.gelu(value, approximate=False)


def segment_ids(offsets, positions):
    hits = (positions[None, :, None] >= offsets[:, None, :]).astype(jnp.int32)
    return jnp.sum(hits, axis=-1)


def fwd_dot(left, right):
    return jnp.dot(left, right, preferred_element_type=jnp.float32)


def contract_rows(left, right):
    return lax.dot_general(
        left, right, (((0,), (0,)), ((), ())), preferred_element_type=jnp.float32
    )


def back_dot(grad_rows, weight):
    return lax.dot_general(
        grad_rows, weight, (((1,), (1,)), ((), ())), preferred_element_type=jnp.float32
    )


def per_device(
    tokens,
    skip_parts,
    lengths,
    cotangent,
    skip_w,
    qkv_w,
    proj_w,
    fc1_w,
    fc2_w,
    skip_bias,
    ln1_gain,
    ln1_bias,
    proj_bias,
    ln2_gain,
    ln2_bias,
    fc1_bias,
    fc2_bias,
):
    row_count, local_len, features = tokens.shape
    row_len = local_len * lax.axis_size("seq")
    head_count = HEADS
    head_dim = HD
    score_scale = HD ** (-0.5)
    tok_count = row_count * local_len
    offsets = jnp.cumsum(lengths, axis=1)
    first_pos = lax.axis_index("seq") * local_len
    query_seg = segment_ids(offsets, first_pos + jnp.arange(local_len, dtype=jnp.int32))
    live_mask = (query_seg < lengths.shape[1]).astype(jnp.float32).reshape(tok_count, 1)
    partial_sum = skip_parts[0].astype(jnp.float32)
    skip_rows = lax.psum_scatter(
        partial_sum.astype(jnp.bfloat16), "seq", scatter_dimension=1, tiled=True
    )
    w_skip, w_qkv, w_proj, w_up, w_down = (
        lax.all_gather(skip_w, "batch", axis=0, tiled=True),
        lax.all_gather(qkv_w, "batch", axis=0, tiled=True),
        lax.all_gather(proj_w, "batch", axis=0, tiled=True),
        lax.all_gather(fc1_w, "batch", axis=0, tiled=True),
        lax.all_gather(fc2_w, "batch", axis=0, tiled=True),
    )
    tok_flat = tokens.reshape(tok_count, features)
    skip_flat = skip_rows.reshape(tok_count, features)
    h_zero = (
        fwd_dot(tok_flat, w_skip[:features]) + fwd_dot(skip_flat, w_skip[features:]) + skip_bias
    )
    normed_one, ln1_back = jax.vjp(layer_norm, h_zero, ln1_gain, ln1_bias)
    act_one = normed_one.astype(jnp.bfloat16)
    qkv_all = fwd_dot(act_one, w_qkv).astype(jnp.bfloat16)
    queries = qkv_all[:, :features].reshape(row_count, local_len, head_count, head_dim)
    keyvals = qkv_all[:, features:].reshape(row_count, local_len, 2 * features)

    def split_block(kv_block):
        block_len = kv_block.shape[1]
        key_heads = kv_block[:, :, :features].reshape(row_count, block_len, head_count, head_dim)
        value_heads = kv_block[:, :, features:].reshape(row_count, block_len, head_count, head_dim)
        return (key_heads, value_heads)

    def attend(running, kv_block, key_seg):
        top_old, norm_old, weighted = running
        key_heads, value_heads = split_block(kv_block)
        same_item = query_seg[:, :, None, None] == key_seg[:, None, None, :]
        scores = (
            jnp.einsum("rthd,rkhd->rthk", queries, key_heads, preferred_element_type=jnp.float32)
            * score_scale
        )
        scores = jnp.where(same_item, scores, -1e30)
        top_new = jnp.maximum(top_old, jnp.max(scores, axis=-1))
        expo = jnp.where(same_item, jnp.exp(scores - top_new[..., None]), 0.0)
        factor = jnp.exp(top_old - top_new)
        norm_new = norm_old * factor + jnp.sum(expo, axis=-1)
        weighted = weighted * factor[..., None] + jnp.einsum(
            "rthk,rkhd->rthd",
            expo.astype(jnp.bfloat16),
            value_heads,
            preferred_element_type=jnp.float32,
        )
        return (top_new, norm_new, weighted)

    start_state = (
        jnp.full((row_count, local_len, head_count), -1e30, jnp.float32),
        jnp.zeros((row_count, local_len, head_count), jnp.float32),
        jnp.zeros((row_count, local_len, head_count, head_dim), jnp.float32),
    )
    kv_piece = lax.all_gather(keyvals, "seq", axis=1, tiled=True)
    piece_len = kv_piece.shape[1]
    block_len = piece_len

    def step(block_index, totals):
        first_key = block_index * block_len
        key_seg = segment_ids(offsets, first_key + jnp.arange(block_len, dtype=jnp.int32))
        return attend(totals, kv_piece, key_seg)

    top_final, norm_final, weighted = lax.fori_loop(0, piece_len // block_len, step, start_state)
    attended = weighted / norm_final[..., None]
    log_total = top_final + jnp.log(norm_final)
    att_low = attended.reshape(tok_count, features).astype(jnp.bfloat16)
    h_one = h_zero + fwd_dot(att_low, w_proj) + proj_bias
    normed_two, ln2_back = jax.vjp(layer_norm, h_one, ln2_gain, ln2_bias)
    act_two = normed_two.astype(jnp.bfloat16)
    up_proj = fwd_dot(act_two, w_up) + fc1_bias
    gelu_out, gelu_back = jax.vjp(exact_gelu, up_proj)
    gelu_low = gelu_out.astype(jnp.bfloat16)
    h_two = h_one + fwd_dot(gelu_low, w_down) + fc2_bias
    output = (h_two * live_mask).astype(jnp.bfloat16).reshape(row_count, local_len, features)
    grad_two = cotangent.reshape(tok_count, features).astype(jnp.float32) * live_mask
    grad_low = grad_two.astype(jnp.bfloat16)
    d_w_down = contract_rows(gelu_low, grad_low)
    d_gelu = back_dot(grad_low, w_down)
    d_up = gelu_back(d_gelu)[0]
    up_low = d_up.astype(jnp.bfloat16)
    d_w_up = contract_rows(act_two, up_low)
    d_act_two = back_dot(up_low, w_up)
    d_h_one, d_ln2_gain, d_ln2_bias = ln2_back(d_act_two)
    d_h_one = d_h_one + grad_two
    proj_low = d_h_one.astype(jnp.bfloat16)
    d_w_proj = contract_rows(att_low, proj_low)
    d_att = (
        back_dot(proj_low, w_proj)
        .astype(jnp.bfloat16)
        .reshape(row_count, local_len, head_count, head_dim)
    )
    row_dot = jnp.sum(d_att.astype(jnp.float32) * attended, axis=-1)
    kv_whole = lax.all_gather(keyvals, "seq", axis=1, tiled=True)
    back_len = math.gcd(row_len, 512)
    d_query_start = jnp.zeros((row_count, local_len, head_count, head_dim), jnp.float32)

    def query_grads(kv_block, key_seg, d_query):
        key_heads, value_heads = split_block(kv_block)
        same_item = query_seg[:, :, None, None] == key_seg[:, None, None, :]
        scores = (
            jnp.einsum("rthd,rkhd->rthk", queries, key_heads, preferred_element_type=jnp.float32)
            * score_scale
        )
        weights = jnp.where(same_item, jnp.exp(scores - log_total[..., None]), 0.0)
        d_weights = jnp.einsum(
            "rthd,rkhd->rthk", d_att, value_heads, preferred_element_type=jnp.float32
        )
        d_scores = (weights * (d_weights - row_dot[..., None])).astype(jnp.bfloat16)
        d_query = (
            d_query
            + jnp.einsum("rthk,rkhd->rthd", d_scores, key_heads, preferred_element_type=jnp.float32)
            * score_scale
        )
        return (d_query, weights, d_scores, key_heads)

    def back_step(block_index, totals):
        first_key = block_index * back_len
        kv_block = lax.dynamic_slice_in_dim(kv_whole, first_key, back_len, 1)
        key_seg = segment_ids(offsets, first_key + jnp.arange(back_len, dtype=jnp.int32))
        d_query, d_keyvals = totals
        d_query, weights, d_scores, key_heads = query_grads(kv_block, key_seg, d_query)
        d_key = (
            jnp.einsum("rthk,rthd->rkhd", d_scores, queries, preferred_element_type=jnp.float32)
            * score_scale
        )
        d_value = jnp.einsum(
            "rthk,rthd->rkhd",
            weights.astype(jnp.bfloat16),
            d_att,
            preferred_element_type=jnp.float32,
        )
        key_grads = jnp.concatenate(
            [
                d_key.reshape(row_count, back_len, features),
                d_value.reshape(row_count, back_len, features),
            ],
            axis=2,
        )
        return (d_query, lax.dynamic_update_slice_in_dim(d_keyvals, key_grads, first_key, 1))

    back_start = (d_query_start, jnp.zeros((row_count, row_len, 2 * features), jnp.float32))
    d_query, d_keyvals = lax.fori_loop(0, row_len // back_len, back_step, back_start)
    d_kv_own = lax.psum_scatter(
        d_keyvals.astype(jnp.bfloat16), "seq", scatter_dimension=1, tiled=True
    ).astype(jnp.float32)
    d_qkv = jnp.concatenate(
        [d_query.reshape(tok_count, features), d_kv_own.reshape(tok_count, 2 * features)], axis=1
    ).astype(jnp.bfloat16)
    d_w_qkv = contract_rows(act_one, d_qkv)
    d_act_one = back_dot(d_qkv, w_qkv)
    d_h_zero, d_ln1_gain, d_ln1_bias = ln1_back(d_act_one)
    d_h_zero = d_h_zero + d_h_one
    zero_low = d_h_zero.astype(jnp.bfloat16)
    d_w_skip = jnp.concatenate(
        [contract_rows(tok_flat, zero_low), contract_rows(skip_flat, zero_low)], axis=0
    )
    d_tokens = back_dot(zero_low, w_skip[:features]).reshape(row_count, local_len, features)
    d_skip = back_dot(zero_low, w_skip[features:]).reshape(row_count, local_len, features)
    vector_sums = lax.psum(
        (
            jnp.sum(d_h_zero, axis=0),
            d_ln1_gain,
            d_ln1_bias,
            jnp.sum(d_h_one, axis=0),
            d_ln2_gain,
            d_ln2_bias,
            jnp.sum(d_up, axis=0),
            jnp.sum(grad_two, axis=0),
        ),
        ("batch", "seq"),
    )
    full_grads = (d_w_skip, d_w_qkv, d_w_proj, d_w_up, d_w_down)
    row_parts = (
        lax.psum_scatter(
            full_grads[0].astype(jnp.bfloat16), "batch", scatter_dimension=0, tiled=True
        ).astype(jnp.float32),
        lax.psum_scatter(
            full_grads[1].astype(jnp.bfloat16), "batch", scatter_dimension=0, tiled=True
        ).astype(jnp.float32),
        lax.psum_scatter(
            full_grads[2].astype(jnp.bfloat16), "batch", scatter_dimension=0, tiled=True
        ).astype(jnp.float32),
        lax.psum_scatter(
            full_grads[3].astype(jnp.bfloat16), "batch", scatter_dimension=0, tiled=True
        ).astype(jnp.float32),
        lax.psum_scatter(
            full_grads[4].astype(jnp.bfloat16), "batch", scatter_dimension=0, tiled=True
        ).astype(jnp.float32),
    )
    weight_grads = (
        lax.psum(row_parts[0].astype(jnp.bfloat16), "seq").astype(jnp.float32),
        lax.psum(row_parts[1].astype(jnp.bfloat16), "seq").astype(jnp.float32),
        lax.psum(row_parts[2].astype(jnp.bfloat16), "seq").astype(jnp.float32),
        lax.psum(row_parts[3].astype(jnp.bfloat16), "seq").astype(jnp.float32),
        lax.psum(row_parts[4].astype(jnp.bfloat16), "seq").astype(jnp.float32),
    )
    return (
        output,
        d_tokens,
        d_skip,
        weight_grads[0],
        weight_grads[1],
        weight_grads[2],
        weight_grads[3],
        weight_grads[4],
        vector_sums[0],
        vector_sums[1],
        vector_sums[2],
        vector_sums[3],
        vector_sums[4],
        vector_sums[5],
        vector_sums[6],
        vector_sums[7],
    )


def solution(mesh):
    in_specs = (
        P("batch", "seq", None),
        P("seq", "batch", None, None),
        P("batch", None),
        P("batch", "seq", None),
        P("batch", None),
        P("batch", None),
        P("batch", None),
        P("batch", None),
        P("batch", None),
        P(),
        P(),
        P(),
        P(),
        P(),
        P(),
        P(),
        P(),
    )
    out_specs = (
        P("batch", "seq", None),
        P("batch", "seq", None),
        P("batch", "seq", None),
        P("batch", None),
        P("batch", None),
        P("batch", None),
        P("batch", None),
        P("batch", None),
        P(),
        P(),
        P(),
        P(),
        P(),
        P(),
        P(),
        P(),
    )
    return jax.shard_map(
        per_device, mesh=mesh, in_specs=in_specs, out_specs=out_specs, check_vma=False
    )
```

profile of v0, /device:TPU:0, one launch (start us, length us, event | category | flops | bytes accessed | tf_op | source)
XLA Modules:
  0.0 1640.8 jit_solution(9548763967133742407)
XLA Ops:
  10.2 60.0 %all-gather.8.cloned.1.call-done = bf16[2304,1152]{1,0:T(8,128)(2,1)} async-done(((bf16[144,1152]{1,0:T(8,128)(2,1)}), bf16[2304,1152]{1,0:T(8,128)(2,1)}) %all-gather.8.cloned.1.call-update) | async-done | bytes 5308432 | tf_op jit(solution)/shard_map/all_gather | solution.py:80
  86.7 56.4 %all-gather.10.cloned.1.call-done = bf16[1152,3456]{1,0:T(8,128)(2,1)} async-done(((bf16[72,3456]{1,0:T(8,128)(2,1)}), bf16[1152,3456]{1,0:T(8,128)(2,1)}) %all-gather.10.cloned.1.call-update) | async-done | bytes 7962640 | tf_op jit(solution)/shard_map/all_gather | solution.py:81
  172.3 81.9 %all-gather.18.cloned.1.call-done = bf16[1664,2304]{1,0:T(8,128)(2,1)} async-done(((bf16[832,2304]{1,0:T(8,128)(2,1)}), bf16[1664,2304]{1,0:T(8,128)(2,1)}) %all-gather.18.cloned.1.call-update) | async-done | bytes 7667728 | tf_op jit(solution)/shard_map/all_gather | solution.py:129
  266.2 36.7 %fusion.24 = (f32[832,16]{0,1:T(8,128)S(1)}, f32[16,1664,832]{1,2,0:T(8,128)}) fusion(pred[832,1664]{1,0:T(8,128)(4,1)S(1)} %broadcast_compare_fusion.1, bf16[1664,16,72]{0,2,1:T(8,128)(2,1)} %bitcast.244, bf16[832,16,72]{0,2,1:T(8,128)(2,1)} %bitcast.237), kind=kOutput, calls=%fused_computation.32 | convolution fusion | flops 3256208384 | bytes 95793152 | tf_op jit(solution)/shard_map/while/body/eval_jaxpr/rthd,rkhd->rthk/dot_general | solution.py:108
  302.9 35.8 %fusion.25 = f32[832,16]{0,1:T(8,128)S(1)} fusion(f32[16,1664,832]{1,2,0:T(8,128)} %get-tuple-element.347, f32[832,16]{0,1:T(8,128)S(1)} %broadcast_maximum_fusion, pred[832,1664]{1,0:T(8,128)(4,1)S(1)} %broadcast_compare_fusion.1), kind=kLoop, calls=%fused_computation.33 | loop fusion | flops 110742528 | bytes 90095616 | tf_op jit(solution)/shard_map/while/body/eval_jaxpr/reduce_sum | solution.py:115
  345.8 39.7 %fusion.92 = (bf16[1,832,16,72]{1,3,2,0:T(8,128)(2,1)}, f32[1,832,16,72]{1,3,2,0:T(8,128)}) fusion(f32[832,16]{0,1:T(8,128)} %get-tuple-element.343, bf16[1664,16,72]{0,2,1:T(8,128)(2,1)} %bitcast.254, f32[16,1664,832]{1,2,0:T(8,128)} %get-tuple-element.347, f32[832,16]{0,1:T(8,128)S(1)} %broadcast_maximum_fusion, ...), kind=kOutput, calls=%fused_computation.152 | convolution fusion | flops 3303399424 | bytes 99733504 | tf_op jit(solution)/shard_map/while/body/eval_jaxpr/rthk,rkhd->rthd/dot_general | solution.py:116
  395.9 48.6 %multiply_convert_fusion = (bf16[832,4608]{1,0:T(8,128)(2,1)}, f32[832,4608]{1,0:T(8,128)}, f32[832,4608]{1,0:T(8,128)}) fusion(f32[4608]{0:T(1024)S(1)} %copy-done.40, bf16[1152,4608]{1,0:T(8,128)(2,1)} %all-gather.14.cloned.1.call-done, f32[832,1152]{1,0:T(8,128)} %copy-done.6, f32[1152]{0:T(1024)S(1)} %copy-done.43, f32[1152]{0:T(1024)S(1)} %copy-done.31, ...), kind=kOutput, calls=%fused_computation.43 | convolution fusion | flops 9091031040 | bytes 52823552 | tf_op jit(solution)/shard_map/dot_general | solution.py:31
  444.5 33.6 %all-gather.16.cloned.1.call-done = bf16[4608,1152]{1,0:T(8,128)(2,1)} async-done(((bf16[288,1152]{1,0:T(8,128)(2,1)}), bf16[4608,1152]{1,0:T(8,128)(2,1)}) %all-gather.16.cloned.1.call-update) | async-done | bytes 10616848 | tf_op jit(solution)/shard_map/all_gather | solution.py:84
  478.1 25.3 %fusion.94 = (f32[4608]{0:T(1024)}, bf16[832,4608]{1,0:T(8,128)(2,1)}) fusion(f32[832,4608]{1,0:T(8,128)} %get-tuple-element.334, bf16[4608,1152]{1,0:T(8,128)(2,1)} %all-gather.16.cloned.1.call-done, bf16[1,832,1152]{2,1,0:T(8,128)(2,1)} %param.22, f32[832]{0:T(1024)S(1)} %copy-done.30, f32[832,4608]{1,0:T(8,128)} %get-tuple-element.352, ...), kind=kOutput, calls=%fused_computation.154 | convolution fusion | flops 8897417216 | bytes 50912512 | tf_op jit(solution)/shard_map/dot_general | solution.py:41
  503.4 19.6 %multiply_reduce_fusion.1 = (f32[1152]{0:T(1024)}, f32[832]{0:T(1024)S(1)}, f32[1152]{0:T(1024)}, f32[832,1152]{1,0:T(8,128)S(1)}) fusion(f32[832,1152]{1,0:T(8,128)S(1)} %copy-done.7, f32[832]{0:T(1024)S(1)} %fusion.78, f32[832]{0:T(1024)S(1)} %broadcast_multiply_fusion, f32[1152]{0:T(1024)S(1)} %copy-done.31, ...), kind=kOutput, calls=%fused_computation.87 | convolution fusion | flops 8840868864 | bytes 25976064 | tf_op jit(solution)/shard_map/dot_general | solution.py:41
  543.0 370.7 %while.10 = (s32[]{:T(128)}, f32[1,832,16,72]{1,3,2,0:T(8,128)}, bf16[1,1664,2304]{1,2,0:T(8,128)(2,1)}, bf16[1,1664,2304]{2,1,0:T(8,128)(2,1)}, s32[1,832]{1,0:...) while((s32[]{:T(128)}, f32[1,832,16,72]{1,3,2,0:T(8,128)}, ...), condition=%wide.region_15.16_spmd.clone, body=%wide.region_13.15_spmd.clone.sunk | while | flops 1248331264 | bytes 107741296 | solution.py:217
  913.6 34.1 %copy.57 = bf16[1,1664,2304]{2,0,1:T(2,128)(2,1)} copy(bf16[1,1664,2304]{1,2,0:T(8,128)(2,1)} %get-tuple-element.214) | data formatting | bytes 15335424
  964.9 18.2 %convolution_convert_fusion.1 = bf16[1152,4608]{1,0:T(8,128)(2,1)} fusion(bf16[832,4608]{1,0:T(8,128)(2,1)} %get-tuple-element.356, f32[832,1152]{1,0:T(8,128)} %copy-done.6, f32[1152]{0:T(1024)S(1)} %copy-done.44, f32[1152]{0:T(1024)S(1)} %copy-done.31, f32[832]{0:T(1024)S(1)} %fusion.78, f32[832]{0:T(1024)S(1)} %broadcast_multiply_fusion), kind=kOutput, calls=%fused_computation.40 | convolution fusion | flops 8843304960 | bytes 22134272 | tf_op jit(solution)/shard_map/dot_general | solution.py:35
  983.2 17.5 %convolution_convert_fusion = bf16[4608,1152]{1,0:T(8,128)(2,1)} fusion(bf16[832,4608]{1,0:T(8,128)(2,1)} %get-tuple-element.333, bf16[1,832,1152]{2,1,0:T(8,128)(2,1)} %param.22, f32[832]{0:T(1024)S(1)} %copy-done.30), kind=kOutput, calls=%fused_computation.39 | convolution fusion | flops 8841388032 | bytes 20204800 | tf_op jit(solution)/shard_map/dot_general | solution.py:35
  1004.4 43.2 %reduce-scatter.22.cloned.1.call-done = bf16[832,2304]{1,0:T(8,128)(2,1)} async-done(((bf16[1664,2304]{1,0:T(8,128)(2,1)}), bf16[832,2304]{1,0:T(8,128)(2,1)}) %reduce-scatter.22.cloned.1.call-update) | async-done | bytes 3833872
  1047.7 17.2 %reshape_bitcast_fusion = bf16[1,832,2304]{2,0,1:T(2,128)(2,1)} fusion(bf16[832,2304]{1,0:T(8,128)(2,1)} %reduce-scatter.22.cloned.1.call-done), kind=kLoop, calls=%fused_computation.59 | loop fusion | bytes 7667712
  1064.9 18.6 %copy.58 = bf16[1,832,2304]{1,2,0:T(8,128)(2,1)} copy(bf16[1,832,2304]{2,0,1:T(2,128)(2,1)} %reshape_bitcast_fusion) | data formatting | bytes 7667712
  1111.9 15.4 convolution_convert_fusion.2
  1127.4 111.6 %reduce-scatter.18.cloned.1.call-done = bf16[72,4608]{1,0:T(8,128)(2,1)} async-done(((bf16[1152,4608]{1,0:T(8,128)(2,1)}), bf16[72,4608]{1,0:T(8,128)(2,1)}) %reduce-scatter.18.cloned.1.call-update) | async-done | bytes 663568 | tf_op jit(solution)/shard_map/reduce_scatter | solution.py:258
  1239.0 124.4 %reduce-scatter.20.cloned.1.call-done = bf16[288,1152]{1,0:T(8,128)(2,1)} async-done(((bf16[4608,1152]{1,0:T(8,128)(2,1)}), bf16[288,1152]{1,0:T(8,128)(2,1)}) %reduce-scatter.20.cloned.1.call-update) | async-done | bytes 663568 | tf_op jit(solution)/shard_map/reduce_scatter | solution.py:261
  1363.4 83.8 %reduce-scatter.16.cloned.1.call-done = bf16[144,1152]{1,0:T(8,128)(2,1)} async-done(((bf16[2304,1152]{1,0:T(8,128)(2,1)}), bf16[144,1152]{1,0:T(8,128)(2,1)}) %reduce-scatter.16.cloned.1.call-update) | async-done | bytes 331792 | tf_op jit(solution)/shard_map/reduce_scatter | solution.py:249
  1447.3 104.3 %reduce-scatter.24.cloned.1.call-done = bf16[72,3456]{1,0:T(8,128)(2,1)} async-done(((bf16[1152,3456]{1,0:T(8,128)(2,1)}), bf16[72,3456]{1,0:T(8,128)(2,1)}) %reduce-scatter.24.cloned.1.call-update) | async-done | bytes 497680
  1551.6 17.2 %fusion.52 = bf16[1,832,1152]{2,1,0:T(8,128)(2,1)} fusion(f32[832,1152]{1,0:T(8,128)} %copy-done.6, bf16[832,4608]{1,0:T(8,128)(2,1)} %get-tuple-element.333, bf16[4608,1152]{1,0:T(8,128)(2,1)} %all-gather.16.cloned.1.call-done, f32[832]{0:T(1024)S(1)} %copy-done.30, f32[1152]{0:T(1024)S(1)} %copy-done.47), kind=kOutput, calls=%fused_computation.101 | convolution fusion | flops 8837038080 | bytes 24043264 | tf_op jit(solution)/shard_map/dot_general | solution.py:31
  1568.9 43.0 %all-reduce.2 = (f32[1152]{0:T(1024)}, f32[1152]{0:T(1024)}, f32[1152]{0:T(1024)}, f32[1152]{0:T(1024)}, f32[1152]{0:T(1024)}, /*index=5*/f32[1152]{0:T(1024)}, f32[4608]{0:T(1024)}, f32[1152]{0:T(1024)}) all-reduce(f32[1152]{0:T(1024)S(1)} %get-tuple-element.294, ...), channel_id=1, replica_groups=mesh['batch'=16,'seq'=2] {'batch','seq'}, use_global_device_ids=true, to_apply=%region_30.31 | all-reduce | flops 12672 | bytes 101376 | tf_op jit(solution)/shard_map/psum | solution.py:234
  (449 shorter events, 536.5 us)
Async XLA Ops:
  8.0 62.1 %copy-start = (bf16[1,832,1152]{2,1,0:T(8,128)(2,1)S(1)}, bf16[1,832,1152]{2,1,0:T(8,128)(2,1)}, u32[]{:S(2)}) copy-start(bf16[1,832,1152]{2,1,0:T(8,128)(2,1)} %param.19) | copy-start | bytes 5750788
  8.0 62.1 %all-gather.8.cloned.1.call-start = ((), (), s32[]{:S(2)}) async-start(), calls=%async_computation.7 | async-start | bytes 5640192 | tf_op jit(solution)/shard_map/all_gather | solution.py:80
  8.8 67.9 %reduce-scatter.14.cloned.1.call-start = ((), (), s32[]{:S(2)}) async-start(), calls=%async_computation.8 | async-start | bytes 5750784 | tf_op jit(solution)/shard_map/reduce_scatter | solution.py:76
  9.3 133.7 %all-gather.10.cloned.1.call-start = ((), (), s32[]{:S(2)}) async-start(), calls=%async_computation.9 | async-start | bytes 8460288 | tf_op jit(solution)/shard_map/all_gather | solution.py:81
  10.1 66.6 %copy-start.41 = (f32[1152]{0:T(1024)S(1)}, f32[1152]{0:T(1024)}, u32[]{:S(2)}) copy-start(f32[1152]{0:T(1024)} %param.28) | copy-start | bytes 13828
  10.1 244.2 %all-gather.18.cloned.1.call-start = ((), (), s32[]{:S(2)}) async-start(), calls=%async_computation.16 | async-start | bytes 11501568 | tf_op jit(solution)/shard_map/all_gather | solution.py:129
  76.6 66.4 %copy-start.32 = (f32[1152]{0:T(1024)S(1)}, f32[1152]{0:T(1024)}, u32[]{:S(2)}) copy-start(f32[1152]{0:T(1024)} %param.29) | copy-start | bytes 13828
  76.6 66.4 %copy-start.45 = (f32[1152]{0:T(1024)S(1)}, f32[1152]{0:T(1024)}, u32[]{:S(2)}) copy-start(f32[1152]{0:T(1024)} %param.30) | copy-start | bytes 13828
  83.7 71.8 %copy-start.20 = (f32[832]{0:T(1024)}, f32[832]{0:T(1024)S(1)}, u32[]{:S(2)}) copy-start(f32[832]{0:T(1024)S(1)} %broadcast_multiply_fusion.1) | copy-start | bytes 9988
  86.7 68.8 %copy-start.28 = (f32[832]{0:T(1024)}, f32[832]{0:T(1024)S(1)}, u32[]{:S(2)}) copy-start(f32[832]{0:T(1024)S(1)} %fusion.77) | copy-start | bytes 9988
  160.1 225.5 %all-gather.12.cloned.1.call-start = ((), (), s32[]{:S(2)}) async-start(), calls=%async_computation.10 | async-start | bytes 2820096 | tf_op jit(solution)/shard_map/all_gather | solution.py:82
  160.7 235.2 %all-gather.14.cloned.1.call-start = ((), (), s32[]{:S(2)}) async-start(), calls=%async_computation.11 | async-start | bytes 11280384 | tf_op jit(solution)/shard_map/all_gather | solution.py:83
  161.4 316.7 %all-gather.16.cloned.1.call-start = ((), (), s32[]{:S(2)}) async-start(), calls=%async_computation.12 | async-start | bytes 11280384 | tf_op jit(solution)/shard_map/all_gather | solution.py:84
  162.2 885.5 %reduce-scatter.22.cloned.1.call-start = ((), (), s32[]{:S(2)}) async-start(), calls=%async_computation.17 | async-start | bytes 11501568
  345.8 39.8 %copy-start.42 = (f32[1152]{0:T(1024)S(1)}, f32[1152]{0:T(1024)}, u32[]{:S(2)}) copy-start(f32[1152]{0:T(1024)} %param.31) | copy-start | bytes 13828
  395.2 49.4 %copy-start.24 = (f32[832]{0:T(1024)}, f32[832]{0:T(1024)S(1)}, u32[]{:S(2)}) copy-start(f32[832]{0:T(1024)S(1)} %multiply_reduce_fusion.5) | copy-start | bytes 9988
  395.8 82.3 %copy-start.30 = (f32[832]{0:T(1024)S(1)}, f32[832]{0:T(1024)}, u32[]{:S(2)}) copy-start(f32[832]{0:T(1024)} %compare_convert_fusion) | copy-start | bytes 9988
  957.4 170.0 %reduce-scatter.26.cloned.1.call-start = ((), (), s32[]{:S(2)}) async-start(), calls=%async_computation.19 | async-start | bytes 2820096
  964.9 274.1 %reduce-scatter.18.cloned.1.call-start = ((), (), s32[]{:S(2)}) async-start(), calls=%async_computation.14 | async-start | bytes 11280384 | tf_op jit(solution)/shard_map/reduce_scatter | solution.py:258
  983.1 380.3 %reduce-scatter.20.cloned.1.call-start = ((), (), s32[]{:S(2)}) async-start(), calls=%async_computation.15 | async-start | bytes 11280384 | tf_op jit(solution)/shard_map/reduce_scatter | solution.py:261
  1000.7 446.6 %reduce-scatter.16.cloned.1.call-start = ((), (), s32[]{:S(2)}) async-start(), calls=%async_computation.13 | async-start | bytes 5640192 | tf_op jit(solution)/shard_map/reduce_scatter | solution.py:249
  1111.2 440.3 %reduce-scatter.24.cloned.1.call-start = ((), (), s32[]{:S(2)}) async-start(), calls=%async_computation.18 | async-start | bytes 8460288
  1127.3 424.3 %copy-start.47 = (f32[1152]{0:T(1024)S(1)}, f32[1152]{0:T(1024)}, u32[]{:S(2)}) copy-start(f32[1152]{0:T(1024)} %param.35) | copy-start | bytes 13828
  1127.3 498.4 %all-reduce.6.cloned.1.call-start = ((), (), s32[]{:S(2)}) async-start(), calls=%async_computation.20 | async-start | bytes 4644864 | tf_op jit(solution)/shard_map/psum | solution.py:266
  (87 other events, 618.0 us)
Sparse Core Ops, SparseCore 0:
  11.0 59.0 all-gather.7
  72.3 70.7 all-gather.9
Sparse Core Ops, SparseCore 1:
  11.5 53.5 reduce-scatter.13
  160.2 94.0 all-gather.17
  256.3 43.3 all-gather.11
  302.0 87.2 all-gather.13
  391.6 86.4 all-gather.15
  957.5 90.1 reduce-scatter.21
  1051.4 63.8 reduce-scatter.25
  1119.7 119.2 reduce-scatter.17
  1243.5 119.9 reduce-scatter.19
  1368.0 79.2 reduce-scatter.15
  1451.8 99.7 reduce-scatter.23
  1554.2 69.4 all-reduce.5
where the time goes:
time: 1650 us; the launch traced here: 1640 us
  waiting for transfers between devices  703 us (43%)
  matrix products  626 us (38%)
  local copies, waits for them, and re-layouts  173 us (10%)
  other arithmetic  76.7 us (5%)
  blocking collectives  43 us (3%)
  between operations  16.6 us (1%)
    unnamed x17, waiting for transfers between devices  151 us
    reduce_scatter x1, waiting for transfers between devices, per_device(): lax.psum_scatter(full_grads[4].astype(jnp.bfloat16), 'batch', scatter_dim...  124 us
    reduce_scatter x1, waiting for transfers between devices, per_device(): lax.psum_scatter(full_grads[3].astype(jnp.bfloat16), 'batch', scatter_dim...  112 us
    dot_general x13, matrix products, query_grads(): jnp.einsum('rthd,rkhd->rthk', d_att, value_heads, preferred_element_type=...  101 us
    dot_general x6, matrix products, fwd_dot(): return jnp.dot(left, right, preferred_element_type=jnp.float32)  98.8 us
    dot_general x13, matrix products, query_grads(): jnp.einsum('rthk,rkhd->rthd', d_scores, key_heads, preferred_element_type...  92.7 us
    unnamed x94, local copies, waits for them, and re-layouts  90.4 us
    reduce_scatter x1, waiting for transfers between devices, per_device(): lax.psum_scatter(full_grads[0].astype(jnp.bfloat16), 'batch', scatter_dim...  83.8 us
  transfers between devices with their start and end apart: 14, of which 9 were waited for; matrix products, arithmetic and copies ran while one was open for 22% of the time, Pallas kernels for 0%

commit v1 on v0

v1 whole, which is shorter than its diff:
```python
import math

import jax
import jax.numpy as jnp
from jax import lax
from jax.experimental import pallas as pl
from jax.experimental.pallas import tpu as pltpu
from jax.sharding import PartitionSpec as P

HEADS = 16
HD = 72
D = 1152
EPS = 1e-05

SCALE=HD**-0.5
C2=SCALE*math.log2(math.e)
REM=576
TILES={
 0:[(256,576,258,832,[(0,256,576,258,832),(1,0,464,0,452)]),
    (0,272,0,258,[(0,0,272,0,258)])],
 1:[(0,464,0,452,[(0,0,464,0,452),(1,0,576,2,576)]),
    (448,272,452,710,[(0,448,272,452,710)]),
    (704,128,710,832,[(0,704,128,710,832)])],
}
NT=(((1,),(1,)),((),()))
TN=(((0,),(0,)),((),()))
def dot(a,b,dims=(((1,),(0,)),((),()))):
    return lax.dot_general(a,b,dims,preferred_element_type=jnp.float32)

def split(n,step):
    out=[];i=0
    while i<n:
        out.append((i,min(step,n-i))); i+=step
    return out

def fwd_kernel(s_ref, qkv_ref, kvr_ref, o_ref, l_ref, *, qstep):
    h=pl.program_id(0)
    @pl.when(h==0)
    def _():
        o_ref[...]=jnp.zeros_like(o_ref); l_ref[...]=jnp.zeros_like(l_ref)
    t=jnp.minimum((72*h)//128, 7)
    lo=72*h-128*t
    base=pl.multiple_of(t*128,128)
    def win(ref,off,r0,n):
        return ref[r0:r0+n, pl.ds(pl.multiple_of(base+off,128),256)]
    def tile(q0,nq,qv0,qv1,keys):
        lane=lax.broadcasted_iota(jnp.int32,(1,256),1)
        hm=(lane>=lo)&(lane<lo+72)
        for (a,n) in split(nq,qstep):
            r0=q0+a
            q=win(qkv_ref,0,r0,n)
            qm=jnp.where(hm,q,jnp.zeros_like(q))
            ss=[]
            for (src,k0,kc,kv0,kv1) in keys:
                k=win(qkv_ref,D,k0,kc) if src==0 else win(kvr_ref,0,k0,kc)
                s=dot(qm,k,NT)
                if kv0>k0 or kv1<k0+kc:
                    kp=k0+lax.broadcasted_iota(jnp.int32,(1,kc),1)
                    s=jnp.where((kp>=kv0)&(kp<kv1),s,-1e30)
                ss.append(s)
            m=jnp.max(ss[0],axis=1,keepdims=True)
            for s in ss[1:]: m=jnp.maximum(m,jnp.max(s,axis=1,keepdims=True))
            mc=m*C2
            l=None; o=None
            for s,(src,k0,kc,kv0,kv1) in zip(ss,keys):
                p=jnp.exp2(s*C2-mc)
                lp=jnp.sum(p,axis=1,keepdims=True)
                v=win(qkv_ref,2*D,k0,kc) if src==0 else win(kvr_ref,D,k0,kc)
                op=dot(p.astype(jnp.bfloat16),v)
                l=lp if l is None else l+lp
                o=op if o is None else o+op
            o=o*(1.0/l)
            lse=mc+jnp.log2(l)
            sl=(slice(r0,r0+n),pl.ds(base,256))
            old=o_ref[sl]; ob=o.astype(jnp.bfloat16)
            hl=lax.broadcasted_iota(jnp.int32,(1,128),1)==h
            oldl=l_ref[r0:r0+n,:]
            if r0<qv0 or r0+n>qv1:
                row=r0+lax.broadcasted_iota(jnp.int32,(n,1),0)
                rv=(row>=qv0)&(row<qv1)
                o_ref[sl]=jnp.where(hm&rv,ob,old)
                l_ref[r0:r0+n,:]=jnp.where(hl&rv,lse,oldl)
            else:
                o_ref[sl]=jnp.where(hm,ob,old)
                l_ref[r0:r0+n,:]=jnp.where(hl,lse,oldl)
    for sidx in (0,1):
        @pl.when(s_ref[0]==sidx)
        def _():
            for tl in TILES[sidx]: tile(*tl)

def full(shape,n=1):
    return pl.BlockSpec(shape,lambda h,s:(0,)*len(shape),pipeline_mode=pl.Buffered(1))
def attn_fwd(sidx,qkv,kvr,qstep=192):
    return pl.pallas_call(
        lambda *r: fwd_kernel(*r,qstep=qstep),
        out_shape=(jax.ShapeDtypeStruct((832,D),jnp.bfloat16),jax.ShapeDtypeStruct((832,128),jnp.float32)),
        grid_spec=pltpu.PrefetchScalarGridSpec(num_scalar_prefetch=1,grid=(HEADS,),
            in_specs=[full((832,3*D)),full((REM,2*D))],
            out_specs=(full((832,D)),full((832,128)))),
        compiler_params=pltpu.CompilerParams(vmem_limit_bytes=60*2**20),
        name="attn_fwd",
    )(sidx,qkv,kvr)

def bwd_kernel(s_ref,qkv_ref,kvr_ref,do_ref,lt_ref,dt_ref,dqkv_ref,dkvr_ref,*,kstep,expl):
    h=pl.program_id(0)
    @pl.when(h==0)
    def _():
        dqkv_ref[...]=jnp.zeros_like(dqkv_ref); dkvr_ref[...]=jnp.zeros_like(dkvr_ref)
    t=jnp.minimum((72*h)//128, 7)
    lo=72*h-128*t
    base=pl.multiple_of(t*128,128)
    def ws(off,r0,n):
        return (slice(r0,r0+n), pl.ds(pl.multiple_of(base+off,128),256))
    def tile(q0,nq,qv0,qv1,keys):
        lane=lax.broadcasted_iota(jnp.int32,(1,256),1)
        hm=(lane>=lo)&(lane<lo+72)
        q=qkv_ref[ws(0,q0,nq)]; qm=jnp.where(hm,q,jnp.zeros_like(q))
        do=do_ref[ws(0,q0,nq)]; dom=jnp.where(hm,do,jnp.zeros_like(do))
        lrow=lt_ref[pl.ds(h,1),:][:,q0:q0+nq]; drow=dt_ref[pl.ds(h,1),:][:,q0:q0+nq]
        if qv0>q0 or qv1<q0+nq:
            qp=q0+lax.broadcasted_iota(jnp.int32,(1,nq),1)
            lrow=jnp.where((qp>=qv0)&(qp<qv1),lrow,1e30)
        dqt=None
        for (src,k00,kcc,kv0,kv1) in keys:
            for (a,kc) in split(kcc,kstep):
                k0=k00+a
                k=qkv_ref[ws(D,k0,kc)] if src==0 else kvr_ref[ws(0,k0,kc)]
                v=qkv_ref[ws(2*D,k0,kc)] if src==0 else kvr_ref[ws(D,k0,kc)]
                st=dot(k,qm,NT)
                p=jnp.exp2(st*C2-lrow)
                if kv0>k0 or kv1<k0+kc:
                    kp=k0+lax.broadcasted_iota(jnp.int32,(kc,1),0)
                    p=jnp.where((kp>=kv0)&(kp<kv1),p,0.0)
                dp=dot(v,dom,NT)
                ds=(p*(dp-drow)).astype(jnp.bfloat16)
                dv=dot(p.astype(jnp.bfloat16),dom)
                dk=dot(ds,qm)*SCALE
                if src==0:
                    dqkv_ref[ws(D,k0,kc)]+=dk.astype(jnp.bfloat16)
                    dqkv_ref[ws(2*D,k0,kc)]+=dv.astype(jnp.bfloat16)
                else:
                    dkvr_ref[ws(0,k0,kc)]+=dk.astype(jnp.bfloat16)
                    dkvr_ref[ws(D,k0,kc)]+=dv.astype(jnp.bfloat16)
                if expl: d=dot(k.T,ds)
                else: d=dot(k,ds,TN)
                dqt=d if dqt is None else dqt+d
        dq=(dqt*SCALE).T
        sl=ws(0,q0,nq)
        dqkv_ref[sl]=dqkv_ref[sl]+jnp.where(hm,dq,0.0).astype(jnp.bfloat16)
    for sidx in (0,1):
        @pl.when(s_ref[0]==sidx)
        def _():
            for tl in TILES[sidx]: tile(*tl)

def attn_bwd(sidx,qkv,kvr,do,lt,dt,kstep=1024,expl=True):
    return pl.pallas_call(
        lambda *r: bwd_kernel(*r,kstep=kstep,expl=expl),
        out_shape=(jax.ShapeDtypeStruct((832,3*D),jnp.bfloat16),jax.ShapeDtypeStruct((REM,2*D),jnp.bfloat16)),
        grid_spec=pltpu.PrefetchScalarGridSpec(num_scalar_prefetch=1,grid=(HEADS,),
            in_specs=[full((832,3*D)),full((REM,2*D)),full((832,D)),full((16,832)),full((16,832))],
            out_specs=(full((832,3*D)),full((REM,2*D)))),
        compiler_params=pltpu.CompilerParams(vmem_limit_bytes=60*2**20),
        name="attn_bwd",
    )(sidx,qkv,kvr,do,lt,dt)


def layer_norm(hidden, gain, shift):
    centred = hidden - jnp.mean(hidden, axis=-1, keepdims=True)
    spread = jnp.mean(centred * centred, axis=-1, keepdims=True)
    return centred * lax.rsqrt(spread + EPS) * gain + shift


def exact_gelu(value):
    return jax.nn.gelu(value, approximate=False)


def segment_ids(offsets, positions):
    hits = (positions[None, :, None] >= offsets[:, None, :]).astype(jnp.int32)
    return jnp.sum(hits, axis=-1)


def fwd_dot(left, right):
    return jnp.dot(left, right, preferred_element_type=jnp.float32)


def contract_rows(left, right):
    return lax.dot_general(
        left, right, (((0,), (0,)), ((), ())), preferred_element_type=jnp.float32
    )


def back_dot(grad_rows, weight):
    return lax.dot_general(
        grad_rows, weight, (((1,), (1,)), ((), ())), preferred_element_type=jnp.float32
    )


class PairAttention:
    def __init__(self, qkv_all):
        self.side = lax.axis_index("seq")
        self.index = self.side.astype(jnp.int32).reshape(1)
        self.qkv = qkv_all
        self.away = jnp.where(self.side == 0, 256, 0)
        sent = lax.dynamic_slice(qkv_all, (self.away, D), (REM, 2 * D))
        self.kv_far = lax.ppermute(sent, "seq", [(0, 1), (1, 0)])

    def forward(self):
        self.out, self.lse = attn_fwd(self.index, self.qkv, self.kv_far, 288)
        return self.out

    def backward(self, d_att):
        pick = (
            lax.broadcasted_iota(jnp.int32, (D, HEADS), 0) // HD
            == lax.broadcasted_iota(jnp.int32, (D, HEADS), 1)
        ).astype(jnp.float32)
        prod = d_att.astype(jnp.float32) * self.out.astype(jnp.float32)
        row_dot = lax.dot_general(
            pick, prod, (((0,), (1,)), ((), ())), precision=lax.Precision.HIGHEST
        )
        lse = self.lse[:, :HEADS].T
        d_qkv, d_far = attn_bwd(self.index, self.qkv, self.kv_far, d_att, lse, row_dot)
        back = lax.ppermute(d_far, "seq", [(0, 1), (1, 0)])
        own = lax.dynamic_slice(d_qkv, (self.away, D), (REM, 2 * D))
        total = (own.astype(jnp.float32) + back.astype(jnp.float32)).astype(jnp.bfloat16)
        return lax.dynamic_update_slice(d_qkv, total, (self.away, D))


class RowAttention:
    def __init__(self, qkv_all, offsets, row_count, local_len):
        self.row_count, self.local_len = row_count, local_len
        self.row_len = local_len * lax.axis_size("seq")
        self.offsets = offsets
        first_pos = lax.axis_index("seq") * local_len
        self.query_seg = segment_ids(offsets, first_pos + jnp.arange(local_len, dtype=jnp.int32))
        self.scale = HD ** (-0.5)
        self.queries = qkv_all[:, :D].reshape(row_count, local_len, HEADS, HD)
        keyvals = qkv_all[:, D:].reshape(row_count, local_len, 2 * D)
        self.kv = lax.all_gather(keyvals, "seq", axis=1, tiled=True)

    def block(self, first, size):
        kv = lax.dynamic_slice_in_dim(self.kv, first, size, 1)
        shape = (self.row_count, size, HEADS, HD)
        key_seg = segment_ids(self.offsets, first + jnp.arange(size, dtype=jnp.int32))
        same = self.query_seg[:, :, None, None] == key_seg[:, None, None, :]
        return kv[:, :, :D].reshape(shape), kv[:, :, D:].reshape(shape), same

    def scores(self, keys):
        return (
            jnp.einsum("rthd,rkhd->rthk", self.queries, keys, preferred_element_type=jnp.float32)
            * self.scale
        )

    def forward(self):
        keys, values, same = self.block(0, self.row_len)
        scores = jnp.where(same, self.scores(keys), -1e30)
        top = jnp.max(scores, axis=-1)
        expo = jnp.where(same, jnp.exp(scores - top[..., None]), 0.0)
        norm = jnp.sum(expo, axis=-1)
        weighted = jnp.einsum(
            "rthk,rkhd->rthd",
            expo.astype(jnp.bfloat16),
            values,
            preferred_element_type=jnp.float32,
        )
        self.attended = weighted / norm[..., None]
        self.log_total = top + jnp.log(norm)
        return self.attended.reshape(-1, D).astype(jnp.bfloat16)

    def backward(self, d_att):
        rows, length = self.row_count, self.local_len
        d_att = d_att.reshape(rows, length, HEADS, HD)
        row_dot = jnp.sum(d_att.astype(jnp.float32) * self.attended, axis=-1)
        size = math.gcd(self.row_len, 512)

        def step(index, totals):
            d_query, d_kv = totals
            keys, values, same = self.block(index * size, size)
            weights = jnp.where(same, jnp.exp(self.scores(keys) - self.log_total[..., None]), 0.0)
            d_weights = jnp.einsum(
                "rthd,rkhd->rthk", d_att, values, preferred_element_type=jnp.float32
            )
            d_scores = (weights * (d_weights - row_dot[..., None])).astype(jnp.bfloat16)
            d_query = d_query + self.scale * jnp.einsum(
                "rthk,rkhd->rthd", d_scores, keys, preferred_element_type=jnp.float32
            )
            d_key = self.scale * jnp.einsum(
                "rthk,rthd->rkhd", d_scores, self.queries, preferred_element_type=jnp.float32
            )
            d_value = jnp.einsum(
                "rthk,rthd->rkhd",
                weights.astype(jnp.bfloat16),
                d_att,
                preferred_element_type=jnp.float32,
            )
            both = jnp.concatenate(
                [d_key.reshape(rows, size, D), d_value.reshape(rows, size, D)], axis=2
            )
            return d_query, lax.dynamic_update_slice_in_dim(d_kv, both, index * size, 1)

        start = (
            jnp.zeros((rows, length, HEADS, HD), jnp.float32),
            jnp.zeros((rows, self.row_len, 2 * D), jnp.float32),
        )
        d_query, d_kv = lax.fori_loop(0, self.row_len // size, step, start)
        d_kv = lax.psum_scatter(
            d_kv.astype(jnp.bfloat16), "seq", scatter_dimension=1, tiled=True
        ).astype(jnp.float32)
        return jnp.concatenate(
            [d_query.reshape(rows * length, D), d_kv.reshape(rows * length, 2 * D)], axis=1
        ).astype(jnp.bfloat16)


def per_device(
    tokens,
    skip_parts,
    lengths,
    cotangent,
    skip_w,
    qkv_w,
    proj_w,
    fc1_w,
    fc2_w,
    skip_bias,
    ln1_gain,
    ln1_bias,
    proj_bias,
    ln2_gain,
    ln2_bias,
    fc1_bias,
    fc2_bias,
):
    row_count, local_len, features = tokens.shape
    tok_count = row_count * local_len
    offsets = jnp.cumsum(lengths, axis=1)
    first_pos = lax.axis_index("seq") * local_len
    query_seg = segment_ids(offsets, first_pos + jnp.arange(local_len, dtype=jnp.int32))
    live_mask = (query_seg < lengths.shape[1]).astype(jnp.float32).reshape(tok_count, 1)
    skip_rows = lax.psum_scatter(skip_parts[0], "seq", scatter_dimension=1, tiled=True)
    w_skip, w_qkv, w_proj, w_up, w_down = (
        lax.all_gather(w, "batch", axis=0, tiled=True)
        for w in (skip_w, qkv_w, proj_w, fc1_w, fc2_w)
    )
    tok_flat = tokens.reshape(tok_count, features)
    skip_flat = skip_rows.reshape(tok_count, features)
    h_zero = (
        fwd_dot(tok_flat, w_skip[:features]) + fwd_dot(skip_flat, w_skip[features:]) + skip_bias
    )
    normed_one, ln1_back = jax.vjp(layer_norm, h_zero, ln1_gain, ln1_bias)
    act_one = normed_one.astype(jnp.bfloat16)
    qkv_all = fwd_dot(act_one, w_qkv).astype(jnp.bfloat16)
    if lax.axis_size("seq") == 2 and row_count == 1 and local_len == 832:
        attention = PairAttention(qkv_all)
    else:
        attention = RowAttention(qkv_all, offsets, row_count, local_len)
    att_low = attention.forward()
    h_one = h_zero + fwd_dot(att_low, w_proj) + proj_bias
    normed_two, ln2_back = jax.vjp(layer_norm, h_one, ln2_gain, ln2_bias)
    act_two = normed_two.astype(jnp.bfloat16)
    up_proj = fwd_dot(act_two, w_up) + fc1_bias
    gelu_out, gelu_back = jax.vjp(exact_gelu, up_proj)
    gelu_low = gelu_out.astype(jnp.bfloat16)
    h_two = h_one + fwd_dot(gelu_low, w_down) + fc2_bias
    output = (h_two * live_mask).astype(jnp.bfloat16).reshape(row_count, local_len, features)
    grad_two = cotangent.reshape(tok_count, features).astype(jnp.float32) * live_mask
    grad_low = grad_two.astype(jnp.bfloat16)
    d_w_down = contract_rows(gelu_low, grad_low)
    d_gelu = back_dot(grad_low, w_down)
    d_up = gelu_back(d_gelu)[0]
    up_low = d_up.astype(jnp.bfloat16)
    d_w_up = contract_rows(act_two, up_low)
    d_act_two = back_dot(up_low, w_up)
    d_h_one, d_ln2_gain, d_ln2_bias = ln2_back(d_act_two)
    d_h_one = d_h_one + grad_two
    proj_low = d_h_one.astype(jnp.bfloat16)
    d_w_proj = contract_rows(att_low, proj_low)
    d_att = back_dot(proj_low, w_proj).astype(jnp.bfloat16)
    d_qkv = attention.backward(d_att)
    d_w_qkv = contract_rows(act_one, d_qkv)
    d_act_one = back_dot(d_qkv, w_qkv)
    d_h_zero, d_ln1_gain, d_ln1_bias = ln1_back(d_act_one)
    d_h_zero = d_h_zero + d_h_one
    zero_low = d_h_zero.astype(jnp.bfloat16)
    d_w_skip = jnp.concatenate(
        [contract_rows(tok_flat, zero_low), contract_rows(skip_flat, zero_low)], axis=0
    )
    d_tokens = back_dot(zero_low, w_skip[:features]).reshape(row_count, local_len, features)
    d_skip = back_dot(zero_low, w_skip[features:]).reshape(row_count, local_len, features)
    vector_sums = lax.psum(
        (
            jnp.sum(d_h_zero, axis=0),
            d_ln1_gain,
            d_ln1_bias,
            jnp.sum(d_h_one, axis=0),
            d_ln2_gain,
            d_ln2_bias,
            jnp.sum(d_up, axis=0),
            jnp.sum(grad_two, axis=0),
        ),
        ("batch", "seq"),
    )
    weight_grads = tuple(
        lax.psum(
            lax.psum_scatter(
                grad.astype(jnp.bfloat16), "batch", scatter_dimension=0, tiled=True
            ),
            "seq",
        ).astype(jnp.float32)
        for grad in (d_w_skip, d_w_qkv, d_w_proj, d_w_up, d_w_down)
    )
    return (output, d_tokens, d_skip, *weight_grads, *vector_sums)


def solution(mesh):
    in_specs = (
        P("batch", "seq", None),
        P("seq", "batch", None, None),
        P("batch", None),
        P("batch", "seq", None),
        *(P("batch", None),) * 5,
        *(P(),) * 8,
    )
    out_specs = (*(P("batch", "seq", None),) * 3, *(P("batch", None),) * 5, *(P(),) * 8)
    return jax.shard_map(
        per_device, mesh=mesh, in_specs=in_specs, out_specs=out_specs, check_vma=False
    )
```

time: 1650 us -> 1090 us (0.66)
  matrix products: 626 us -> 240 us
  local copies, waits for them, and re-layouts: 173 us -> 13.5 us
  Pallas kernels: 0 us -> 86.8 us
  other arithmetic: 76.7 us -> 23 us
  waiting for transfers between devices: 703 us -> 662 us
    dot_general x67 -> x1, matrix products: 384 us -> 3.41 us  [backward(): lax.dot_general(pick, prod, (((0,), (1,)), ((), ())), precision=lax.Preci...]
    ppermute x0 -> x2, waiting for transfers between devices: none -> 109 us  [the longest x1 57.1 us: __init__(): self.kv_far = lax.ppermute(sent, 'seq', [(0, 1), (1, 0)])]
    pallas_call x0 -> x2, Pallas kernels: none -> 86.8 us  [the longest x1 56.1 us: attn_bwd(): pl.pallas_call(lambda *r: bwd_kernel(*r, kstep=kstep, expl=expl), out_sha...]
    unnamed x94 -> x76, local copies, waits for them, and re-layouts: 90.4 us -> 9.95 us
    all_gather x6 -> x5, waiting for transfers between devices: 232 us -> 170 us  [per_device(): lax.all_gather(w, 'batch', axis=0, tiled=True)]
    reduce_scatter x4, waiting for transfers between devices: 320 us -> 274 us  [the longest x3 274 us: per_device(): lax.psum_scatter(grad.astype(jnp.bfloat16), 'batch', scatter_dimension=0,...]
    unnamed x17 -> x14, waiting for transfers between devices: 151 us -> 108 us
    slice x19 -> x0, local copies, waits for them, and re-layouts: 42.5 us -> none  [the longest x14 20.8 us: split_block(): kv_block[:, :, features:]]
  transfers between devices with their start and end apart: 14 -> 14, of which waited for: 9 -> 10; matrix products, arithmetic and copies ran while one was open for 22% -> 19% of each run, Pallas kernels for 0% -> 3%
where the time goes in v1:
time: 1090 us
  waiting for transfers between devices  662 us (61%)
  matrix products  240 us (22%)
  Pallas kernels  86.8 us (8%)
  blocking collectives  42.7 us (4%)
  other arithmetic  23 us (2%)
  between operations  16.4 us (2%)
  local copies, waits for them, and re-layouts  13.5 us (1%)
    reduce_scatter x3, waiting for transfers between devices, per_device(): lax.psum_scatter(grad.astype(jnp.bfloat16), 'batch', scatter_dimension=0,...  274 us
    all_gather x5, waiting for transfers between devices, per_device(): lax.all_gather(w, 'batch', axis=0, tiled=True)  170 us
    unnamed x14, waiting for transfers between devices  108 us
    dot_general x6, matrix products, fwd_dot(): return jnp.dot(left, right, preferred_element_type=jnp.float32)  98.1 us
    dot_general x6, matrix products, back_dot(): lax.dot_general(grad_rows, weight, (((1,), (1,)), ((), ())), preferred_el...  74.3 us
    dot_general x6, matrix products, contract_rows(): lax.dot_general(left, right, (((0,), (0,)), ((), ())), preferred_element_...  64.3 us
    ppermute x1, waiting for transfers between devices, __init__(): self.kv_far = lax.ppermute(sent, 'seq', [(0, 1), (1, 0)])  57.1 us
    pallas_call x1, Pallas kernels, attn_bwd(): pl.pallas_call(lambda *r: bwd_kernel(*r, kstep=kstep, expl=expl), out_sha...  56.1 us
  transfers between devices with their start and end apart: 14, of which 10 were waited for; matrix products, arithmetic and copies ran while one was open for 19% of the time, Pallas kernels for 3%

profile of v1, /device:TPU:0, one launch (start us, length us, event | category | flops | bytes accessed | tf_op | source)
XLA Modules:
  0.0 1086.6 jit_solution(12870952799898791715)
XLA Ops:
  12.1 58.1 %all-gather.6.cloned.1.call-done = bf16[2304,1152]{1,0:T(8,128)(2,1)} async-done(((bf16[144,1152]{1,0:T(8,128)(2,1)}), bf16[2304,1152]{1,0:T(8,128)(2,1)}) %all-gather.6.cloned.1.call-update) | async-done | bytes 5308432 | tf_op jit(solution)/shard_map/all_gather | solution.py:340
  86.7 56.4 %all-gather.8.cloned.1.call-done = bf16[1152,3456]{1,0:T(8,128)(2,1)} async-done(((bf16[72,3456]{1,0:T(8,128)(2,1)}), bf16[1152,3456]{1,0:T(8,128)(2,1)}) %all-gather.8.cloned.1.call-update) | async-done | bytes 7962640 | tf_op jit(solution)/shard_map/all_gather | solution.py:340
  143.1 12.5 %convolution_convert_fusion.6.r_1_ = bf16[832,3456]{1,0:T(8,128)(2,1)S(1)} fusion(bf16[1152,3456]{1,0:T(8,128)(2,1)} %all-gather.8.cloned.1.call-done, f32[832,1152]{1,0:T(8,128)} %copy-done.4, f32[1152]{0:T(1024)S(1)} %copy-done.33, f32[1152]{0:T(1024)S(1)} %copy-done.25, f32[832]{0:T(1024)S(1)} %fusion.51, f32[832]{0:T(1024)S(1)} %broadcast_multiply_fusion.1), kind=kOutput, calls=%fused_computation.23 | convolution fusion | flops 6632570880 | bytes 17563136 | tf_op jit(solution)/shard_map/dot_general | solution.py:183
  162.9 57.1 %collective-permute-done.r_2_ = bf16[576,2304]{1,0:T(8,128)(2,1)} collective-permute-done((bf16[576,2304]{1,0:T(8,128)(2,1)}, bf16[576,2304]{1,0:T(8,128)(2,1)}, u32[]{:S(2)}, u32[]{:S(2)}) %collective-permute-start) | collective-permute-done | bytes 2654240 | tf_op jit(solution)/shard_map/ppermute | solution.py:205
  220.0 30.7 %attn_fwd.1 = (bf16[832,1152]{1,0:T(8,128)(2,1)}, f32[832,128]{1,0:T(8,128)}) custom-call(s32[1]{0:T(128)} %bitcast.3.r_0_, bf16[832,3456]{1,0:T(8,128)(2,1)} %copy-done.1, bf16[576,2304]{1,0:T(8,128)(2,1)} %collective-permute-done.r_2_), custom_call_target="tpu_custom_call" | custom-call | tf_op jit(solution)/shard_map/attn_fwd/pallas_call | solution.py:94
  261.5 15.0 %all-gather.12.cloned.1.call-done = bf16[1152,4608]{1,0:T(8,128)(2,1)} async-done(((bf16[72,4608]{1,0:T(8,128)(2,1)}), bf16[1152,4608]{1,0:T(8,128)(2,1)}) %all-gather.12.cloned.1.call-update) | async-done | bytes 10616848 | tf_op jit(solution)/shard_map/all_gather | solution.py:340
  276.5 48.2 %multiply_convert_fusion = (bf16[832,4608]{1,0:T(8,128)(2,1)}, f32[832,4608]{1,0:T(8,128)}, f32[832,4608]{1,0:T(8,128)}) fusion(f32[4608]{0:T(1024)S(1)} %copy-done.30, bf16[1152,4608]{1,0:T(8,128)(2,1)} %all-gather.12.cloned.1.call-done, f32[832,1152]{1,0:T(8,128)} %copy-done.2, f32[1152]{0:T(1024)S(1)} %copy-done.35, f32[1152]{0:T(1024)S(1)} %copy-done.27, ...), kind=kOutput, calls=%fused_computation.5 | convolution fusion | flops 9091031040 | bytes 52823552 | tf_op jit(solution)/shard_map/dot_general | solution.py:183
  324.7 40.9 %all-gather.14.cloned.1.call-done = bf16[4608,1152]{1,0:T(8,128)(2,1)} async-done(((bf16[288,1152]{1,0:T(8,128)(2,1)}), bf16[4608,1152]{1,0:T(8,128)(2,1)}) %all-gather.14.cloned.1.call-update) | async-done | bytes 10616848 | tf_op jit(solution)/shard_map/all_gather | solution.py:340
  365.6 25.0 %fusion.60 = (f32[4608]{0:T(1024)S(1)}, bf16[832,4608]{1,0:T(8,128)(2,1)}) fusion(f32[832,4608]{1,0:T(8,128)} %get-tuple-element.50, bf16[4608,1152]{1,0:T(8,128)(2,1)} %all-gather.14.cloned.1.call-done, bf16[1,832,1152]{2,1,0:T(8,128)(2,1)} %param.20, f32[832]{0:T(1024)S(1)} %compare_convert_fusion, f32[832,4608]{1,0:T(8,128)} %get-tuple-element.58, ...), kind=kOutput, calls=%fused_computation.110 | convolution fusion | flops 8897417216 | bytes 50912512 | tf_op jit(solution)/shard_map/dot_general | solution.py:193
  390.7 19.2 %multiply_reduce_fusion = (f32[1152]{0:T(1024)S(1)}, f32[832]{0:T(1024)S(1)}, f32[1152]{0:T(1024)S(1)}, f32[832,1152]{1,0:T(8,128)S(1)}) fusion(f32[832,1152]{1,0:T(8,128)S(1)} %copy-done.3, f32[832]{0:T(1024)S(1)} %fusion.52, f32[832]{0:T(1024)S(1)} %broadcast_multiply_fusion, f32[1152]{0:T(1024)S(1)} %copy-done.27, ...), kind=kOutput, calls=%fused_computation.43 | convolution fusion | flops 8840868864 | bytes 25976064 | tf_op jit(solution)/shard_map/dot_general | solution.py:193
  419.6 56.1 %attn_bwd.1 = (bf16[832,3456]{1,0:T(8,128)(2,1)}, bf16[576,2304]{1,0:T(8,128)(2,1)}) custom-call(s32[1]{0:T(128)} %bitcast.3.r_0_, bf16[832,3456]{1,0:T(8,128)(2,1)} %copy-done.1, bf16[576,2304]{1,0:T(8,128)(2,1)} %collective-permute-done.r_2_, bf16[832,1152]{1,0:T(8,128)(2,1)} %copy-done.8, f32[16,832]{1,0:T(8,128)} %slice_bitcast_fusion.r_4_, ...), custom_call_target="tpu_custom_call" | custom-call | tf_op jit(solution)/shard_map/attn_bwd/pallas_call | solution.py:156
  475.7 7.4 convolution_convert_fusion.3
  483.6 52.1 %collective-permute-done.1 = bf16[576,2304]{1,0:T(8,128)(2,1)} collective-permute-done((bf16[576,2304]{1,0:T(8,128)(2,1)}, bf16[576,2304]{1,0:T(8,128)(2,1)}, u32[]{:S(2)}, u32[]{:S(2)}) %collective-permute-start.1) | collective-permute-done | bytes 2654240 | tf_op jit(solution)/shard_map/ppermute | solution.py:222
  540.6 13.3 %multiply_reduce_fusion.1 = (f32[1152]{0:T(1024)S(1)}, f32[832]{0:T(1024)S(1)}, f32[1152]{0:T(1024)S(1)}, f32[832,1152]{1,0:T(8,128)S(1)}) fusion(f32[832,1152]{1,0:T(8,128)S(1)} %copy-done.5, f32[832]{0:T(1024)S(1)} %copy-done.23, f32[832]{0:T(1024)S(1)} %copy-done.15, f32[1152]{0:T(1024)S(1)} %copy-done.26, bf16[832,3456]{1,0:T(8,128)(2,1)} %fusion.24, ...), kind=kOutput, calls=%fused_computation.44 | convolution fusion | flops 6632567808 | bytes 21404928 | tf_op jit(solution)/shard_map/dot_general | solution.py:193
  567.1 14.7 %convolution_convert_fusion.2 = bf16[1152,3456]{1,0:T(8,128)(2,1)} fusion(bf16[832,3456]{1,0:T(8,128)(2,1)} %fusion.24, f32[832,1152]{1,0:T(8,128)} %copy-done.4, f32[1152]{0:T(1024)S(1)} %copy-done.34, f32[1152]{0:T(1024)S(1)} %copy-done.26, f32[832]{0:T(1024)S(1)} %copy-done.23, f32[832]{0:T(1024)S(1)} %copy-done.15), kind=kOutput, calls=%fused_computation.19 | convolution fusion | flops 6633676800 | bytes 17563136 | tf_op jit(solution)/shard_map/dot_general | solution.py:187
  581.8 17.9 %convolution_convert_fusion.1 = bf16[1152,4608]{1,0:T(8,128)(2,1)} fusion(bf16[832,4608]{1,0:T(8,128)(2,1)} %get-tuple-element.62, f32[832,1152]{1,0:T(8,128)} %copy-done.2, f32[1152]{0:T(1024)S(1)} %copy-done.35, f32[1152]{0:T(1024)S(1)} %copy-done.27, f32[832]{0:T(1024)S(1)} %fusion.52, f32[832]{0:T(1024)S(1)} %broadcast_multiply_fusion), kind=kOutput, calls=%fused_computation.2 | convolution fusion | flops 8843304960 | bytes 22134272 | tf_op jit(solution)/shard_map/dot_general | solution.py:187
  600.0 17.5 %convolution_convert_fusion = bf16[4608,1152]{1,0:T(8,128)(2,1)} fusion(bf16[832,4608]{1,0:T(8,128)(2,1)} %get-tuple-element.49, bf16[1,832,1152]{2,1,0:T(8,128)(2,1)} %param.20, f32[832]{0:T(1024)S(1)} %compare_convert_fusion), kind=kOutput, calls=%fused_computation.1 | convolution fusion | flops 8841388032 | bytes 20204800 | tf_op jit(solution)/shard_map/dot_general | solution.py:187
  617.7 25.7 %reduce-scatter.13.cloned.1.call-done = bf16[144,1152]{1,0:T(8,128)(2,1)} async-done(((bf16[2304,1152]{1,0:T(8,128)(2,1)}), bf16[144,1152]{1,0:T(8,128)(2,1)}) %reduce-scatter.13.cloned.1.call-update) | async-done | bytes 331792 | tf_op jit(solution)/shard_map/reduce_scatter | solution.py:403
  643.4 104.6 %reduce-scatter.19.cloned.1.call-done = bf16[72,3456]{1,0:T(8,128)(2,1)} async-done(((bf16[1152,3456]{1,0:T(8,128)(2,1)}), bf16[72,3456]{1,0:T(8,128)(2,1)}) %reduce-scatter.19.cloned.1.call-update) | async-done | bytes 497680
  747.9 124.1 %reduce-scatter.15.cloned.1.call-done = bf16[72,4608]{1,0:T(8,128)(2,1)} async-done(((bf16[1152,4608]{1,0:T(8,128)(2,1)}), bf16[72,4608]{1,0:T(8,128)(2,1)}) %reduce-scatter.15.cloned.1.call-update) | async-done | bytes 663568 | tf_op jit(solution)/shard_map/reduce_scatter | solution.py:403
  872.1 123.9 %reduce-scatter.17.cloned.1.call-done = bf16[288,1152]{1,0:T(8,128)(2,1)} async-done(((bf16[4608,1152]{1,0:T(8,128)(2,1)}), bf16[288,1152]{1,0:T(8,128)(2,1)}) %reduce-scatter.17.cloned.1.call-update) | async-done | bytes 663568 | tf_op jit(solution)/shard_map/reduce_scatter | solution.py:403
  996.0 17.3 %fusion.23 = bf16[1,832,1152]{2,1,0:T(8,128)(2,1)} fusion(f32[832,1152]{1,0:T(8,128)} %copy-done.2, bf16[832,4608]{1,0:T(8,128)(2,1)} %get-tuple-element.49, bf16[4608,1152]{1,0:T(8,128)(2,1)} %all-gather.14.cloned.1.call-done, f32[832]{0:T(1024)S(1)} %compare_convert_fusion, f32[1152]{0:T(1024)S(1)} %copy-done.36), kind=kOutput, calls=%fused_computation.61 | convolution fusion | flops 8837038080 | bytes 24043264 | tf_op jit(solution)/shard_map/dot_general | solution.py:183
  1013.4 42.7 %all-reduce.2 = (f32[1152]{0:T(1024)}, f32[1152]{0:T(1024)}, f32[1152]{0:T(1024)}, f32[1152]{0:T(1024)}, f32[1152]{0:T(1024)}, /*index=5*/f32[1152]{0:T(1024)}, f32[4608]{0:T(1024)}, f32[1152]{0:T(1024)}) all-reduce(f32[1152]{0:T(1024)S(1)} %get-tuple-element.30, ...), channel_id=1, replica_groups=mesh['batch'=16,'seq'=2] {'batch','seq'}, use_global_device_ids=true, to_apply=%region_22.23 | all-reduce | flops 12672 | bytes 101376 | tf_op jit(solution)/shard_map/psum | solution.py:388
  1056.1 7.2 convolution_bitcast_fusion
  (144 shorter events, 82.4 us)
Async XLA Ops:
  8.0 62.1 %copy-start = (bf16[1,832,1152]{2,1,0:T(8,128)(2,1)S(1)}, bf16[1,832,1152]{2,1,0:T(8,128)(2,1)}, u32[]{:S(2)}) copy-start(bf16[1,832,1152]{2,1,0:T(8,128)(2,1)} %param.17) | copy-start | bytes 5750788
  8.0 62.1 %all-gather.6.cloned.1.call-start = ((), (), s32[]{:S(2)}) async-start(), calls=%async_computation.6 | async-start | bytes 5640192 | tf_op jit(solution)/shard_map/all_gather | solution.py:340
  8.8 67.9 %reduce-scatter.11.cloned.1.call-start = ((), (), s32[]{:S(2)}) async-start(), calls=%async_computation.7 | async-start | bytes 5750784 | tf_op jit(solution)/shard_map/reduce_scatter | solution.py:338
  9.3 133.7 %all-gather.8.cloned.1.call-start = ((), (), s32[]{:S(2)}) async-start(), calls=%async_computation.8 | async-start | bytes 8460288 | tf_op jit(solution)/shard_map/all_gather | solution.py:340
  10.1 241.8 %all-gather.10.cloned.1.call-start = ((), (), s32[]{:S(2)}) async-start(), calls=%async_computation.9 | async-start | bytes 2820096 | tf_op jit(solution)/shard_map/all_gather | solution.py:340
  10.8 265.6 %all-gather.12.cloned.1.call-start = ((), (), s32[]{:S(2)}) async-start(), calls=%async_computation.10 | async-start | bytes 11280384 | tf_op jit(solution)/shard_map/all_gather | solution.py:340
  11.4 354.2 %all-gather.14.cloned.1.call-start = ((), (), s32[]{:S(2)}) async-start(), calls=%async_computation.11 | async-start | bytes 11280384 | tf_op jit(solution)/shard_map/all_gather | solution.py:340
  12.0 605.7 %reduce-scatter.21.cloned.1.call-start = ((), (), s32[]{:S(2)}) async-start(), calls=%async_computation.16 | async-start | bytes 2820096
  12.0 64.6 %copy-start.31 = (f32[1152]{0:T(1024)S(1)}, f32[1152]{0:T(1024)}, u32[]{:S(2)}) copy-start(f32[1152]{0:T(1024)} %param.26) | copy-start | bytes 13828
  83.7 59.4 %copy-start.25 = (f32[1152]{0:T(1024)S(1)}, f32[1152]{0:T(1024)}, u32[]{:S(2)}) copy-start(f32[1152]{0:T(1024)} %param.27) | copy-start | bytes 13828
  83.7 59.4 %copy-start.33 = (f32[1152]{0:T(1024)S(1)}, f32[1152]{0:T(1024)}, u32[]{:S(2)}) copy-start(f32[1152]{0:T(1024)} %param.28) | copy-start | bytes 13828
  83.7 71.9 %copy-start.14 = (f32[832]{0:T(1024)}, f32[832]{0:T(1024)S(1)}, u32[]{:S(2)}) copy-start(f32[832]{0:T(1024)S(1)} %broadcast_multiply_fusion.1) | copy-start | bytes 9988
  86.7 68.9 %copy-start.22 = (f32[832]{0:T(1024)}, f32[832]{0:T(1024)S(1)}, u32[]{:S(2)}) copy-start(f32[832]{0:T(1024)S(1)} %fusion.51) | copy-start | bytes 9988
  159.9 60.1 %collective-permute-start = (bf16[576,2304]{1,0:T(8,128)(2,1)}, bf16[576,2304]{1,0:T(8,128)(2,1)}, u32[]{:S(2)}, u32[]{:S(2)}) collective-permute-start(bf16[576,2304]{1,0:T(8,128)(2,1)} %constant_dynamic-slice_fusion), channel_id=1, source_target_pairs={{0,1},{1,0},{2,3},{3,2},{4,5},{5,4},{6,7},{7,6},{8,9},{9,8},{10,11... | collective-permute-start | bytes 7962632 | tf_op jit(solution)/shard_map/ppermute | solution.py:205
  220.0 32.0 %copy-start.32 = (f32[1152]{0:T(1024)S(1)}, f32[1152]{0:T(1024)}, u32[]{:S(2)}) copy-start(f32[1152]{0:T(1024)} %param.29) | copy-start | bytes 13828
  260.9 63.9 %copy-start.18 = (f32[832]{0:T(1024)}, f32[832]{0:T(1024)S(1)}, u32[]{:S(2)}) copy-start(f32[832]{0:T(1024)S(1)} %multiply_reduce_fusion.4) | copy-start | bytes 9988
  365.6 25.0 %copy-start.3 = (f32[832,1152]{1,0:T(8,128)S(1)}, f32[832,1152]{1,0:T(8,128)}, u32[]{:S(2)}) copy-start(f32[832,1152]{1,0:T(8,128)} %copy-done.2) | copy-start | bytes 11501572
  475.7 60.0 %collective-permute-start.1 = (bf16[576,2304]{1,0:T(8,128)(2,1)}, bf16[576,2304]{1,0:T(8,128)(2,1)}, u32[]{:S(2)}, u32[]{:S(2)}) collective-permute-start(bf16[576,2304]{1,0:T(8,128)(2,1)} %get-tuple-element.23), channel_id=1, source_target_pairs={{0,1},{1,0},{2,3},{3,2},{4,5},{5,4},{6,7},{7,6},{8,9},{9,8},{10,11... | collective-permute-start | bytes 7962632 | tf_op jit(solution)/shard_map/ppermute | solution.py:222
  483.2 160.2 %reduce-scatter.13.cloned.1.call-start = ((), (), s32[]{:S(2)}) async-start(), calls=%async_computation.12 | async-start | bytes 5640192 | tf_op jit(solution)/shard_map/reduce_scatter | solution.py:403
  566.4 181.5 %reduce-scatter.19.cloned.1.call-start = ((), (), s32[]{:S(2)}) async-start(), calls=%async_computation.15 | async-start | bytes 8460288
  581.8 290.3 %reduce-scatter.15.cloned.1.call-start = ((), (), s32[]{:S(2)}) async-start(), calls=%async_computation.13 | async-start | bytes 11280384 | tf_op jit(solution)/shard_map/reduce_scatter | solution.py:403
  599.8 396.2 %reduce-scatter.17.cloned.1.call-start = ((), (), s32[]{:S(2)}) async-start(), calls=%async_computation.14 | async-start | bytes 11280384 | tf_op jit(solution)/shard_map/reduce_scatter | solution.py:403
  617.6 378.5 %copy-start.36 = (f32[1152]{0:T(1024)S(1)}, f32[1152]{0:T(1024)}, u32[]{:S(2)}) copy-start(f32[1152]{0:T(1024)} %param.33) | copy-start | bytes 13828
  617.6 452.3 %all-reduce.6.cloned.1.call-start = ((), (), s32[]{:S(2)}) async-start(), calls=%async_computation.17 | async-start | bytes 4644864 | tf_op jit(solution)/shard_map/psum | solution.py:402
  (28 other events, 163.4 us)
Sparse Core Ops, SparseCore 0:
  11.0 59.0 all-gather.5
  72.3 70.7 all-gather.7
  145.2 41.6 all-gather.9
  189.1 87.3 all-gather.11
  278.6 86.9 all-gather.13
  483.3 62.6 reduce-scatter.20
  566.5 76.8 reduce-scatter.12
  648.0 99.8 reduce-scatter.18
  752.0 120.0 reduce-scatter.14
  876.0 119.9 reduce-scatter.16
Sparse Core Ops, SparseCore 1:
  11.5 53.5 reduce-scatter.10
  996.1 69.5 all-reduce.5

commit v2 on v1

--- a/solution.py
+++ b/solution.py
@@ -10,6 +10,7 @@
 HEADS = 16
 HD = 72
 D = 1152
+ROWS = 16
 EPS = 1e-05
 
 SCALE=HD**-0.5
@@ -164,6 +165,262 @@
     )(sidx,qkv,kvr,do,lt,dt)
 
 
+ERF_A = (
+    -2.72614225801306e-10, 2.77068142495902e-08, -2.10102402082508e-06, -5.69250639462346e-05,
+    -7.34990630326855e-04, -2.95459980854025e-03, -1.60960333262415e-02,
+)
+ERF_B = (
+    -1.45660718464996e-05, -2.13374055278905e-04, -1.68282697438203e-03, -7.37332916720468e-03,
+    -1.42647390514189e-02,
+)
+
+
+def erf(v):
+    v = jnp.clip(v, -4.0, 4.0)
+    square = v * v
+    top, bottom = ERF_A[0], ERF_B[0]
+    for term in ERF_A[1:]:
+        top = top * square + term
+    for term in ERF_B[1:]:
+        bottom = bottom * square + term
+    return v * top / bottom
+
+
+def mlp_up(act, weight, bias, tile=768):
+    rows, width = act.shape[0], weight.shape[1]
+
+    def kernel(a_ref, w_ref, b_ref, g_ref, d_ref):
+        u = dot(a_ref[...], w_ref[...]) + b_ref[...]
+        phi = 0.5 + 0.5 * erf(u * math.sqrt(0.5))
+        g_ref[...] = (u * phi).astype(jnp.bfloat16)
+        density = jnp.exp(u * u * -0.5) * (1.0 / math.sqrt(2.0 * math.pi))
+        d_ref[...] = (phi + u * density).astype(jnp.bfloat16)
+
+    out = jax.ShapeDtypeStruct((rows, width), jnp.bfloat16)
+    return pl.pallas_call(
+        kernel,
+        grid=(width // tile,),
+        out_shape=(out, out),
+        in_specs=[
+            pl.BlockSpec((rows, D), lambda t: (0, 0), pipeline_mode=pl.Buffered(1)),
+            pl.BlockSpec((D, tile), lambda t: (0, t)),
+            pl.BlockSpec((1, tile), lambda t: (0, t)),
+        ],
+        out_specs=(pl.BlockSpec((rows, tile), lambda t: (0, t)),) * 2,
+        compiler_params=pltpu.CompilerParams(vmem_limit_bytes=60 * 2**20),
+        cost_estimate=pl.CostEstimate(
+            flops=2 * rows * D * width, bytes_accessed=2 * D * width, transcendentals=rows * width
+        ),
+        name="mlp_up",
+    )(act, weight, bias.reshape(1, width))
+
+
+def ordered_transpose(at, value, held):
+    held[...] = value.astype(jnp.float32).T.reshape(held.shape)
+    blocks = []
+    for crel in (0, 1):
+        for yrel in (0, 1):
+            for zrel in range(4):
+                zz = lax.rem(at[0] + zrel, 4)
+                yy = at[1] + yrel - 2 * at[1] * yrel
+                cc = at[2] + crel - 2 * at[2] * crel
+                blocks.append(held[zz * 4 + yy * 2 + cc])
+    return jnp.concatenate(blocks, 0).astype(jnp.bfloat16)
+
+
+def mlp_back(at, act, grad, gelu, slope, w_up, w_down):
+    rows = act.shape[0]
+    half = rows // 2
+
+    def kernel(at, a_ref, e_ref, g_ref, s_ref, wu_ref, wd_ref, *refs):
+        dn_mine, dn_other, up_mine, up_other, h_ref, c_ref, b_ref, a_t, g_t, du_ref, held = refs
+        t = pl.program_id(0)
+        y, c, x = at[1], at[2], at[3]
+
+        @pl.when(t == 0)
+        def _():
+            a_t[...] = ordered_transpose(at, a_ref[...], held)
+            h_ref[...] = jnp.zeros_like(h_ref)
+            c_ref[...] = jnp.zeros_like(c_ref)
+
+        bias = None
+        for i in (0, 1):
+            part = slice(i * half, (i + 1) * half)
+            du = dot(e_ref[part], wd_ref[...], NT) * s_ref[part].astype(jnp.float32)
+            total = jnp.sum(du, axis=0, keepdims=True)
+            bias = total if bias is None else bias + total
+            du = du.astype(jnp.bfloat16)
+            du_ref[part] = du
+            h_ref[part] += dot(g_ref[part], wd_ref[...])
+            c_ref[part] += dot(du, wu_ref[...], NT)
+        b_ref[...] = bias
+        g_t[...] = g_ref[...].T
+        for yy in (0, 1):
+            both = dot(g_t[yy * 576 : yy * 576 + 576], e_ref[...])
+            low, high = both[:288], both[288:]
+            yrel = yy + y - 2 * yy * y
+            for ref, value in (
+                (dn_mine, jnp.where(c == 0, low, high)),
+                (dn_other, jnp.where(c == 0, high, low)),
+            ):
+                value = value.astype(jnp.bfloat16)
+                ref[x, 0, yrel] = value[:144]
+                ref[1 - x, 0, yrel] = value[144:]
+        for i, ref in ((0, up_mine), (1, up_other)):
+            both = dot(a_t[i * 576 : i * 576 + 576], du_ref[...])
+            for j in range(8):
+                ref[j // 4, j % 4] = both[j * 72 : j * 72 + 72].astype(jnp.bfloat16)
+
+    def part(t, at):
+        return lax.rem(at[0] + t, 4)
+
+    once = pl.Buffered(1)
+    down = jax.ShapeDtypeStruct((2, 4, 2, 144, D), jnp.bfloat16)
+    up = jax.ShapeDtypeStruct((2, 4, 72, 4 * D), jnp.bfloat16)
+    whole = jax.ShapeDtypeStruct((rows, D), jnp.float32)
+    down_spec = pl.BlockSpec((2, 1, 2, 144, D), lambda t, at: (0, t, 0, 0, 0))
+    up_spec = pl.BlockSpec((2, 4, 72, D), lambda t, at: (0, 0, 0, part(t, at)))
+    whole_spec = pl.BlockSpec((rows, D), lambda t, at: (0, 0), pipeline_mode=once)
+    by_column = pl.BlockSpec((rows, D), lambda t, at: (0, part(t, at)))
+    return pl.pallas_call(
+        kernel,
+        out_shape=(down, down, up, up, whole, whole, jax.ShapeDtypeStruct((1, 4 * D), jnp.float32)),
+        grid_spec=pltpu.PrefetchScalarGridSpec(
+            num_scalar_prefetch=1,
+            grid=(4,),
+            in_specs=[
+                whole_spec,
+                whole_spec,
+                by_column,
+                by_column,
+                pl.BlockSpec((D, D), lambda t, at: (0, part(t, at))),
+                pl.BlockSpec((D, D), lambda t, at: (part(t, at), 0)),
+            ],
+            out_specs=(
+                down_spec,
+                down_spec,
+                up_spec,
+                up_spec,
+                whole_spec,
+                whole_spec,
+                pl.BlockSpec((1, D), lambda t, at: (0, part(t, at))),
+            ),
+            scratch_shapes=[
+                pltpu.VMEM((D, rows), jnp.bfloat16),
+                pltpu.VMEM((D, rows), jnp.bfloat16),
+                pltpu.VMEM((rows, D), jnp.bfloat16),
+                pltpu.VMEM((16, 72, rows), jnp.float32),
+            ],
+        ),
+        compiler_params=pltpu.CompilerParams(vmem_limit_bytes=62 * 2**20),
+        cost_estimate=pl.CostEstimate(
+            flops=10 * rows * D * 4 * D, bytes_accessed=64 * 2**20, transcendentals=0
+        ),
+        name="mlp_back",
+    )(at, act, grad, gelu, slope, w_up, w_down)
+
+
+def qkv_back(at, act, act_far, grad, grad_far, weight):
+    rows, far = act.shape[0], act_far.shape[0]
+
+    def kernel(at, a_ref, f_ref, g_ref, h_ref, w_ref, mine, other, c_ref, a_t, f_t, held, held_far):
+        t = pl.program_id(0)
+
+        @pl.when(t == 0)
+        def _():
+            a_t[...] = ordered_transpose(at, a_ref[...], held)
+            f_t[...] = ordered_transpose(at, f_ref[...], held_far)
+            c_ref[...] = jnp.zeros_like(c_ref)
+
+        c_ref[...] += dot(g_ref[...], w_ref[...], NT)
+        away = jnp.where(t > 0, h_ref[...], jnp.zeros_like(h_ref))
+        for i, ref in ((0, mine), (1, other)):
+            part = slice(i * 576, (i + 1) * 576)
+            both = dot(a_t[part], g_ref[...]) + dot(f_t[part], away)
+            for j in range(8):
+                ref[j // 4, j % 4] = both[j * 72 : j * 72 + 72].astype(jnp.bfloat16)
+
+    once = pl.Buffered(1)
+    split = jax.ShapeDtypeStruct((2, 4, 72, 3 * D), jnp.bfloat16)
+    split_spec = pl.BlockSpec((2, 4, 72, D), lambda t, at: (0, 0, 0, t))
+    return pl.pallas_call(
+        kernel,
+        out_shape=(split, split, jax.ShapeDtypeStruct((rows, D), jnp.float32)),
+        grid_spec=pltpu.PrefetchScalarGridSpec(
+            num_scalar_prefetch=1,
+            grid=(3,),
+            in_specs=[
+                pl.BlockSpec((rows, D), lambda t, at: (0, 0), pipeline_mode=once),
+                pl.BlockSpec((far, D), lambda t, at: (0, 0), pipeline_mode=once),
+                pl.BlockSpec((rows, D), lambda t, at: (0, t)),
+                pl.BlockSpec((far, D), lambda t, at: (0, jnp.maximum(t - 1, 0))),
+                pl.BlockSpec((D, D), lambda t, at: (0, t)),
+            ],
+            out_specs=(
+                split_spec,
+                split_spec,
+                pl.BlockSpec((rows, D), lambda t, at: (0, 0), pipeline_mode=once),
+            ),
+            scratch_shapes=[
+                pltpu.VMEM((D, rows), jnp.bfloat16),
+                pltpu.VMEM((D, far), jnp.bfloat16),
+                pltpu.VMEM((16, 72, rows), jnp.float32),
+                pltpu.VMEM((16, 72, far), jnp.float32),
+            ],
+        ),
+        compiler_params=pltpu.CompilerParams(vmem_limit_bytes=60 * 2**20),
+        cost_estimate=pl.CostEstimate(
+            flops=16 * rows * D * D, bytes_accessed=40 * 2**20, transcendentals=0
+        ),
+        name="qkv_back",
+    )(at, act, act_far, grad, grad_far, weight)
+
+
+def skip_back(at, tok, skip, grad):
+    rows = tok.shape[0]
+
+    def kernel(at, t_ref, s_ref, g_ref, mine, other, in_t):
+        i = pl.program_id(0)
+
+        @pl.when(i == 0)
+        def _():
+            in_t[0:D] = t_ref[...].T
+            in_t[D:] = s_ref[...].T
+
+        first = pl.multiple_of(lax.rem(at[0] + i, 4) * 576, 16)
+        both = dot(in_t[pl.ds(first, 576)], g_ref[...])
+        for yy in (0, 1):
+            low, high = both[yy * 288 : yy * 288 + 144], both[yy * 288 + 144 : yy * 288 + 288]
+            yrel = yy + at[1] - 2 * yy * at[1]
+            for ref, value in (
+                (mine, jnp.where(at[2] == 0, low, high)),
+                (other, jnp.where(at[2] == 0, high, low)),
+            ):
+                value = value.astype(jnp.bfloat16)
+                ref[at[3], 0, yrel] = value[:72]
+                ref[1 - at[3], 0, yrel] = value[72:]
+
+    split = jax.ShapeDtypeStruct((2, 4, 2, 72, D), jnp.bfloat16)
+    split_spec = pl.BlockSpec((2, 1, 2, 72, D), lambda t, at: (0, t, 0, 0, 0))
+    whole_spec = pl.BlockSpec((rows, D), lambda t, at: (0, 0), pipeline_mode=pl.Buffered(1))
+    return pl.pallas_call(
+        kernel,
+        out_shape=(split, split),
+        grid_spec=pltpu.PrefetchScalarGridSpec(
+            num_scalar_prefetch=1,
+            grid=(4,),
+            in_specs=[whole_spec] * 3,
+            out_specs=(split_spec, split_spec),
+            scratch_shapes=[pltpu.VMEM((2 * D, rows), jnp.bfloat16)],
+        ),
+        compiler_params=pltpu.CompilerParams(vmem_limit_bytes=40 * 2**20),
+        cost_estimate=pl.CostEstimate(
+            flops=4 * rows * D * D, bytes_accessed=12 * 2**20, transcendentals=0
+        ),
+        name="skip_back",
+    )(at, tok, skip, grad)
+
+
 def layer_norm(hidden, gain, shift):
     centred = hidden - jnp.mean(hidden, axis=-1, keepdims=True)
     spread = jnp.mean(centred * centred, axis=-1, keepdims=True)
@@ -193,36 +450,6 @@
     return lax.dot_general(
         grad_rows, weight, (((1,), (1,)), ((), ())), preferred_element_type=jnp.float32
     )
-
-
-class PairAttention:
-    def __init__(self, qkv_all):
-        self.side = lax.axis_index("seq")
-        self.index = self.side.astype(jnp.int32).reshape(1)
-        self.qkv = qkv_all
-        self.away = jnp.where(self.side == 0, 256, 0)
-        sent = lax.dynamic_slice(qkv_all, (self.away, D), (REM, 2 * D))
-        self.kv_far = lax.ppermute(sent, "seq", [(0, 1), (1, 0)])
-
-    def forward(self):
-        self.out, self.lse = attn_fwd(self.index, self.qkv, self.kv_far, 288)
-        return self.out
-
-    def backward(self, d_att):
-        pick = (
-            lax.broadcasted_iota(jnp.int32, (D, HEADS), 0) // HD
-            == lax.broadcasted_iota(jnp.int32, (D, HEADS), 1)
-        ).astype(jnp.float32)
-        prod = d_att.astype(jnp.float32) * self.out.astype(jnp.float32)
-        row_dot = lax.dot_general(
-            pick, prod, (((0,), (1,)), ((), ())), precision=lax.Precision.HIGHEST
-        )
-        lse = self.lse[:, :HEADS].T
-        d_qkv, d_far = attn_bwd(self.index, self.qkv, self.kv_far, d_att, lse, row_dot)
-        back = lax.ppermute(d_far, "seq", [(0, 1), (1, 0)])
-        own = lax.dynamic_slice(d_qkv, (self.away, D), (REM, 2 * D))
-        total = (own.astype(jnp.float32) + back.astype(jnp.float32)).astype(jnp.bfloat16)
-        return lax.dynamic_update_slice(d_qkv, total, (self.away, D))
 
 
 class RowAttention:
@@ -348,10 +575,7 @@
     normed_one, ln1_back = jax.vjp(layer_norm, h_zero, ln1_gain, ln1_bias)
     act_one = normed_one.astype(jnp.bfloat16)
     qkv_all = fwd_dot(act_one, w_qkv).astype(jnp.bfloat16)
-    if lax.axis_size("seq") == 2 and row_count == 1 and local_len == 832:
-        attention = PairAttention(qkv_all)
-    else:
-        attention = RowAttention(qkv_all, offsets, row_count, local_len)
+    attention = RowAttention(qkv_all, offsets, row_count, local_len)
     att_low = attention.forward()
     h_one = h_zero + fwd_dot(att_low, w_proj) + proj_bias
     normed_two, ln2_back = jax.vjp(layer_norm, h_one, ln2_gain, ln2_bias)
@@ -410,6 +634,314 @@
     return (output, d_tokens, d_skip, *weight_grads, *vector_sums)
 
 
+YSW = [(b, b ^ 2) for b in range(16)]
+CSW = [(b, b ^ 1) for b in range(16)]
+ZUP = [(b, (b + 4) % 16) for b in range(16)]
+
+
+def swap_y(v):
+    return lax.ppermute(v, "batch", YSW)
+
+
+def swap_core(v):
+    return lax.ppermute(v, "batch", CSW)
+
+
+def next_z(v):
+    return lax.ppermute(v, "batch", ZUP)
+
+
+def swap_seq(v):
+    return lax.ppermute(v, "seq", [(0, 1), (1, 0)])
+
+
+def place():
+    b = lax.axis_index("batch").astype(jnp.int32)
+    return b // 4, (b // 2) % 2, b % 2
+
+
+def f32(v):
+    return v.astype(jnp.float32)
+
+
+def b16(v):
+    return v.astype(jnp.bfloat16)
+
+
+def core_pair(shard):
+    core = place()[2]
+    half = shard.shape[1] // 2
+    low, high = shard[:, :half], shard[:, half:]
+    keep = jnp.where(core == 0, low, high)
+    got = swap_core(jnp.where(core == 0, high, low))
+    return jnp.where(
+        core == 0, jnp.concatenate([keep, got], 0), jnp.concatenate([got, keep], 0)
+    )
+
+
+def tied(*values):
+    return lax.optimization_barrier(values)
+
+
+def with_core(own):
+    return own + [swap_core(v) for v in own]
+
+
+def assemble(pieces, halves):
+    rows, cols = pieces[0].shape
+    shape = (8 * rows, 2 * cols) if halves else (16 * rows, cols)
+
+    def kernel(at, *refs):
+        ins, out, held, came, left = refs[:16], refs[16], refs[17], refs[18], refs[19]
+        z, y, c = at[0], at[1], at[2]
+        loads = [
+            pltpu.make_async_copy(ins[j], held.at[j], came.at[j]) for j in range(16)
+        ]
+        for load in loads:
+            load.start()
+        stores = []
+        for j in range(16):
+            core = c if j < 8 else 1 - c
+            yy = y if j % 8 < 4 else 1 - y
+            zz = lax.rem(z - j % 4 + 4, 4)
+            if halves:
+                first = pl.multiple_of((zz * 2 + yy) * rows, 16)
+                target = out.at[
+                    pl.ds(first, rows), pl.ds(pl.multiple_of(core * cols, 128), cols)
+                ]
+            else:
+                first = pl.multiple_of((zz * 4 + yy * 2 + core) * rows, 16)
+                target = out.at[pl.ds(first, rows), :]
+            loads[j].wait()
+            stores.append(pltpu.make_async_copy(held.at[j], target, left.at[j]))
+            stores[-1].start()
+        for store in stores:
+            store.wait()
+
+    return pl.pallas_call(
+        kernel,
+        out_shape=jax.ShapeDtypeStruct(shape, pieces[0].dtype),
+        in_specs=[pl.BlockSpec(memory_space=pltpu.SMEM)]
+        + [pl.BlockSpec(memory_space=pl.ANY)] * 16,
+        out_specs=pl.BlockSpec(memory_space=pl.ANY),
+        scratch_shapes=[
+            pltpu.VMEM((16, rows, cols), pieces[0].dtype),
+            pltpu.SemaphoreType.DMA((16,)),
+            pltpu.SemaphoreType.DMA((16,)),
+        ],
+        compiler_params=pltpu.CompilerParams(vmem_limit_bytes=16 * 2**20),
+        cost_estimate=pl.CostEstimate(
+            flops=0, bytes_accessed=64 * rows * cols, transcendentals=0
+        ),
+        name="assemble",
+    )(jnp.stack(place()), *pieces)
+
+
+def take(v, axis, index):
+    return lax.dynamic_index_in_dim(v, index, axis, keepdims=False)
+
+
+def added(left, right):
+    return b16(f32(left) + f32(right))
+
+
+def by_side(side, own, other):
+    own, other = f32(own), f32(other)
+    return jnp.where(
+        side == 0, jnp.concatenate([own, other], 0), jnp.concatenate([other, own], 0)
+    )
+
+
+def vector_step(value, bit, axis="batch"):
+    if axis == "seq":
+        return value + swap_seq(value)
+    return value + lax.ppermute(value, "batch", [(b, b ^ bit) for b in range(16)])
+
+
+def sc_scatter(grad):
+    part = lax.psum_scatter(grad, "batch", scatter_dimension=0, tiled=True)
+    return f32(part) + f32(swap_seq(part))
+
+
+def per_device_pair(
+    tokens,
+    skip_parts,
+    lengths,
+    cotangent,
+    skip_w,
+    qkv_w,
+    proj_w,
+    fc1_w,
+    fc2_w,
+    skip_bias,
+    ln1_gain,
+    ln1_bias,
+    proj_bias,
+    ln2_gain,
+    ln2_bias,
+    fc1_bias,
+    fc2_bias,
+):
+    count = tokens.shape[1]
+    side = lax.axis_index("seq").astype(jnp.int32)
+    index = side.reshape(1)
+    at = jnp.stack([*place(), side])
+    shared = jnp.where(side == 0, 256, 0)
+    live = (
+        (side * count + lax.broadcasted_iota(jnp.int32, (count, 1), 0)) < jnp.sum(lengths)
+    ).astype(jnp.float32)
+
+    parts = skip_parts.reshape(2, count, D)
+    skip_far = swap_seq(take(parts, 0, 1 - side))
+    tok_flat = tokens.reshape(count, D)
+
+    q0 = core_pair(jnp.concatenate([qkv_w, proj_w], 1))
+    s0 = skip_w
+    s1, t0 = next_z(s0), swap_y(s0)
+    s1, t0 = tied(s1, t0)
+    s2, t1 = next_z(s1), swap_y(s1)
+    s2, t1, s1, q0 = tied(s2, t1, s1, q0)
+    s3, t2, q1 = next_z(s2), swap_y(s2), next_z(q0)
+    s3, t2, s2, q0 = tied(s3, t2, s2, q0)
+    t3, r0 = swap_y(s3), swap_y(q0)
+    w_skip = assemble(with_core([s0, s1, s2, s3, t0, t1, t2, t3]), False)
+    r0, q1, w_skip, skip_far = tied(r0, q1, w_skip, skip_far)
+    q2, r1 = next_z(q1), swap_y(q1)
+    skip_flat = b16(f32(take(parts, 0, side)) + f32(skip_far))
+    h_zero = fwd_dot(tok_flat, w_skip[:D]) + fwd_dot(skip_flat, w_skip[D:]) + skip_bias
+    normed_one, ln1_back = jax.vjp(layer_norm, h_zero, ln1_gain, ln1_bias)
+    act_one = b16(normed_one)
+    act_send = lax.dynamic_slice(act_one, (shared, 0), (REM, D))
+    q2, r1, act_one, act_send = tied(q2, r1, act_one, act_send)
+    act_far = swap_seq(act_send)
+    u0 = core_pair(fc1_w)
+    q3, r2 = next_z(q2), swap_y(q2)
+    q3, r2, u0, q2 = tied(q3, r2, u0, q2)
+    r3, u1 = swap_y(q3), next_z(u0)
+    r3, u1, q3 = tied(r3, u1, q3)
+    u2, v0 = next_z(u1), swap_y(u0)
+    w_qp = assemble(with_core([q0, q1, q2, q3, r0, r1, r2, r3]), True)
+    w_qkv, w_proj = w_qp[:, : 3 * D], w_qp[:, 3 * D :]
+    qkv = b16(fwd_dot(act_one, w_qkv))
+    kv_far = b16(fwd_dot(act_far, w_qkv[:, D:]))
+    u2, v0, qkv, kv_far, fc2_w = tied(u2, v0, qkv, kv_far, fc2_w)
+    w_down = lax.all_gather(fc2_w, "batch", axis=0, tiled=True)
+    u3, v1, v2 = next_z(u2), swap_y(u1), swap_y(u2)
+    att, lse = attn_fwd(index, qkv, kv_far, 288)
+    u3, v1, v2, att = tied(u3, v1, v2, att)
+    v3 = swap_y(u3)
+    h_one = h_zero + fwd_dot(att, w_proj) + proj_bias
+    normed_two, ln2_back = jax.vjp(layer_norm, h_one, ln2_gain, ln2_bias)
+    act_two = b16(normed_two)
+    w_up = assemble(with_core([u0, u1, u2, u3, v0, v1, v2, v3]), True)
+    gelu_low, slope = mlp_up(act_two, w_up, fc1_bias)
+
+    grad_two = f32(cotangent.reshape(count, D)) * live
+    grad_low = b16(grad_two)
+    dn, dn_got, up, up_got, h_add, d_act_two, d_up_bias = mlp_back(
+        at, act_two, grad_low, gelu_low, slope, w_up, w_down
+    )
+    dn_got, up_got, d_act_two = tied(dn_got, up_got, d_act_two)
+    dn_got, up_got = swap_core(dn_got), swap_core(up_got)
+    output = b16((h_one + h_add + fc2_bias) * live).reshape(1, count, D)
+    d_h_one, d_ln2_gain, d_ln2_bias = ln2_back(d_act_two)
+    d_h_one = d_h_one + grad_two
+    proj_low = b16(d_h_one)
+    d_att = b16(back_dot(proj_low, w_proj))
+    d_proj = b16(contract_rows(att, proj_low))
+    dn_got, up_got, d_att, d_proj = tied(dn_got, up_got, d_att, d_proj)
+    out_proj = sc_scatter(d_proj)
+    dn_send, up_send = added(dn[1], dn_got[1]), added(up[1], up_got[1])
+    dn_got_x, up_got_y = swap_seq(dn_send), swap_y(up_send)
+    dn, up = added(dn[0], dn_got[0]), added(up[0], up_got[0])
+    pick = (
+        lax.broadcasted_iota(jnp.int32, (D, HEADS), 0) // HD
+        == lax.broadcasted_iota(jnp.int32, (D, HEADS), 1)
+    ).astype(jnp.float32)
+    row_dot = lax.dot_general(
+        pick, f32(d_att) * f32(att), (((0,), (1,)), ((), ())), precision=lax.Precision.HIGHEST
+    )
+    d_qkv, d_far = attn_bwd(index, qkv, kv_far, d_att, lse[:, :HEADS].T, row_dot)
+    dn, up, dn_got, up_got, d_qkv, d_far = tied(dn, up, dn_got_x, up_got_y, d_qkv, d_far)
+    dn_next, up_next = added(dn[3], dn_got[3]), added(up[3], up_got[3])
+    dn_next, up_next = next_z(dn_next), next_z(up_next)
+    far = b16(back_dot(d_far, w_qkv[:, D:]))
+    dn_next, up_next, far, d_far, d_qkv = tied(dn_next, up_next, far, d_far, d_qkv)
+    far = swap_seq(far)
+    dn_next, up_next = (
+        next_z(b16(f32(dn[2]) + f32(dn_got[2]) + f32(dn_next))),
+        next_z(b16(f32(up[2]) + f32(up_got[2]) + f32(up_next))),
+    )
+    q, q_got, d_act_one = qkv_back(at, act_one, act_far, d_qkv, d_far, w_qkv)
+    dn_next, up_next, far, d_act_one, q_got = tied(dn_next, up_next, far, d_act_one, q_got)
+    q_got = swap_core(q_got)
+    dn_next, up_next = (
+        next_z(b16(f32(dn[1]) + f32(dn_got[1]) + f32(dn_next))),
+        next_z(b16(f32(up[1]) + f32(up_got[1]) + f32(up_next))),
+    )
+    here = lax.dynamic_slice(d_act_one, (shared, 0), (REM, D))
+    d_act_one = lax.dynamic_update_slice(d_act_one, here + f32(far), (shared, 0))
+    d_h_zero, d_ln1_gain, d_ln1_bias = ln1_back(d_act_one)
+    d_h_zero = d_h_zero + d_h_one
+    zero_low = b16(d_h_zero)
+    q_got, zero_low = tied(q_got, zero_low)
+    q_send = added(q[1], q_got[1])
+    q_got_y = swap_y(q_send)
+    q = added(q[0], q_got[0])
+    k, k_got = skip_back(at, tok_flat, skip_flat, zero_low)
+    sums = jnp.concatenate(
+        [
+            jnp.sum(d_h_zero, axis=0),
+            d_ln1_gain,
+            d_ln1_bias,
+            jnp.sum(d_h_one, axis=0),
+            d_ln2_gain,
+            d_ln2_bias,
+            d_up_bias[0],
+            jnp.sum(grad_two, axis=0),
+        ]
+    ).reshape(-1, 128)
+    dn_next, up_next, k, k_got, zero_low = tied(dn_next, up_next, k, k_got, zero_low)
+    d_tokens = back_dot(zero_low, w_skip[:D]).reshape(1, count, D)
+    dn_sum = b16(f32(dn[0]) + f32(dn_got[0]) + f32(dn_next))
+    up_sum = b16(f32(up[0]) + f32(up_got[0]) + f32(up_next))
+    dn_next, up_next, k_got = swap_y(dn_sum[1]), swap_seq(up_sum), swap_core(k_got)
+    sums = vector_step(sums, 1)
+    out_up = f32(up_sum) + f32(up_next)
+    q, q_got, k, k_got, dn_next, dn_sum, sums, zero_low, d_tokens = tied(
+        q, q_got_y, k, k_got, dn_next, dn_sum, sums, zero_low, d_tokens
+    )
+    d_skip = back_dot(zero_low, w_skip[D:]).reshape(1, count, D)
+    q_next = next_z(added(q[3], q_got[3]))
+    k_got_x = swap_seq(added(k[1], k_got[1]))
+    k = added(k[0], k_got[0])
+    dn_sum = added(dn_sum[0], dn_next)
+    dn_next = swap_seq(dn_sum)
+    sums = vector_step(sums, 2)
+    q, q_next, q_got, dn_next, sums, d_skip = tied(q, q_next, q_got, dn_next, sums, d_skip)
+    out_down = by_side(side, dn_sum, dn_next)
+    q_next = next_z(b16(f32(q[2]) + f32(q_got[2]) + f32(q_next)))
+    sums = vector_step(sums, 4)
+    q, q_next, q_got, k, k_got, sums = tied(q, q_next, q_got, k, k_got_x, sums)
+    q_next = next_z(b16(f32(q[1]) + f32(q_got[1]) + f32(q_next)))
+    k_next = next_z(added(k[3], k_got[3]))
+    sums = vector_step(sums, 8)
+    q, q_next, q_got, k_next, k, k_got, sums = tied(q, q_next, q_got, k_next, k, k_got, sums)
+    q_sum = b16(f32(q[0]) + f32(q_got[0]) + f32(q_next))
+    q_next = swap_seq(q_sum)
+    out_qkv = f32(q_sum) + f32(q_next)
+    sums = vector_step(sums, 0, "seq").reshape(-1)
+    k_next = next_z(b16(f32(k[2]) + f32(k_got[2]) + f32(k_next)))
+    k_next = next_z(b16(f32(k[1]) + f32(k_got[1]) + f32(k_next)))
+    k_sum = b16(f32(k[0]) + f32(k_got[0]) + f32(k_next))
+    k_sum = added(k_sum[0], swap_y(k_sum[1]))
+    out_skip = by_side(side, k_sum, swap_seq(k_sum))
+    starts = [0, D, 2 * D, 3 * D, 4 * D, 5 * D, 6 * D, 10 * D, 11 * D]
+    sums = [sums[a:b] for a, b in zip(starts, starts[1:])]
+    grads = (out_skip, out_qkv, out_proj, out_up, out_down)
+    return (output, d_tokens, d_skip, *grads, *sums)
+
+
 def solution(mesh):
     in_specs = (
         P("batch", "seq", None),
@@ -420,6 +952,12 @@
         *(P(),) * 8,
     )
     out_specs = (*(P("batch", "seq", None),) * 3, *(P("batch", None),) * 5, *(P(),) * 8)
+    pair = mesh.shape["batch"] == ROWS and mesh.shape["seq"] == 2
     return jax.shard_map(
-        per_device, mesh=mesh, in_specs=in_specs, out_specs=out_specs, check_vma=False
-    )
+        per_device_pair if pair else per_device,
+        mesh=mesh,
+        in_specs=in_specs,
+        out_specs=out_specs,
+        check_vma=False,
+
+    )

time: 1090 us -> 742 us (0.68)
  waiting for transfers between devices: 662 us -> 236 us
  matrix products: 240 us -> 63.2 us
  Pallas kernels: 86.8 us -> 256 us
  other arithmetic: 23 us -> 74.4 us
  starting transfers between devices: 2.57 us -> 52.1 us
  blocking collectives: 42.7 us -> 0 us
  local copies, waits for them, and re-layouts: 13.5 us -> 36 us
    reduce_scatter x4 -> x0, waiting for transfers between devices: 274 us -> none  [the longest x3 274 us: per_device(): lax.psum_scatter(grad.astype(jnp.bfloat16), 'batch', scatter_dimension=0,...]
    all_gather x5 -> x1, waiting for transfers between devices: 170 us -> 0.01 us  [per_device_pair(): w_down = lax.all_gather(fc2_w, 'batch', axis=0, tiled=True)]
    pallas_call x0 -> x7, Pallas kernels: none -> 168 us  [the longest x1 70.9 us: mlp_back(): pl.pallas_call(kernel, out_shape=(down, down, up, up, whole, whole, jax.S...]
    ppermute x2 -> x82, waiting for transfers between devices: 109 us -> 236 us  [the longest x21 106 us: next_z(): return lax.ppermute(v, 'batch', ZUP)]
    unnamed x14 -> x3, waiting for transfers between devices: 108 us -> 0.04 us
    dot_general x6 -> x5, matrix products: 98.1 us -> 27.1 us  [fwd_dot(): return jnp.dot(left, right, preferred_element_type=jnp.float32)]
    dot_general x6 -> x1, matrix products: 64.3 us -> 4.73 us  [contract_rows(): lax.dot_general(left, right, (((0,), (0,)), ((), ())), preferred_element_...]
    ppermute x2 -> x82, starting transfers between devices: 1.47 us -> 52 us  [the longest x16 18.1 us: swap_y(): return lax.ppermute(v, 'batch', YSW)]
  transfers between devices with their start and end apart: 14 -> 84, of which waited for: 10 -> 26; matrix products, arithmetic and copies ran while one was open for 19% -> 20% of each run, Pallas kernels for 3% -> 25%
where the time goes in v2:
time: 742 us; the launch traced here: 733 us
  Pallas kernels  256 us (35%)
  waiting for transfers between devices  236 us (32%)
  other arithmetic  74.4 us (10%)
  matrix products  63.2 us (9%)
  starting transfers between devices  52.1 us (7%)
  local copies, waits for them, and re-layouts  36 us (5%)
  between operations  15.6 us (2%)
    ppermute x21, waiting for transfers between devices, next_z(): return lax.ppermute(v, 'batch', ZUP)  106 us
    ppermute x16, waiting for transfers between devices, swap_y(): return lax.ppermute(v, 'batch', YSW)  81.4 us
    pallas_call x1, Pallas kernels, mlp_back(): pl.pallas_call(kernel, out_shape=(down, down, up, up, whole, whole, jax.S...  70.9 us
    pallas_call x1, Pallas kernels, attn_bwd(): pl.pallas_call(lambda *r: bwd_kernel(*r, kstep=kstep, expl=expl), out_sha...  56.5 us
    pallas_call x1, Pallas kernels, mlp_up(): pl.pallas_call(kernel, grid=(width // tile,), out_shape=(out, out), in_sp...  42 us
    convert_element_type x23, other arithmetic, b16(): return v.astype(jnp.bfloat16)  40 us
    pallas_call x1, Pallas kernels, qkv_back(): pl.pallas_call(kernel, out_shape=(split, split, jax.ShapeDtypeStruct((row...  31.8 us
    pallas_call x1, Pallas kernels, attn_fwd(): pl.pallas_call(lambda *r: fwd_kernel(*r, qstep=qstep), out_shape=(jax.Sha...  31 us
  transfers between devices with their start and end apart: 84, of which 26 were waited for; matrix products, arithmetic and copies ran while one was open for 20% of the time, Pallas kernels for 25%

profile of v2, /device:TPU:0, one launch (start us, length us, event | category | flops | bytes accessed | tf_op | source)
XLA Modules:
  0.0 732.5 jit_solution(4080972983027213733)
XLA Ops:
  23.0 8.1 %collective-permute-done.2.refs_2_ = bf16[144,1152]{1,0:T(8,128)(2,1)S(1)} collective-permute-done((bf16[144,1152]{1,0:T(8,128)(2,1)S(1)}, bf16[144,1152]{1,0:T(8,128)(2,1)S(1)}, u32[]{:S(2)}, u32[]{:S(2)}) %collective-permute-start.2) | collective-permute-done | bytes 331808 | tf_op jit(solution)/shard_map/ppermute | solution.py:651
  33.0 8.0 %collective-permute-done.5.refs_3_ = bf16[144,1152]{1,0:T(8,128)(2,1)S(1)} collective-permute-done((bf16[144,1152]{1,0:T(8,128)(2,1)S(1)}, bf16[144,1152]{1,0:T(8,128)(2,1)S(1)}, u32[]{:S(2)}, u32[]{:S(2)}) %collective-permute-start.5) | collective-permute-done | bytes 331808 | tf_op jit(solution)/shard_map/ppermute | solution.py:651
  82.0 7.1 collective-permute-done.19.refs_2_
  90.3 16.3 %collective-permute-done.21.refs_3_ = bf16[144,2304]{1,0:T(8,128)(2,1)S(1)} collective-permute-done((bf16[144,2304]{1,0:T(8,128)(2,1)S(1)}, bf16[144,2304]{1,0:T(8,128)(2,1)S(1)}, u32[]{:S(2)}, u32[]{:S(2)}) %collective-permute-start.21) | collective-permute-done | bytes 663584 | tf_op jit(solution)/shard_map/ppermute | solution.py:651
  108.2 13.2 %collective-permute-done.24.refs_7_ = bf16[144,2304]{1,0:T(8,128)(2,1)S(1)} collective-permute-done((bf16[144,2304]{1,0:T(8,128)(2,1)S(1)}, bf16[144,2304]{1,0:T(8,128)(2,1)S(1)}, u32[]{:S(2)}, u32[]{:S(2)}) %collective-permute-start.24) | collective-permute-done | bytes 663584 | tf_op jit(solution)/shard_map/ppermute | solution.py:643
  134.1 9.6 %convolution_convert_fusion.1.r_1_ = bf16[832,3456]{1,0:T(8,128)(2,1)} fusion(bf16[832,1152]{1,0:T(8,128)(2,1)S(1)} %add_convert_fusion.7.a_ref, bf16[1152,4608]{1,0:T(8,128)(2,1)S(1)} %assemble.4), kind=kOutput, calls=%fused_computation.1 | convolution fusion | flops 6627778560 | bytes 15630336 | tf_op jit(solution)/shard_map/dot_general | solution.py:440
  143.7 12.4 %collective-permute-done.36.f_ref = bf16[576,1152]{1,0:T(8,128)(2,1)S(1)} collective-permute-done((bf16[576,1152]{1,0:T(8,128)(2,1)S(1)}, bf16[576,1152]{1,0:T(8,128)(2,1)S(1)}, u32[]{:S(2)}, u32[]{:S(2)}) %collective-permute-start.36) | collective-permute-done | bytes 1327136 | tf_op jit(solution)/shard_map/ppermute | solution.py:655
  167.1 31.0 %attn_fwd.1 = (bf16[832,1152]{1,0:T(8,128)(2,1)}, f32[832,128]{1,0:T(8,128)}) custom-call(s32[1]{0:T(128)} %bitcast.8.r_0_, bf16[832,3456]{1,0:T(8,128)(2,1)} %convolution_convert_fusion.1.r_1_, bf16[576,2304]{1,0:T(8,128)(2,1)} %fusion.4.r_2_), custom_call_target="tpu_custom_call" | custom-call | tf_op jit(solution)/shard_map/attn_fwd/pallas_call | solution.py:95
  208.2 16.8 %collective-permute-done.40.refs_7_ = bf16[144,2304]{1,0:T(8,128)(2,1)S(1)} collective-permute-done((bf16[144,2304]{1,0:T(8,128)(2,1)S(1)}, bf16[144,2304]{1,0:T(8,128)(2,1)S(1)}, u32[]{:S(2)}, u32[]{:S(2)}) %collective-permute-start.40) | collective-permute-done | bytes 663584 | tf_op jit(solution)/shard_map/ppermute | solution.py:643
  235.7 42.0 %mlp_up.1 = (bf16[832,4608]{1,0:T(8,128)(2,1)}, bf16[832,4608]{1,0:T(8,128)(2,1)}) custom-call(bf16[832,1152]{1,0:T(8,128)(2,1)} %get-tuple-element.280.a_ref, bf16[1152,4608]{1,0:T(8,128)(2,1)} %copy-done.1, f32[1,4608]{1,0:T(1,128)} %reshape.237.b_ref), custom_call_target="tpu_custom_call" | custom-call | flops 8833204224 | bytes 10616832 | tf_op jit(solution)/shard_map/mlp_up/pallas_call | solution.py:200
  277.8 70.9 %mlp_back.1 = (bf16[2,4,2,144,1152]{4,3,2,1,0:T(8,128)(2,1)}, bf16[2,4,2,144,1152]{4,3,2,1,0:T(8,128)(2,1)}, bf16[2,4,72,4608]{3,2,1,0:T(8,128)(2,1)}, bf16[2,4,...) custom-call(s32[4]{0:T(128)} %pad_add_fusion.1.at, ...), custom_call_target="tpu_custom_call" | custom-call | flops 44166021120 | bytes 67108864 | tf_op jit(solution)/shard_map/mlp_back/pallas_call | solution.py:285
  367.3 7.1 convolution_convert_fusion.2.r_3_
  388.0 6.9 slice.316.w_ref
  402.2 56.5 %attn_bwd.1 = (bf16[832,3456]{1,0:T(8,128)(2,1)}, bf16[576,2304]{1,0:T(8,128)(2,1)}) custom-call(s32[1]{0:T(128)} %bitcast.8.r_0_, bf16[832,3456]{1,0:T(8,128)(2,1)} %convolution_convert_fusion.1.r_1_, bf16[576,2304]{1,0:T(8,128)(2,1)} %fusion.4.r_2_, bf16[832,1152]{1,0:T(8,128)(2,1)} %convolution_convert_fusion.2.r_3_, f32[16,832]{1,0:T(8,128)} %slice_bitcast_fusion.3.r_4_, ...), custom_call_target="tpu_custom_call" | custom-call | tf_op jit(solution)/shard_map/attn_bwd/pallas_call | solution.py:157
  461.7 7.2 fusion.17
  468.9 12.5 %collective-permute-done.54 = bf16[72,4608]{1,0:T(8,128)(2,1)S(1)} collective-permute-done((bf16[72,4608]{1,0:T(8,128)(2,1)S(1)}, bf16[72,4608]{1,0:T(8,128)(2,1)S(1)}, u32[]{:S(2)}, u32[]{:S(2)}) %collective-permute-start.54) | collective-permute-done | bytes 663584 | tf_op jit(solution)/shard_map/ppermute | solution.py:651
  481.5 13.9 %collective-permute-done.53 = bf16[2,144,1152]{2,1,0:T(8,128)(2,1)S(1)} collective-permute-done((bf16[2,144,1152]{2,1,0:T(8,128)(2,1)S(1)}, bf16[2,144,1152]{2,1,0:T(8,128)(2,1)S(1)}, u32[]{:S(2)}, u32[]{:S(2)}) %collective-permute-start.53) | collective-permute-done | bytes 663584 | tf_op jit(solution)/shard_map/ppermute | solution.py:651
  499.9 31.8 %qkv_back.1 = (bf16[2,4,72,3456]{3,2,1,0:T(8,128)(2,1)}, bf16[2,4,72,3456]{3,2,1,0:T(8,128)(2,1)}, f32[832,1152]{1,0:T(8,128)}) custom-call(s32[4]{0:T(128)} %pad_add_fusion.1.at, bf16[832,1152]{1,0:T(8,128)(2,1)} %copy-done.41, bf16[576,1152]{1,0:T(8,128)(2,1)} %copy-done.70, bf16[832,3456]{1,0:T(8,128)(2,1)} %get-tuple-element.184.g_ref, ...), custom_call_target="tpu_custom_call" | custom-call | flops 17666408448 | bytes 41943040 | tf_op jit(solution)/shard_map/qkv_back/pallas_call | solution.py:346
  551.8 9.9 %skip_back.1 = (bf16[2,4,2,72,1152]{4,3,2,1,0:T(8,128)(2,1)S(1)}, bf16[2,4,2,72,1152]{4,3,2,1,0:T(8,128)(2,1)}) custom-call(s32[4]{0:T(128)S(1)} %copy-done.26, bf16[832,1152]{1,0:T(8,128)(2,1)S(1)} %bitcast.143, bf16[832,1152]{1,0:T(8,128)(2,1)S(1)} %copy-done.6, bf16[832,1152]{1,0:T(8,128)(2,1)S(1)} %get-tuple-element.212.g_ref), custom_call_target="tpu_custom_call" | custom-call | flops 4416602112 | bytes 12582912 | tf_op jit(solution)/shard_map/skip_back/pallas_call | solution.py:406
  582.9 40.2 %collective-permute-done.63 = bf16[144,1152]{1,0:T(8,128)(2,1)S(1)} collective-permute-done((bf16[144,1152]{1,0:T(8,128)(2,1)S(1)}, bf16[144,1152]{1,0:T(8,128)(2,1)S(1)}, u32[]{:S(2)}, u32[]{:S(2)}) %collective-permute-start.63) | collective-permute-done | bytes 331808 | tf_op jit(solution)/shard_map/ppermute | solution.py:643
  647.1 9.6 %collective-permute-done.68 = bf16[72,3456]{1,0:T(8,128)(2,1)S(1)} collective-permute-done((bf16[72,3456]{1,0:T(8,128)(2,1)S(1)}, bf16[72,3456]{1,0:T(8,128)(2,1)S(1)}, u32[]{:S(2)}, u32[]{:S(2)}) %collective-permute-start.68) | collective-permute-done | bytes 497696 | tf_op jit(solution)/shard_map/ppermute | solution.py:651
  656.7 10.7 %collective-permute-done.69 = bf16[4,2,72,1152]{3,2,1,0:T(8,128)(2,1)S(1)} collective-permute-done((bf16[4,2,72,1152]{3,2,1,0:T(8,128)(2,1)S(1)}, bf16[4,2,72,1152]{3,2,1,0:T(8,128)(2,1)S(1)}, u32[]{:S(2)}, u32[]{:S(2)}) %collective-permute-start.69) | collective-permute-done | bytes 1327136 | tf_op jit(solution)/shard_map/ppermute | solution.py:655
  673.5 19.7 %collective-permute-done.73 = f32[99,128]{1,0:T(8,128)S(1)} collective-permute-done((f32[99,128]{1,0:T(8,128)S(1)}, f32[99,128]{1,0:T(8,128)S(1)}, u32[]{:S(2)}, u32[]{:S(2)}) %collective-permute-start.73) | collective-permute-done | bytes 50720 | tf_op jit(solution)/shard_map/ppermute | solution.py:758
  696.4 7.8 %collective-permute-done.74 = bf16[2,72,1152]{2,1,0:T(8,128)(2,1)S(1)} collective-permute-done((bf16[2,72,1152]{2,1,0:T(8,128)(2,1)S(1)}, bf16[2,72,1152]{2,1,0:T(8,128)(2,1)S(1)}, u32[]{:S(2)}, u32[]{:S(2)}) %collective-permute-start.74) | collective-permute-done | bytes 331808 | tf_op jit(solution)/shard_map/ppermute | solution.py:651
  (408 shorter events, 247.7 us)
Async XLA Ops:
  7.2 270.6 %all-gather.2.cloned.1.call-start = ((), (), s32[]{:S(2)}) async-start(), calls=%async_computation.1 | async-start | bytes 11280384 | tf_op jit(solution)/shard_map/all_gather | solution.py:828
  16.1 54.7 %collective-permute-start.18 = (bf16[832,1152]{1,0:T(8,128)(2,1)}, bf16[832,1152]{1,0:T(8,128)(2,1)}, u32[]{:S(2)}, u32[]{:S(2)}) collective-permute-start(bf16[832,1152]{1,0:T(8,128)(2,1)} %dynamic-slice_bitcast_fusion), channel_id=1, source_target_pairs={{0,1},{1,0},{2,3},{3,2},{4,5},{5,4},{6,7},{7,6},{8,9},{9,8},{10,11... | collective-permute-start | bytes 5750792 | tf_op jit(solution)/shard_map/ppermute | solution.py:655
  57.6 32.7 %collective-permute-start.23 = (bf16[72,2304]{1,0:T(8,128)(2,1)}, bf16[72,2304]{1,0:T(8,128)(2,1)S(1)}, u32[]{:S(2)}, u32[]{:S(2)}) collective-permute-start(bf16[72,2304]{1,0:T(8,128)(2,1)} %get-tuple-element.265), channel_id=1, source_target_pairs={{0,2},{2,0},{4,6},{6,4},{8,10},{10,8},{12,14},{14,12},{16,18},{18,... | collective-permute-start | bytes 995336 | tf_op jit(solution)/shard_map/ppermute | solution.py:647
  124.9 31.1 %collective-permute-start.36 = (bf16[576,1152]{1,0:T(8,128)(2,1)S(1)}, bf16[576,1152]{1,0:T(8,128)(2,1)S(1)}, u32[]{:S(2)}, u32[]{:S(2)}) collective-permute-start(bf16[576,1152]{1,0:T(8,128)(2,1)S(1)} %constant_dynamic-slice_fusion), channel_id=1, source_target_pairs={{0,1},{1,0},{2,3},{3,2},{4,5},{5,4},{6,7},{7,6},{8,9},{9,8},{10,11... | collective-permute-start | bytes 3981320 | tf_op jit(solution)/shard_map/ppermute | solution.py:655
  126.4 34.5 %collective-permute-start.27 = (bf16[144,2304]{1,0:T(8,128)(2,1)S(1)}, bf16[144,2304]{1,0:T(8,128)(2,1)S(1)}, u32[]{:S(2)}, u32[]{:S(2)}) collective-permute-start(bf16[144,2304]{1,0:T(8,128)(2,1)S(1)} %maximum_select_fusion.2.refs_0_), channel_id=1, source_target_pairs={{0,4},{2,6},{4,0},{6,2},{8,12},{10,14},{12,8},{14,10},{16,20},{18,... | collective-permute-start | bytes 1990664 | tf_op jit(solution)/shard_map/ppermute | solution.py:643
  127.0 34.7 %collective-permute-start.26 = (bf16[144,2304]{1,0:T(8,128)(2,1)S(1)}, bf16[144,2304]{1,0:T(8,128)(2,1)}, u32[]{:S(2)}, u32[]{:S(2)}) collective-permute-start(bf16[144,2304]{1,0:T(8,128)(2,1)S(1)} %collective-permute-done.25.refs_1_), channel_id=1, source_target_pairs={{0,8},{2,10},{4,12},{6,14},{8,16},{10,18},{12,20},{14,22},{16,24},... | collective-permute-start | bytes 1990664 | tf_op jit(solution)/shard_map/ppermute | solution.py:651
  161.8 409.7 %reduce-scatter.4.cloned.1.call-start = ((), (), s32[]{:S(2)}) async-start(), calls=%async_computation.2 | async-start | bytes 2820096
  161.8 36.2 %collective-permute-start.38 = (bf16[144,2304]{1,0:T(8,128)(2,1)S(1)}, bf16[144,2304]{1,0:T(8,128)(2,1)S(1)}, u32[]{:S(2)}, u32[]{:S(2)}) collective-permute-start(bf16[144,2304]{1,0:T(8,128)(2,1)S(1)} %collective-permute-done.25.refs_1_), channel_id=1, source_target_pairs={{0,4},{2,6},{4,0},{6,2},{8,12},{10,14},{12,8},{14,10},{16,20},{18,... | collective-permute-start | bytes 1990664 | tf_op jit(solution)/shard_map/ppermute | solution.py:643
  162.9 35.3 %collective-permute-start.37 = (bf16[144,2304]{1,0:T(8,128)(2,1)}, bf16[144,2304]{1,0:T(8,128)(2,1)S(1)}, u32[]{:S(2)}, u32[]{:S(2)}) collective-permute-start(bf16[144,2304]{1,0:T(8,128)(2,1)} %collective-permute-done.26.refs_2_), channel_id=1, source_target_pairs={{0,8},{2,10},{4,12},{6,14},{8,16},{10,18},{12,20},{14,22},{16,24},... | collective-permute-start | bytes 1990664 | tf_op jit(solution)/shard_map/ppermute | solution.py:651
  162.9 36.5 %collective-permute-start.39 = (bf16[144,2304]{1,0:T(8,128)(2,1)}, bf16[144,2304]{1,0:T(8,128)(2,1)}, u32[]{:S(2)}, u32[]{:S(2)}) collective-permute-start(bf16[144,2304]{1,0:T(8,128)(2,1)} %collective-permute-done.26.refs_2_), channel_id=1, source_target_pairs={{0,4},{2,6},{4,0},{6,2},{8,12},{10,14},{12,8},{14,10},{16,20},{18,... | collective-permute-start | bytes 1990664 | tf_op jit(solution)/shard_map/ppermute | solution.py:643
  166.5 41.0 %collective-permute-start.41 = (bf16[144,2304]{1,0:T(8,128)(2,1)S(1)}, bf16[144,2304]{1,0:T(8,128)(2,1)}, u32[]{:S(2)}, u32[]{:S(2)}) collective-permute-start(bf16[144,2304]{1,0:T(8,128)(2,1)S(1)} %maximum_select_fusion.2.refs_0_), channel_id=1, source_target_pairs={{0,2},{2,0},{4,6},{6,4},{8,10},{10,8},{12,14},{14,12},{16,18},{18,... | collective-permute-start | bytes 1990664 | tf_op jit(solution)/shard_map/ppermute | solution.py:647
  166.6 41.0 %collective-permute-start.42 = (bf16[144,2304]{1,0:T(8,128)(2,1)S(1)}, bf16[144,2304]{1,0:T(8,128)(2,1)}, u32[]{:S(2)}, u32[]{:S(2)}) collective-permute-start(bf16[144,2304]{1,0:T(8,128)(2,1)S(1)} %collective-permute-done.25.refs_1_), channel_id=1, source_target_pairs={{0,2},{2,0},{4,6},{6,4},{8,10},{10,8},{12,14},{14,12},{16,18},{18,... | collective-permute-start | bytes 1990664 | tf_op jit(solution)/shard_map/ppermute | solution.py:647
  380.3 78.4 %collective-permute-start.52 = (bf16[4,72,4608]{2,1,0:T(8,128)(2,1)}, bf16[4,72,4608]{2,1,0:T(8,128)(2,1)}, u32[]{:S(2)}, u32[]{:S(2)}) collective-permute-start(bf16[4,72,4608]{2,1,0:T(8,128)(2,1)} %get-tuple-element.252), channel_id=1, source_target_pairs={{0,4},{2,6},{4,0},{6,2},{8,12},{10,14},{12,8},{14,10},{16,20},{18,... | collective-permute-start | bytes 7962632 | tf_op jit(solution)/shard_map/ppermute | solution.py:643
  386.8 71.9 %collective-permute-start.51 = (bf16[4,2,144,1152]{3,2,1,0:T(8,128)(2,1)}, bf16[4,2,144,1152]{3,2,1,0:T(8,128)(2,1)}, u32[]{:S(2)}, u32[]{:S(2)}) collective-permute-start(bf16[4,2,144,1152]{3,2,1,0:T(8,128)(2,1)} %get-tuple-element.254), channel_id=1, source_target_pairs={{0,1},{1,0},{2,3},{3,2},{4,5},{5,4},{6,7},{7,6},{8,9},{9,8},{10,11... | collective-permute-start | bytes 7962632 | tf_op jit(solution)/shard_map/ppermute | solution.py:655
  461.6 33.7 %collective-permute-start.53 = (bf16[2,144,1152]{2,1,0:T(8,128)(2,1)S(1)}, bf16[2,144,1152]{2,1,0:T(8,128)(2,1)S(1)}, u32[]{:S(2)}, u32[]{:S(2)}) collective-permute-start(bf16[2,144,1152]{2,1,0:T(8,128)(2,1)S(1)} %fusion.46), channel_id=1, source_target_pairs={{0,8},{2,10},{4,12},{6,14},{8,16},{10,18},{12,20},{14,22},{16,24},... | collective-permute-start | bytes 1990664 | tf_op jit(solution)/shard_map/ppermute | solution.py:651
  497.5 34.2 %collective-permute-start.56 = (bf16[72,4608]{1,0:T(8,128)(2,1)}, bf16[72,4608]{1,0:T(8,128)(2,1)}, u32[]{:S(2)}, u32[]{:S(2)}) collective-permute-start(bf16[72,4608]{1,0:T(8,128)(2,1)} %fusion.39), channel_id=1, source_target_pairs={{0,8},{2,10},{4,12},{6,14},{8,16},{10,18},{12,20},{14,22},{16,24},... | collective-permute-start | bytes 1990664 | tf_op jit(solution)/shard_map/ppermute | solution.py:651
  499.9 31.9 %collective-permute-start.55 = (bf16[2,144,1152]{2,1,0:T(8,128)(2,1)}, bf16[2,144,1152]{2,1,0:T(8,128)(2,1)S(1)}, u32[]{:S(2)}, u32[]{:S(2)}) collective-permute-start(bf16[2,144,1152]{2,1,0:T(8,128)(2,1)} %fusion.40), channel_id=1, source_target_pairs={{0,8},{2,10},{4,12},{6,14},{8,16},{10,18},{12,20},{14,22},{16,24},... | collective-permute-start | bytes 1990664 | tf_op jit(solution)/shard_map/ppermute | solution.py:651
  499.9 31.9 %collective-permute-start.57 = (bf16[576,1152]{1,0:T(8,128)(2,1)}, bf16[576,1152]{1,0:T(8,128)(2,1)}, u32[]{:S(2)}, u32[]{:S(2)}) collective-permute-start(bf16[576,1152]{1,0:T(8,128)(2,1)} %fusion.17), channel_id=1, source_target_pairs={{0,1},{1,0},{2,3},{3,2},{4,5},{5,4},{6,7},{7,6},{8,9},{9,8},{10,11... | collective-permute-start | bytes 3981320 | tf_op jit(solution)/shard_map/ppermute | solution.py:655
  567.1 56.0 %collective-permute-start.62 = (bf16[2,4,2,72,1152]{4,3,2,1,0:T(8,128)(2,1)}, bf16[2,4,2,72,1152]{4,3,2,1,0:T(8,128)(2,1)}, u32[]{:S(2)}, u32[]{:S(2)}) collective-permute-start(bf16[2,4,2,72,1152]{4,3,2,1,0:T(8,128)(2,1)} %get-tuple-element.202), channel_id=1, source_target_pairs={{0,2},{2,0},{4,6},{6,4},{8,10},{10,8},{12,14},{14,12},{16,18},{18,... | collective-permute-start | bytes 7962632 | tf_op jit(solution)/shard_map/ppermute | solution.py:647
  570.0 53.1 %collective-permute-start.59 = (bf16[4,72,3456]{2,1,0:T(8,128)(2,1)}, bf16[4,72,3456]{2,1,0:T(8,128)(2,1)}, u32[]{:S(2)}, u32[]{:S(2)}) collective-permute-start(bf16[4,72,3456]{2,1,0:T(8,128)(2,1)} %get-tuple-element.256), channel_id=1, source_target_pairs={{0,4},{2,6},{4,0},{6,2},{8,12},{10,14},{12,8},{14,10},{16,20},{18,... | collective-permute-start | bytes 5971976 | tf_op jit(solution)/shard_map/ppermute | solution.py:643
  571.4 101.3 %collective-permute-start.79 = (bf16[72,1152]{1,0:T(8,128)(2,1)}, bf16[72,1152]{1,0:T(8,128)(2,1)S(1)}, u32[]{:S(2)}, u32[]{:S(2)}) collective-permute-start(bf16[72,1152]{1,0:T(8,128)(2,1)} %reduce-scatter.4.cloned.1.call-done), channel_id=1, source_target_pairs={{0,1},{1,0},{2,3},{3,2},{4,5},{5,4},{6,7},{7,6},{8,9},{9,8},{10,11... | collective-permute-start | bytes 497672 | tf_op jit(solution)/shard_map/ppermute | solution.py:655
  575.3 47.9 %collective-permute-start.63 = (bf16[144,1152]{1,0:T(8,128)(2,1)S(1)}, bf16[144,1152]{1,0:T(8,128)(2,1)S(1)}, u32[]{:S(2)}, u32[]{:S(2)}) collective-permute-start(bf16[144,1152]{1,0:T(8,128)(2,1)S(1)} %slice_bitcast_fusion), channel_id=1, source_target_pairs={{0,4},{2,6},{4,0},{6,2},{8,12},{10,14},{12,8},{14,10},{16,20},{18,... | collective-permute-start | bytes 995336 | tf_op jit(solution)/shard_map/ppermute | solution.py:643
  635.3 32.1 %collective-permute-start.69 = (bf16[4,2,72,1152]{3,2,1,0:T(8,128)(2,1)S(1)}, bf16[4,2,72,1152]{3,2,1,0:T(8,128)(2,1)S(1)}, u32[]{:S(2)}, u32[]{:S(2)}) collective-permute-start(bf16[4,2,72,1152]{3,2,1,0:T(8,128)(2,1)S(1)} %get-tuple-element.259), channel_id=1, source_target_pairs={{0,1},{1,0},{2,3},{3,2},{4,5},{5,4},{6,7},{7,6},{8,9},{9,8},{10,11... | collective-permute-start | bytes 3981320 | tf_op jit(solution)/shard_map/ppermute | solution.py:655
  646.7 46.7 %collective-permute-start.80 = (bf16[72,4608]{1,0:T(8,128)(2,1)S(1)}, bf16[72,4608]{1,0:T(8,128)(2,1)S(1)}, u32[]{:S(2)}, u32[]{:S(2)}) collective-permute-start(bf16[72,4608]{1,0:T(8,128)(2,1)S(1)} %fusion.35), channel_id=1, source_target_pairs={{0,1},{1,0},{2,3},{3,2},{4,5},{5,4},{6,7},{7,6},{8,9},{9,8},{10,11... | collective-permute-start | bytes 1990664 | tf_op jit(solution)/shard_map/ppermute | solution.py:655
  (138 other events, 1736.5 us)
Sparse Core Ops, SparseCore 0:
  161.9 98.8 all-gather.1
  396.7 73.8 reduce-scatter.3

commit v3 on v2

--- a/solution.py
+++ b/solution.py
@@ -34,11 +34,15 @@
         out.append((i,min(step,n-i))); i+=step
     return out
 
-def fwd_kernel(s_ref, qkv_ref, kvr_ref, o_ref, l_ref, *, qstep):
-    h=pl.program_id(0)
-    @pl.when(h==0)
+def fwd_kernel(s_ref, qkv_ref, kvr_ref, *refs, qstep, first):
+    o_ref, l_ref = refs[-2:]
+    h = pl.program_id(0) + first
+
+    @pl.when(h == first)
     def _():
-        o_ref[...]=jnp.zeros_like(o_ref); l_ref[...]=jnp.zeros_like(l_ref)
+        for ref, old in zip((o_ref, l_ref), refs[:-2] or (None, None)):
+            ref[...] = jnp.zeros_like(ref) if old is None else old[...]
+
     t=jnp.minimum((72*h)//128, 7)
     lo=72*h-128*t
     base=pl.multiple_of(t*128,128)
@@ -91,22 +95,36 @@
 
 def full(shape,n=1):
     return pl.BlockSpec(shape,lambda h,s:(0,)*len(shape),pipeline_mode=pl.Buffered(1))
-def attn_fwd(sidx,qkv,kvr,qstep=192):
+def attn_fwd(sidx, qkv, kvr, first, count, prev=(), qstep=288):
     return pl.pallas_call(
-        lambda *r: fwd_kernel(*r,qstep=qstep),
-        out_shape=(jax.ShapeDtypeStruct((832,D),jnp.bfloat16),jax.ShapeDtypeStruct((832,128),jnp.float32)),
-        grid_spec=pltpu.PrefetchScalarGridSpec(num_scalar_prefetch=1,grid=(HEADS,),
-            in_specs=[full((832,3*D)),full((REM,2*D))],
-            out_specs=(full((832,D)),full((832,128)))),
-        compiler_params=pltpu.CompilerParams(vmem_limit_bytes=60*2**20),
+        lambda *r: fwd_kernel(*r, qstep=qstep, first=first),
+        out_shape=(
+            jax.ShapeDtypeStruct((832, D), jnp.bfloat16),
+            jax.ShapeDtypeStruct((832, 128), jnp.float32),
+        ),
+        grid_spec=pltpu.PrefetchScalarGridSpec(
+            num_scalar_prefetch=1,
+            grid=(count,),
+            in_specs=[full((832, 3 * D)), full((REM, 2 * D))] + [full(v.shape) for v in prev],
+            out_specs=(full((832, D)), full((832, 128))),
+        ),
+        compiler_params=pltpu.CompilerParams(vmem_limit_bytes=60 * 2**20),
+        cost_estimate=pl.CostEstimate(
+            flops=count * 1200 * 10**6, bytes_accessed=12 * 2**20, transcendentals=0
+        ),
         name="attn_fwd",
-    )(sidx,qkv,kvr)
-
-def bwd_kernel(s_ref,qkv_ref,kvr_ref,do_ref,lt_ref,dt_ref,dqkv_ref,dkvr_ref,*,kstep,expl):
-    h=pl.program_id(0)
-    @pl.when(h==0)
+    )(sidx, qkv, kvr, *prev)
+
+
+def bwd_kernel(s_ref, qkv_ref, kvr_ref, do_ref, lt_ref, dt_ref, *refs, kstep, expl, first):
+    dqkv_ref, dkvr_ref = refs[-2:]
+    h = pl.program_id(0) + first
+
+    @pl.when(h == first)
     def _():
-        dqkv_ref[...]=jnp.zeros_like(dqkv_ref); dkvr_ref[...]=jnp.zeros_like(dkvr_ref)
+        for ref, old in zip((dqkv_ref, dkvr_ref), refs[:-2] or (None, None)):
+            ref[...] = jnp.zeros_like(ref) if old is None else old[...]
+
     t=jnp.minimum((72*h)//128, 7)
     lo=72*h-128*t
     base=pl.multiple_of(t*128,128)
@@ -153,98 +171,159 @@
         def _():
             for tl in TILES[sidx]: tile(*tl)
 
-def attn_bwd(sidx,qkv,kvr,do,lt,dt,kstep=1024,expl=True):
+def attn_bwd(sidx, qkv, kvr, do, lt, dt, first, count, prev=(), kstep=1024, expl=True):
     return pl.pallas_call(
-        lambda *r: bwd_kernel(*r,kstep=kstep,expl=expl),
-        out_shape=(jax.ShapeDtypeStruct((832,3*D),jnp.bfloat16),jax.ShapeDtypeStruct((REM,2*D),jnp.bfloat16)),
-        grid_spec=pltpu.PrefetchScalarGridSpec(num_scalar_prefetch=1,grid=(HEADS,),
-            in_specs=[full((832,3*D)),full((REM,2*D)),full((832,D)),full((16,832)),full((16,832))],
-            out_specs=(full((832,3*D)),full((REM,2*D)))),
-        compiler_params=pltpu.CompilerParams(vmem_limit_bytes=60*2**20),
+        lambda *r: bwd_kernel(*r, kstep=kstep, expl=expl, first=first),
+        out_shape=(
+            jax.ShapeDtypeStruct((832, 3 * D), jnp.bfloat16),
+            jax.ShapeDtypeStruct((REM, 2 * D), jnp.bfloat16),
+        ),
+        grid_spec=pltpu.PrefetchScalarGridSpec(
+            num_scalar_prefetch=1,
+            grid=(count,),
+            in_specs=[
+                full((832, 3 * D)),
+                full((REM, 2 * D)),
+                full((832, D)),
+                full((16, 832)),
+                full((16, 832)),
+            ]
+            + [full(v.shape) for v in prev],
+            out_specs=(full((832, 3 * D)), full((REM, 2 * D))),
+        ),
+        compiler_params=pltpu.CompilerParams(vmem_limit_bytes=60 * 2**20),
+        cost_estimate=pl.CostEstimate(
+            flops=count * 2500 * 10**6, bytes_accessed=20 * 2**20, transcendentals=0
+        ),
         name="attn_bwd",
-    )(sidx,qkv,kvr,do,lt,dt)
-
-
-ERF_A = (
-    -2.72614225801306e-10, 2.77068142495902e-08, -2.10102402082508e-06, -5.69250639462346e-05,
-    -7.34990630326855e-04, -2.95459980854025e-03, -1.60960333262415e-02,
-)
-ERF_B = (
-    -1.45660718464996e-05, -2.13374055278905e-04, -1.68282697438203e-03, -7.37332916720468e-03,
-    -1.42647390514189e-02,
-)
-
-
-def erf(v):
-    v = jnp.clip(v, -4.0, 4.0)
-    square = v * v
-    top, bottom = ERF_A[0], ERF_B[0]
-    for term in ERF_A[1:]:
-        top = top * square + term
-    for term in ERF_B[1:]:
-        bottom = bottom * square + term
-    return v * top / bottom
-
-
-def mlp_up(act, weight, bias, tile=768):
+    )(sidx, qkv, kvr, do, lt, dt, *prev)
+
+
+ERFC = (0.5 * 1.061405429, -0.5 * 1.453152027, 0.5 * 1.421413741, -0.5 * 0.284496736, 0.5 * 0.254829592)
+
+
+def normal_cdf(u):
+    expo = jnp.exp2(u * u * (-0.5 * math.log2(math.e)))
+    below = 1.0 + (0.3275911 * math.sqrt(0.5)) * jnp.abs(u)
+    step = pltpu.reciprocal(below, approx=True)
+    step = step * (2.0 - below * step)
+    tail = ERFC[0]
+    for term in ERFC[1:]:
+        tail = tail * step + term
+    tail = tail * step * expo
+    return jnp.where(u < 0.0, tail, 1.0 - tail), expo
+
+
+def mlp_up(at, act, weight, bias, grad, tile=D, chunks=4):
     rows, width = act.shape[0], weight.shape[1]
-
-    def kernel(a_ref, w_ref, b_ref, g_ref, d_ref):
-        u = dot(a_ref[...], w_ref[...]) + b_ref[...]
-        phi = 0.5 + 0.5 * erf(u * math.sqrt(0.5))
-        g_ref[...] = (u * phi).astype(jnp.bfloat16)
-        density = jnp.exp(u * u * -0.5) * (1.0 / math.sqrt(2.0 * math.pi))
-        d_ref[...] = (phi + u * density).astype(jnp.bfloat16)
+    steps = width // tile
+    size = rows // chunks
+
+    def kernel(at, a_ref, w_ref, b_ref, e_ref, g_ref, d_ref, mine, other, held):
+        t = pl.program_id(0)
+
+        def forward():
+            for i in range(chunks):
+                part = slice(i * size, (i + 1) * size)
+                u = dot(a_ref[part], w_ref[...]) + b_ref[...]
+                phi, expo = normal_cdf(u)
+                g = (u * phi).astype(jnp.bfloat16)
+                g_ref[part] = g
+                d_ref[part] = (phi + u * expo * (1.0 / math.sqrt(2.0 * math.pi))).astype(jnp.bfloat16)
+
+        def keep():
+            held[...] = g_ref[...].T
+
+        def back():
+            for yy in (0, 1):
+                both = dot(held[yy * 576 : yy * 576 + 576], e_ref[...])
+                low, high = both[:288], both[288:]
+                yrel = yy + at[1] - 2 * yy * at[1]
+                for ref, value in (
+                    (mine, jnp.where(at[2] == 0, low, high)),
+                    (other, jnp.where(at[2] == 0, high, low)),
+                ):
+                    value = value.astype(jnp.bfloat16)
+                    ref[at[3], yrel, 0] = value[:144]
+                    ref[1 - at[3], yrel, 0] = value[144:]
+
+        @pl.when(t == 0)
+        def _():
+            forward()
+            keep()
+
+        @pl.when((t > 0) & (t < steps))
+        def _():
+            back()
+            forward()
+            keep()
+
+        @pl.when(t == steps)
+        def _():
+            back()
 
     out = jax.ShapeDtypeStruct((rows, width), jnp.bfloat16)
+    split = jax.ShapeDtypeStruct((2, 2, 4, 144, D), jnp.bfloat16)
+
+    def now(t):
+        return jnp.minimum(t, steps - 1)
+
+    whole = pl.BlockSpec((rows, D), lambda t, at: (0, 0), pipeline_mode=pl.Buffered(1))
+    by_column = pl.BlockSpec((rows, tile), lambda t, at: (0, now(t)))
+    split_spec = pl.BlockSpec((2, 2, 1, 144, D), lambda t, at: (0, 0, jnp.maximum(t - 1, 0), 0, 0))
     return pl.pallas_call(
         kernel,
-        grid=(width // tile,),
-        out_shape=(out, out),
-        in_specs=[
-            pl.BlockSpec((rows, D), lambda t: (0, 0), pipeline_mode=pl.Buffered(1)),
-            pl.BlockSpec((D, tile), lambda t: (0, t)),
-            pl.BlockSpec((1, tile), lambda t: (0, t)),
-        ],
-        out_specs=(pl.BlockSpec((rows, tile), lambda t: (0, t)),) * 2,
+        out_shape=(out, out, split, split),
+        grid_spec=pltpu.PrefetchScalarGridSpec(
+            num_scalar_prefetch=1,
+            grid=(steps + 1,),
+            in_specs=[
+                whole,
+                pl.BlockSpec((D, tile), lambda t, at: (0, now(t))),
+                pl.BlockSpec((1, tile), lambda t, at: (0, now(t))),
+                whole,
+            ],
+            out_specs=(by_column, by_column, split_spec, split_spec),
+            scratch_shapes=[pltpu.VMEM((tile, rows), jnp.bfloat16)],
+        ),
         compiler_params=pltpu.CompilerParams(vmem_limit_bytes=60 * 2**20),
         cost_estimate=pl.CostEstimate(
-            flops=2 * rows * D * width, bytes_accessed=2 * D * width, transcendentals=rows * width
+            flops=4 * rows * D * width,
+            bytes_accessed=5 * D * width,
+            transcendentals=rows * width,
         ),
         name="mlp_up",
-    )(act, weight, bias.reshape(1, width))
-
-
-def ordered_transpose(at, value, held):
+    )(at, act, weight, bias.reshape(1, width), grad)
+
+
+def ordered_transpose(at, value, held, ring=True):
     held[...] = value.astype(jnp.float32).T.reshape(held.shape)
     blocks = []
     for crel in (0, 1):
         for yrel in (0, 1):
             for zrel in range(4):
-                zz = lax.rem(at[0] + zrel, 4)
+                zz = lax.rem(at[0] + zrel, 4) if ring else zrel
                 yy = at[1] + yrel - 2 * at[1] * yrel
                 cc = at[2] + crel - 2 * at[2] * crel
                 blocks.append(held[zz * 4 + yy * 2 + cc])
     return jnp.concatenate(blocks, 0).astype(jnp.bfloat16)
 
 
-def mlp_back(at, act, grad, gelu, slope, w_up, w_down):
-    rows = act.shape[0]
-    half = rows // 2
+def mlp_back(at, act, grad, gelu, slope, w_up, w_down, halves=1, tile=768):
+    rows, width = gelu.shape
+    half = rows // halves
 
     def kernel(at, a_ref, e_ref, g_ref, s_ref, wu_ref, wd_ref, *refs):
-        dn_mine, dn_other, up_mine, up_other, h_ref, c_ref, b_ref, a_t, g_t, du_ref, held = refs
-        t = pl.program_id(0)
-        y, c, x = at[1], at[2], at[3]
-
-        @pl.when(t == 0)
+        mine, other, h_ref, c_ref, b_ref, a_t, du_ref, held = refs
+
+        @pl.when(pl.program_id(0) == 0)
         def _():
-            a_t[...] = ordered_transpose(at, a_ref[...], held)
+            a_t[...] = ordered_transpose(at, a_ref[...], held, ring=False)
             h_ref[...] = jnp.zeros_like(h_ref)
             c_ref[...] = jnp.zeros_like(c_ref)
 
         bias = None
-        for i in (0, 1):
+        for i in range(halves):
             part = slice(i * half, (i + 1) * half)
             du = dot(e_ref[part], wd_ref[...], NT) * s_ref[part].astype(jnp.float32)
             total = jnp.sum(du, axis=0, keepdims=True)
@@ -254,85 +333,70 @@
             h_ref[part] += dot(g_ref[part], wd_ref[...])
             c_ref[part] += dot(du, wu_ref[...], NT)
         b_ref[...] = bias
-        g_t[...] = g_ref[...].T
-        for yy in (0, 1):
-            both = dot(g_t[yy * 576 : yy * 576 + 576], e_ref[...])
-            low, high = both[:288], both[288:]
-            yrel = yy + y - 2 * yy * y
-            for ref, value in (
-                (dn_mine, jnp.where(c == 0, low, high)),
-                (dn_other, jnp.where(c == 0, high, low)),
-            ):
-                value = value.astype(jnp.bfloat16)
-                ref[x, 0, yrel] = value[:144]
-                ref[1 - x, 0, yrel] = value[144:]
-        for i, ref in ((0, up_mine), (1, up_other)):
+        for i, ref in ((0, mine), (1, other)):
             both = dot(a_t[i * 576 : i * 576 + 576], du_ref[...])
             for j in range(8):
                 ref[j // 4, j % 4] = both[j * 72 : j * 72 + 72].astype(jnp.bfloat16)
 
-    def part(t, at):
-        return lax.rem(at[0] + t, 4)
-
     once = pl.Buffered(1)
-    down = jax.ShapeDtypeStruct((2, 4, 2, 144, D), jnp.bfloat16)
-    up = jax.ShapeDtypeStruct((2, 4, 72, 4 * D), jnp.bfloat16)
     whole = jax.ShapeDtypeStruct((rows, D), jnp.float32)
-    down_spec = pl.BlockSpec((2, 1, 2, 144, D), lambda t, at: (0, t, 0, 0, 0))
-    up_spec = pl.BlockSpec((2, 4, 72, D), lambda t, at: (0, 0, 0, part(t, at)))
+    split = jax.ShapeDtypeStruct((2, 4, 72, width), jnp.bfloat16)
+    split_spec = pl.BlockSpec((2, 4, 72, tile), lambda t, at: (0, 0, 0, t))
     whole_spec = pl.BlockSpec((rows, D), lambda t, at: (0, 0), pipeline_mode=once)
-    by_column = pl.BlockSpec((rows, D), lambda t, at: (0, part(t, at)))
+    by_column = pl.BlockSpec((rows, tile), lambda t, at: (0, t))
+    weight_column = pl.BlockSpec((D, tile), lambda t, at: (0, t))
     return pl.pallas_call(
         kernel,
-        out_shape=(down, down, up, up, whole, whole, jax.ShapeDtypeStruct((1, 4 * D), jnp.float32)),
+        out_shape=(
+            split,
+            split,
+            whole,
+            whole,
+            jax.ShapeDtypeStruct((1, width), jnp.float32),
+        ),
         grid_spec=pltpu.PrefetchScalarGridSpec(
             num_scalar_prefetch=1,
-            grid=(4,),
+            grid=(width // tile,),
             in_specs=[
                 whole_spec,
                 whole_spec,
                 by_column,
                 by_column,
-                pl.BlockSpec((D, D), lambda t, at: (0, part(t, at))),
-                pl.BlockSpec((D, D), lambda t, at: (part(t, at), 0)),
+                weight_column,
+                pl.BlockSpec((tile, D), lambda t, at: (t, 0)),
             ],
             out_specs=(
-                down_spec,
-                down_spec,
-                up_spec,
-                up_spec,
+                split_spec,
+                split_spec,
                 whole_spec,
                 whole_spec,
-                pl.BlockSpec((1, D), lambda t, at: (0, part(t, at))),
+                pl.BlockSpec((1, tile), lambda t, at: (0, t)),
             ),
             scratch_shapes=[
                 pltpu.VMEM((D, rows), jnp.bfloat16),
-                pltpu.VMEM((D, rows), jnp.bfloat16),
-                pltpu.VMEM((rows, D), jnp.bfloat16),
+                pltpu.VMEM((rows, tile), jnp.bfloat16),
                 pltpu.VMEM((16, 72, rows), jnp.float32),
             ],
         ),
         compiler_params=pltpu.CompilerParams(vmem_limit_bytes=62 * 2**20),
         cost_estimate=pl.CostEstimate(
-            flops=10 * rows * D * 4 * D, bytes_accessed=64 * 2**20, transcendentals=0
+            flops=8 * rows * D * width, bytes_accessed=50 * 2**20, transcendentals=0
         ),
         name="mlp_back",
     )(at, act, grad, gelu, slope, w_up, w_down)
 
 
-def qkv_back(at, act, act_far, grad, grad_far, weight):
+def qkv_grad(at, act, act_far, grad, grad_far):
     rows, far = act.shape[0], act_far.shape[0]
 
-    def kernel(at, a_ref, f_ref, g_ref, h_ref, w_ref, mine, other, c_ref, a_t, f_t, held, held_far):
+    def kernel(at, a_ref, f_ref, g_ref, h_ref, mine, other, a_t, f_t, held, held_far):
         t = pl.program_id(0)
 
         @pl.when(t == 0)
         def _():
             a_t[...] = ordered_transpose(at, a_ref[...], held)
             f_t[...] = ordered_transpose(at, f_ref[...], held_far)
-            c_ref[...] = jnp.zeros_like(c_ref)
-
-        c_ref[...] += dot(g_ref[...], w_ref[...], NT)
+
         away = jnp.where(t > 0, h_ref[...], jnp.zeros_like(h_ref))
         for i, ref in ((0, mine), (1, other)):
             part = slice(i * 576, (i + 1) * 576)
@@ -345,7 +409,7 @@
     split_spec = pl.BlockSpec((2, 4, 72, D), lambda t, at: (0, 0, 0, t))
     return pl.pallas_call(
         kernel,
-        out_shape=(split, split, jax.ShapeDtypeStruct((rows, D), jnp.float32)),
+        out_shape=(split, split),
         grid_spec=pltpu.PrefetchScalarGridSpec(
             num_scalar_prefetch=1,
             grid=(3,),
@@ -354,13 +418,8 @@
                 pl.BlockSpec((far, D), lambda t, at: (0, 0), pipeline_mode=once),
                 pl.BlockSpec((rows, D), lambda t, at: (0, t)),
                 pl.BlockSpec((far, D), lambda t, at: (0, jnp.maximum(t - 1, 0))),
-                pl.BlockSpec((D, D), lambda t, at: (0, t)),
             ],
-            out_specs=(
-                split_spec,
-                split_spec,
-                pl.BlockSpec((rows, D), lambda t, at: (0, 0), pipeline_mode=once),
-            ),
+            out_specs=(split_spec, split_spec),
             scratch_shapes=[
                 pltpu.VMEM((D, rows), jnp.bfloat16),
                 pltpu.VMEM((D, far), jnp.bfloat16),
@@ -370,10 +429,10 @@
         ),
         compiler_params=pltpu.CompilerParams(vmem_limit_bytes=60 * 2**20),
         cost_estimate=pl.CostEstimate(
-            flops=16 * rows * D * D, bytes_accessed=40 * 2**20, transcendentals=0
-        ),
-        name="qkv_back",
-    )(at, act, act_far, grad, grad_far, weight)
+            flops=10 * rows * D * D, bytes_accessed=40 * 2**20, transcendentals=0
+        ),
+        name="qkv_grad",
+    )(at, act, act_far, grad, grad_far)
 
 
 def skip_back(at, tok, skip, grad):
@@ -392,16 +451,11 @@
         for yy in (0, 1):
             low, high = both[yy * 288 : yy * 288 + 144], both[yy * 288 + 144 : yy * 288 + 288]
             yrel = yy + at[1] - 2 * yy * at[1]
-            for ref, value in (
-                (mine, jnp.where(at[2] == 0, low, high)),
-                (other, jnp.where(at[2] == 0, high, low)),
-            ):
-                value = value.astype(jnp.bfloat16)
-                ref[at[3], 0, yrel] = value[:72]
-                ref[1 - at[3], 0, yrel] = value[72:]
-
-    split = jax.ShapeDtypeStruct((2, 4, 2, 72, D), jnp.bfloat16)
-    split_spec = pl.BlockSpec((2, 1, 2, 72, D), lambda t, at: (0, t, 0, 0, 0))
+            mine[yrel, 0] = jnp.where(at[2] == 0, low, high).astype(jnp.bfloat16)
+            other[yrel, 0] = jnp.where(at[2] == 0, high, low).astype(jnp.bfloat16)
+
+    split = jax.ShapeDtypeStruct((2, 4, 144, D), jnp.bfloat16)
+    split_spec = pl.BlockSpec((2, 1, 144, D), lambda t, at: (0, t, 0, 0))
     whole_spec = pl.BlockSpec((rows, D), lambda t, at: (0, 0), pipeline_mode=pl.Buffered(1))
     return pl.pallas_call(
         kernel,
@@ -687,54 +741,78 @@
     return own + [swap_core(v) for v in own]
 
 
-def assemble(pieces, halves):
+def assemble(pieces, kind):
     rows, cols = pieces[0].shape
-    shape = (8 * rows, 2 * cols) if halves else (16 * rows, cols)
+    split, halves, paired = kind == "split", kind.endswith("halves"), kind == "halves"
+    if split:
+        shapes = [(8 * rows, 3 * D), (8 * rows, D)]
+    elif halves:
+        shapes = [(8 * rows, 2 * cols)]
+    else:
+        shapes = [(16 * rows, cols)]
 
     def kernel(at, *refs):
-        ins, out, held, came, left = refs[:16], refs[16], refs[17], refs[18], refs[19]
-        z, y, c = at[0], at[1], at[2]
-        loads = [
-            pltpu.make_async_copy(ins[j], held.at[j], came.at[j]) for j in range(16)
-        ]
+        ins, outs, (held, came, left) = refs[:16], refs[16:-3], refs[-3:]
+        z, y, c, x = at[0], at[1], at[2], at[3]
+        loads = [pltpu.make_async_copy(ins[j], held.at[j], came.at[j]) for j in range(16)]
         for load in loads:
             load.start()
-        stores = []
+        waits = []
         for j in range(16):
             core = c if j < 8 else 1 - c
             yy = y if j % 8 < 4 else 1 - y
-            zz = lax.rem(z - j % 4 + 4, 4)
-            if halves:
-                first = pl.multiple_of((zz * 2 + yy) * rows, 16)
-                target = out.at[
-                    pl.ds(first, rows), pl.ds(pl.multiple_of(core * cols, 128), cols)
-                ]
+            away = j % 4
+            if paired and j % 8 in (4, 5):
+                away = away + x - 2 * away * x
+            zz = lax.rem(z - away + 4, 4)
+            loads[j].wait()
+            if not split:
+                if halves:
+                    first = pl.multiple_of((zz * 2 + yy) * rows, 16)
+                    at_cols = pl.ds(pl.multiple_of(core * cols, 128), cols)
+                    target = outs[0].at[pl.ds(first, rows), at_cols]
+                else:
+                    first = pl.multiple_of((zz * 4 + yy * 2 + core) * rows, 16)
+                    target = outs[0].at[pl.ds(first, rows), :]
+                store = pltpu.make_async_copy(held.at[j], target, left.at[j])
+                store.start()
+                waits.append((None, store))
+                continue
+            at_rows = pl.ds(pl.multiple_of((zz * 2 + yy) * rows, 16), rows)
+            at_cols = pl.ds(pl.multiple_of(core * (2 * D), 128), D)
+            store = pltpu.make_async_copy(
+                held.at[j, :, pl.ds(0, D)], outs[0].at[at_rows, at_cols], left.at[j]
+            )
+            store.start()
+            waits.append((None, store))
+            for which, target in ((0, outs[0].at[at_rows, pl.ds(D, D)]), (1, outs[1].at[at_rows, :])):
+                store = pltpu.make_async_copy(held.at[j, :, pl.ds(D, D)], target, left.at[16 + j])
+                pl.when(core == which)(store.start)
+                waits.append((core == which, store))
+        for needed, store in waits:
+            if needed is None:
+                store.wait()
             else:
-                first = pl.multiple_of((zz * 4 + yy * 2 + core) * rows, 16)
-                target = out.at[pl.ds(first, rows), :]
-            loads[j].wait()
-            stores.append(pltpu.make_async_copy(held.at[j], target, left.at[j]))
-            stores[-1].start()
-        for store in stores:
-            store.wait()
-
-    return pl.pallas_call(
+                pl.when(needed)(store.wait)
+
+    out = pl.pallas_call(
         kernel,
-        out_shape=jax.ShapeDtypeStruct(shape, pieces[0].dtype),
+        out_shape=[jax.ShapeDtypeStruct(v, pieces[0].dtype) for v in shapes],
         in_specs=[pl.BlockSpec(memory_space=pltpu.SMEM)]
         + [pl.BlockSpec(memory_space=pl.ANY)] * 16,
-        out_specs=pl.BlockSpec(memory_space=pl.ANY),
+        out_specs=[pl.BlockSpec(memory_space=pl.ANY)] * len(shapes),
         scratch_shapes=[
             pltpu.VMEM((16, rows, cols), pieces[0].dtype),
             pltpu.SemaphoreType.DMA((16,)),
-            pltpu.SemaphoreType.DMA((16,)),
+            pltpu.SemaphoreType.DMA((32,)),
         ],
         compiler_params=pltpu.CompilerParams(vmem_limit_bytes=16 * 2**20),
         cost_estimate=pl.CostEstimate(
             flops=0, bytes_accessed=64 * rows * cols, transcendentals=0
         ),
         name="assemble",
-    )(jnp.stack(place()), *pieces)
+    )(jnp.stack([*place(), lax.axis_index("seq").astype(jnp.int32)]), *pieces)
+    return out if split else out[0]
 
 
 def take(v, axis, index):
@@ -758,9 +836,15 @@
     return value + lax.ppermute(value, "batch", [(b, b ^ bit) for b in range(16)])
 
 
-def sc_scatter(grad):
-    part = lax.psum_scatter(grad, "batch", scatter_dimension=0, tiled=True)
-    return f32(part) + f32(swap_seq(part))
+def z_scatter(blocks):
+    groups = [[q + 4 * z for z in range(4)] for q in range(4)]
+    return lax.psum_scatter(
+        blocks, "batch", scatter_dimension=0, tiled=True, axis_index_groups=groups
+    )
+
+
+def sc_sum(grad):
+    return lax.psum_scatter(grad, "batch", scatter_dimension=0, tiled=True)
 
 
 def per_device_pair(
@@ -797,63 +881,82 @@
 
     q0 = core_pair(jnp.concatenate([qkv_w, proj_w], 1))
     s0 = skip_w
-    s1, t0 = next_z(s0), swap_y(s0)
+    s1, t0, s0c = next_z(s0), swap_y(s0), swap_core(s0)
     s1, t0 = tied(s1, t0)
     s2, t1 = next_z(s1), swap_y(s1)
-    s2, t1, s1, q0 = tied(s2, t1, s1, q0)
+    s2, t1, s1, q0, t0, s0c = tied(s2, t1, s1, q0, t0, s0c)
     s3, t2, q1 = next_z(s2), swap_y(s2), next_z(q0)
-    s3, t2, s2, q0 = tied(s3, t2, s2, q0)
+    s1c, t0c = swap_core(s1), swap_core(t0)
+    s3, t2, s2, q0, t1, s1c, t0c = tied(s3, t2, s2, q0, t1, s1c, t0c)
     t3, r0 = swap_y(s3), swap_y(q0)
-    w_skip = assemble(with_core([s0, s1, s2, s3, t0, t1, t2, t3]), False)
-    r0, q1, w_skip, skip_far = tied(r0, q1, w_skip, skip_far)
+    s2c, s3c, t1c, t2c = swap_core(s2), swap_core(s3), swap_core(t1), swap_core(t2)
+    s2c, s3c, t1c, t2c, t3, skip_far = tied(s2c, s3c, t1c, t2c, t3, skip_far)
+    w_skip = assemble(
+        [s0, s1, s2, s3, t0, t1, t2, t3, s0c, s1c, s2c, s3c, t0c, t1c, t2c, swap_core(t3)], "rows"
+    )
+    r0, q1, w_skip, q0 = tied(r0, q1, w_skip, q0)
     q2, r1 = next_z(q1), swap_y(q1)
     skip_flat = b16(f32(take(parts, 0, side)) + f32(skip_far))
     h_zero = fwd_dot(tok_flat, w_skip[:D]) + fwd_dot(skip_flat, w_skip[D:]) + skip_bias
     normed_one, ln1_back = jax.vjp(layer_norm, h_zero, ln1_gain, ln1_bias)
     act_one = b16(normed_one)
     act_send = lax.dynamic_slice(act_one, (shared, 0), (REM, D))
-    q2, r1, act_one, act_send = tied(q2, r1, act_one, act_send)
+    u0 = core_pair(fc1_w)
+    q2, r1, act_one, act_send, u0, q1 = tied(q2, r1, act_one, act_send, u0, q1)
     act_far = swap_seq(act_send)
-    u0 = core_pair(fc1_w)
     q3, r2 = next_z(q2), swap_y(q2)
-    q3, r2, u0, q2 = tied(q3, r2, u0, q2)
+    q0c, q1c, r0c = swap_core(q0), swap_core(q1), swap_core(r0)
+    q3, r2, u0, q2, q0c, q1c, r0c, r1 = tied(q3, r2, u0, q2, q0c, q1c, r0c, r1)
     r3, u1 = swap_y(q3), next_z(u0)
-    r3, u1, q3 = tied(r3, u1, q3)
+    q2c, q3c, r1c, r2c = swap_core(q2), swap_core(q3), swap_core(r1), swap_core(r2)
+    r3, u1, q3, q2c, q3c, r1c, r2c = tied(r3, u1, q3, q2c, q3c, r1c, r2c)
     u2, v0 = next_z(u1), swap_y(u0)
-    w_qp = assemble(with_core([q0, q1, q2, q3, r0, r1, r2, r3]), True)
-    w_qkv, w_proj = w_qp[:, : 3 * D], w_qp[:, 3 * D :]
+    w_qkv, w_proj = assemble(
+        [q0, q1, q2, q3, r0, r1, r2, r3, q0c, q1c, q2c, q3c, r0c, r1c, r2c, swap_core(r3)], "split"
+    )
+    u2, v0, w_qkv, w_proj, u1, u0, act_far = tied(u2, v0, w_qkv, w_proj, u1, u0, act_far)
+    u3, v1 = next_z(u2), swap_y(u1)
+    u0c, u1c, v0c = swap_core(u0), swap_core(u1), swap_core(v0)
     qkv = b16(fwd_dot(act_one, w_qkv))
     kv_far = b16(fwd_dot(act_far, w_qkv[:, D:]))
-    u2, v0, qkv, kv_far, fc2_w = tied(u2, v0, qkv, kv_far, fc2_w)
+    u3, v1, u2, u0c, u1c, v0c, qkv, kv_far, fc2_w = tied(
+        u3, v1, u2, u0c, u1c, v0c, qkv, kv_far, fc2_w
+    )
     w_down = lax.all_gather(fc2_w, "batch", axis=0, tiled=True)
-    u3, v1, v2 = next_z(u2), swap_y(u1), swap_y(u2)
-    att, lse = attn_fwd(index, qkv, kv_far, 288)
-    u3, v1, v2, att = tied(u3, v1, v2, att)
-    v3 = swap_y(u3)
+    v2, v3 = swap_y(u2), swap_y(u3)
+    u2c, u3c, v1c = swap_core(u2), swap_core(u3), swap_core(v1)
+    att, lse = attn_fwd(index, qkv, kv_far, 0, HEADS)
+    v2, v3, u2c, u3c, v1c, att = tied(v2, v3, u2c, u3c, v1c, att)
+    v2c, v3c = swap_core(v2), swap_core(v3)
     h_one = h_zero + fwd_dot(att, w_proj) + proj_bias
     normed_two, ln2_back = jax.vjp(layer_norm, h_one, ln2_gain, ln2_bias)
     act_two = b16(normed_two)
-    w_up = assemble(with_core([u0, u1, u2, u3, v0, v1, v2, v3]), True)
-    gelu_low, slope = mlp_up(act_two, w_up, fc1_bias)
+    w_up = assemble(
+        [u0, u1, u2, u3, v0, v1, v2, v3, u0c, u1c, u2c, u3c, v0c, v1c, v2c, v3c], "ringhalves"
+    )
 
     grad_two = f32(cotangent.reshape(count, D)) * live
     grad_low = b16(grad_two)
-    dn, dn_got, up, up_got, h_add, d_act_two, d_up_bias = mlp_back(
+    gelu_low, slope, dn, dn_got = mlp_up(at, act_two, w_up, fc1_bias, grad_low)
+    dn_got, gelu_low, slope, w_down = tied(dn_got, gelu_low, slope, w_down)
+    dn_got = swap_core(dn_got)
+    up, up_got, h_add, d_act_two, d_up_bias = mlp_back(
         at, act_two, grad_low, gelu_low, slope, w_up, w_down
     )
-    dn_got, up_got, d_act_two = tied(dn_got, up_got, d_act_two)
-    dn_got, up_got = swap_core(dn_got), swap_core(up_got)
+    dn, dn_got, up_got, d_act_two = tied(dn, dn_got, up_got, d_act_two)
+    up_got = swap_core(up_got)
+    dn_far = swap_seq(added(dn[1], dn_got[1]))
+    dn = added(dn[0], dn_got[0])
     output = b16((h_one + h_add + fc2_bias) * live).reshape(1, count, D)
     d_h_one, d_ln2_gain, d_ln2_bias = ln2_back(d_act_two)
     d_h_one = d_h_one + grad_two
     proj_low = b16(d_h_one)
+    d_proj = b16(contract_rows(att, proj_low))
     d_att = b16(back_dot(proj_low, w_proj))
-    d_proj = b16(contract_rows(att, proj_low))
-    dn_got, up_got, d_att, d_proj = tied(dn_got, up_got, d_att, d_proj)
-    out_proj = sc_scatter(d_proj)
-    dn_send, up_send = added(dn[1], dn_got[1]), added(up[1], up_got[1])
-    dn_got_x, up_got_y = swap_seq(dn_send), swap_y(up_send)
-    dn, up = added(dn[0], dn_got[0]), added(up[0], up_got[0])
+    d_att, d_proj, up_got, output, dn = tied(d_att, d_proj, up_got, output, dn)
+    proj_part = sc_sum(d_proj)
+    up_far = swap_y(added(up[1], up_got[1]))
+    up = added(up[0], up_got[0])
     pick = (
         lax.broadcasted_iota(jnp.int32, (D, HEADS), 0) // HD
         == lax.broadcasted_iota(jnp.int32, (D, HEADS), 1)
@@ -861,34 +964,41 @@
     row_dot = lax.dot_general(
         pick, f32(d_att) * f32(att), (((0,), (1,)), ((), ())), precision=lax.Precision.HIGHEST
     )
-    d_qkv, d_far = attn_bwd(index, qkv, kv_far, d_att, lse[:, :HEADS].T, row_dot)
-    dn, up, dn_got, up_got, d_qkv, d_far = tied(dn, up, dn_got_x, up_got_y, d_qkv, d_far)
-    dn_next, up_next = added(dn[3], dn_got[3]), added(up[3], up_got[3])
-    dn_next, up_next = next_z(dn_next), next_z(up_next)
+    lse = lse[:, :HEADS].T
+    d_qkv, d_far = attn_bwd(index, qkv, kv_far, d_att, lse, row_dot, 0, HEADS)
     far = b16(back_dot(d_far, w_qkv[:, D:]))
-    dn_next, up_next, far, d_far, d_qkv = tied(dn_next, up_next, far, d_far, d_qkv)
-    far = swap_seq(far)
-    dn_next, up_next = (
-        next_z(b16(f32(dn[2]) + f32(dn_got[2]) + f32(dn_next))),
-        next_z(b16(f32(up[2]) + f32(up_got[2]) + f32(up_next))),
-    )
-    q, q_got, d_act_one = qkv_back(at, act_one, act_far, d_qkv, d_far, w_qkv)
-    dn_next, up_next, far, d_act_one, q_got = tied(dn_next, up_next, far, d_act_one, q_got)
+    far, d_qkv, d_far, dn, dn_far, up, up_far, proj_part = tied(
+        far, d_qkv, d_far, dn, dn_far, up, up_far, proj_part
+    )
+    up = added(up, up_far)
+    dn_send = [added(dn[1, 0:2], dn_far[1, 0:2]), added(dn[1, 2:4], dn_far[1, 2:4])]
+    dn = added(dn[0], dn_far[0])
+    far, d_qkv, d_far, dn, dn_send, up = tied(far, d_qkv, d_far, dn, dn_send, up)
+    up_part = z_scatter(up.reshape(4 * 72, 4 * D))
+    low_far = swap_seq(far[: REM // 2])
+    dn_low = swap_y(dn_send[0])
+    q, q_got = qkv_grad(at, act_one, act_far, d_qkv, d_far)
+    d_qkv, q, q_got, low_far, dn_low, far = tied(d_qkv, q, q_got, low_far, dn_low, far)
     q_got = swap_core(q_got)
-    dn_next, up_next = (
-        next_z(b16(f32(dn[1]) + f32(dn_got[1]) + f32(dn_next))),
-        next_z(b16(f32(up[1]) + f32(up_got[1]) + f32(up_next))),
-    )
+    high_far = swap_seq(far[REM // 2 :])
+    dn_high = swap_y(dn_send[1])
+    d_act_one = back_dot(d_qkv, w_qkv)
+    q_got, d_act_one, high_far, dn_high = tied(q_got, d_act_one, high_far, dn_high)
+    far = f32(jnp.concatenate([low_far, high_far], 0))
     here = lax.dynamic_slice(d_act_one, (shared, 0), (REM, D))
-    d_act_one = lax.dynamic_update_slice(d_act_one, here + f32(far), (shared, 0))
+    d_act_one = lax.dynamic_update_slice(d_act_one, here + far, (shared, 0))
+    q_send = [added(q[1, i], q_got[1, i]) for i in range(4)]
+    q_y = {i: swap_y(q_send[i]) for i in (3, 2)}
+    q = added(q[0], q_got[0])
+    dn_part = z_scatter(added(dn, jnp.concatenate([dn_low, dn_high], 0)).reshape(4 * 144, D))
     d_h_zero, d_ln1_gain, d_ln1_bias = ln1_back(d_act_one)
     d_h_zero = d_h_zero + d_h_one
     zero_low = b16(d_h_zero)
-    q_got, zero_low = tied(q_got, zero_low)
-    q_send = added(q[1], q_got[1])
-    q_got_y = swap_y(q_send)
-    q = added(q[0], q_got[0])
     k, k_got = skip_back(at, tok_flat, skip_flat, zero_low)
+
+    def onward(mine, got, so_far):
+        return next_z(b16(f32(mine) + f32(got) + f32(so_far)))
+
     sums = jnp.concatenate(
         [
             jnp.sum(d_h_zero, axis=0),
@@ -901,41 +1011,47 @@
             jnp.sum(grad_two, axis=0),
         ]
     ).reshape(-1, 128)
-    dn_next, up_next, k, k_got, zero_low = tied(dn_next, up_next, k, k_got, zero_low)
+    q_y[3], q_y[2], q, q_send, k, k_got, zero_low, sums = tied(
+        q_y[3], q_y[2], q, q_send, k, k_got, zero_low, sums
+    )
+    k_got = swap_core(k_got)
+    q_next = next_z(added(q[3], q_y[3]))
+    q_y[1], q_y[0] = swap_y(q_send[1]), swap_y(q_send[0])
     d_tokens = back_dot(zero_low, w_skip[:D]).reshape(1, count, D)
-    dn_sum = b16(f32(dn[0]) + f32(dn_got[0]) + f32(dn_next))
-    up_sum = b16(f32(up[0]) + f32(up_got[0]) + f32(up_next))
-    dn_next, up_next, k_got = swap_y(dn_sum[1]), swap_seq(up_sum), swap_core(k_got)
     sums = vector_step(sums, 1)
-    out_up = f32(up_sum) + f32(up_next)
-    q, q_got, k, k_got, dn_next, dn_sum, sums, zero_low, d_tokens = tied(
-        q, q_got_y, k, k_got, dn_next, dn_sum, sums, zero_low, d_tokens
-    )
+    q_next, q_y, k, k_got, sums, zero_low, d_tokens = tied(
+        q_next, q_y, k, k_got, sums, zero_low, d_tokens
+    )
+    q_next = onward(q[2], q_y[2], q_next)
+    k_send = [added(k[1, i], k_got[1, i]) for i in range(4)]
+    k_y = {i: swap_y(k_send[i]) for i in (3, 2)}
+    k = added(k[0], k_got[0])
+    sums = vector_step(sums, 0, "seq")
     d_skip = back_dot(zero_low, w_skip[D:]).reshape(1, count, D)
-    q_next = next_z(added(q[3], q_got[3]))
-    k_got_x = swap_seq(added(k[1], k_got[1]))
-    k = added(k[0], k_got[0])
-    dn_sum = added(dn_sum[0], dn_next)
-    dn_next = swap_seq(dn_sum)
+    q_next, k_y, k, k_send, sums, d_skip = tied(q_next, k_y, k, k_send, sums, d_skip)
+    q_next = onward(q[1], q_y[1], q_next)
+    k_next = next_z(added(k[3], k_y[3]))
+    k_y[1], k_y[0] = swap_y(k_send[1]), swap_y(k_send[0])
+    q_next, k_next, k_y, up_part, proj_part = tied(q_next, k_next, k_y, up_part, proj_part)
+    up_far = swap_seq(up_part)
+    proj_far = swap_seq(proj_part)
+    q_sum = b16(f32(q[0]) + f32(q_y[0]) + f32(q_next))
+    q_got = swap_seq(q_sum)
+    k_next = onward(k[2], k_y[2], k_next)
     sums = vector_step(sums, 2)
-    q, q_next, q_got, dn_next, sums, d_skip = tied(q, q_next, q_got, dn_next, sums, d_skip)
-    out_down = by_side(side, dn_sum, dn_next)
-    q_next = next_z(b16(f32(q[2]) + f32(q_got[2]) + f32(q_next)))
-    sums = vector_step(sums, 4)
-    q, q_next, q_got, k, k_got, sums = tied(q, q_next, q_got, k, k_got_x, sums)
-    q_next = next_z(b16(f32(q[1]) + f32(q_got[1]) + f32(q_next)))
-    k_next = next_z(added(k[3], k_got[3]))
-    sums = vector_step(sums, 8)
-    q, q_next, q_got, k_next, k, k_got, sums = tied(q, q_next, q_got, k_next, k, k_got, sums)
-    q_sum = b16(f32(q[0]) + f32(q_got[0]) + f32(q_next))
-    q_next = swap_seq(q_sum)
-    out_qkv = f32(q_sum) + f32(q_next)
-    sums = vector_step(sums, 0, "seq").reshape(-1)
-    k_next = next_z(b16(f32(k[2]) + f32(k_got[2]) + f32(k_next)))
-    k_next = next_z(b16(f32(k[1]) + f32(k_got[1]) + f32(k_next)))
-    k_sum = b16(f32(k[0]) + f32(k_got[0]) + f32(k_next))
-    k_sum = added(k_sum[0], swap_y(k_sum[1]))
-    out_skip = by_side(side, k_sum, swap_seq(k_sum))
+    q_got, k_next, k_y, sums, dn_part, proj_far, up_far = tied(
+        q_got, k_next, k_y, sums, dn_part, proj_far, up_far
+    )
+    dn_got = swap_seq(dn_part)
+    out_up = f32(up_part) + f32(up_far)
+    out_proj = f32(proj_part) + f32(proj_far)
+    out_qkv = f32(q_sum) + f32(q_got)
+    k_next = onward(k[1], k_y[1], k_next)
+    k_next, k_y, sums, dn_got = tied(k_next, k_y, sums, dn_got)
+    out_down = by_side(side, dn_part, dn_got)
+    k_sum = b16(f32(k[0]) + f32(k_y[0]) + f32(k_next))
+    out_skip = f32(k_sum) + f32(swap_seq(k_sum))
+    sums = vector_step(vector_step(sums, 4), 8).reshape(-1)
     starts = [0, D, 2 * D, 3 * D, 4 * D, 5 * D, 6 * D, 10 * D, 11 * D]
     sums = [sums[a:b] for a, b in zip(starts, starts[1:])]
     grads = (out_skip, out_qkv, out_proj, out_up, out_down)

time: 742 us -> 654 us (0.88)
  waiting for transfers between devices: 236 us -> 182 us
  Pallas kernels: 256 us -> 229 us
  local copies, waits for them, and re-layouts: 36 us -> 23.2 us
  matrix products: 63.2 us -> 73.1 us
    ppermute x21 -> x15, waiting for transfers between devices: 106 us -> 52.9 us  [next_z(): return lax.ppermute(v, 'batch', ZUP)]
    pallas_call x8, Pallas kernels: 246 us -> 219 us  [the longest x1 56.8 us: attn_bwd(): pl.pallas_call(lambda *r: bwd_kernel(*r, kstep=kstep, expl=expl, first=fi...]
    dot_general x4 -> x5, matrix products: 25.9 us -> 37.9 us  [back_dot(): lax.dot_general(grad_rows, weight, (((1,), (1,)), ((), ())), preferred_el...]
    ppermute x4, waiting for transfers between devices: 19.7 us -> 9.09 us  [vector_step(): lax.ppermute(value, 'batch', [(b, b ^ bit) for b in range(16)])]
    ppermute x21 -> x15, starting transfers between devices: 14.1 us -> 4.39 us  [next_z(): return lax.ppermute(v, 'batch', ZUP)]
    convert_element_type x23 -> x21, other arithmetic: 40 us -> 49.2 us  [b16(): return v.astype(jnp.bfloat16)]
    ppermute x16 -> x23, waiting for transfers between devices: 81.4 us -> 89.9 us  [swap_y(): return lax.ppermute(v, 'batch', YSW)]
    ppermute x16 -> x23, starting transfers between devices: 18.1 us -> 24.9 us  [swap_y(): return lax.ppermute(v, 'batch', YSW)]
  transfers between devices with their start and end apart: 84 -> 87, of which waited for: 26 -> 40; matrix products, arithmetic and copies ran while one was open for 20% -> 22% of each run, Pallas kernels for 25% -> 35%
where the time goes in v3:
time: 654 us; the launch traced here: 645 us
  Pallas kernels  229 us (35%)
  waiting for transfers between devices  182 us (28%)
  other arithmetic  73.7 us (11%)
  matrix products  73.1 us (11%)
  starting transfers between devices  48.6 us (7%)
  local copies, waits for them, and re-layouts  23.2 us (4%)
  between operations  15.2 us (2%)
    ppermute x23, waiting for transfers between devices, swap_y(): return lax.ppermute(v, 'batch', YSW)  89.9 us
    pallas_call x1, Pallas kernels, attn_bwd(): pl.pallas_call(lambda *r: bwd_kernel(*r, kstep=kstep, expl=expl, first=fi...  56.8 us
    ppermute x15, waiting for transfers between devices, next_z(): return lax.ppermute(v, 'batch', ZUP)  52.9 us
    pallas_call x1, Pallas kernels, mlp_back(): pl.pallas_call(kernel, out_shape=(split, split, whole, whole, jax.ShapeDt...  51.7 us
    convert_element_type x21, other arithmetic, b16(): return v.astype(jnp.bfloat16)  49.2 us
    pallas_call x1, Pallas kernels, mlp_up(): pl.pallas_call(kernel, out_shape=(out, out, split, split), grid_spec=pltp...  42.5 us
    dot_general x5, matrix products, back_dot(): lax.dot_general(grad_rows, weight, (((1,), (1,)), ((), ())), preferred_el...  37.9 us
    pallas_call x1, Pallas kernels, attn_fwd(): pl.pallas_call(lambda *r: fwd_kernel(*r, qstep=qstep, first=first), out_s...  31.2 us
  transfers between devices with their start and end apart: 87, of which 40 were waited for; matrix products, arithmetic and copies ran while one was open for 22% of the time, Pallas kernels for 35%

profile of v3, /device:TPU:0, one launch (start us, length us, event | category | flops | bytes accessed | tf_op | source)
XLA Modules:
  0.0 644.9 jit_solution(9097960360244359832)
XLA Ops:
  22.3 7.8 %collective-permute-done.3.refs_5_ = bf16[144,1152]{1,0:T(8,128)(2,1)S(1)} collective-permute-done((bf16[144,1152]{1,0:T(8,128)(2,1)S(1)}, bf16[144,1152]{1,0:T(8,128)(2,1)S(1)}, u32[]{:S(2)}, u32[]{:S(2)}) %collective-permute-start.3) | collective-permute-done | bytes 331808 | tf_op jit(solution)/shard_map/ppermute | solution.py:697
  49.0 7.3 %collective-permute-done.16.refs_7_ = bf16[144,1152]{1,0:T(8,128)(2,1)S(1)} collective-permute-done((bf16[144,1152]{1,0:T(8,128)(2,1)}, bf16[144,1152]{1,0:T(8,128)(2,1)S(1)}, u32[]{:S(2)}, u32[]{:S(2)}) %collective-permute-start.16) | collective-permute-done | bytes 331808 | tf_op jit(solution)/shard_map/ppermute | solution.py:697
  79.0 6.8 %collective-permute-done.20.refs_5_ = bf16[144,2304]{1,0:T(8,128)(2,1)S(1)} collective-permute-done((bf16[144,2304]{1,0:T(8,128)(2,1)S(1)}, bf16[144,2304]{1,0:T(8,128)(2,1)S(1)}, u32[]{:S(2)}, u32[]{:S(2)}) %collective-permute-start.20) | collective-permute-done | bytes 663584 | tf_op jit(solution)/shard_map/ppermute | solution.py:697
  90.3 15.2 %collective-permute-done.23.refs_6_ = bf16[144,2304]{1,0:T(8,128)(2,1)S(1)} collective-permute-done((bf16[144,2304]{1,0:T(8,128)(2,1)S(1)}, bf16[144,2304]{1,0:T(8,128)(2,1)S(1)}, u32[]{:S(2)}, u32[]{:S(2)}) %collective-permute-start.23) | collective-permute-done | bytes 663584 | tf_op jit(solution)/shard_map/ppermute | solution.py:697
  113.2 12.9 %collective-permute-done.27.refs_7_ = bf16[144,2304]{1,0:T(8,128)(2,1)S(1)} collective-permute-done((bf16[144,2304]{1,0:T(8,128)(2,1)S(1)}, bf16[144,2304]{1,0:T(8,128)(2,1)S(1)}, u32[]{:S(2)}, u32[]{:S(2)}) %collective-permute-start.27) | collective-permute-done | bytes 663584 | tf_op jit(solution)/shard_map/ppermute | solution.py:697
  137.3 9.1 %collective-permute-done.34.refs_4_ = bf16[144,2304]{1,0:T(8,128)(2,1)S(1)} collective-permute-done((bf16[144,2304]{1,0:T(8,128)(2,1)S(1)}, bf16[144,2304]{1,0:T(8,128)(2,1)S(1)}, u32[]{:S(2)}, u32[]{:S(2)}) %collective-permute-start.34) | collective-permute-done | bytes 663584 | tf_op jit(solution)/shard_map/ppermute | solution.py:697
  150.5 9.7 %convolution_convert_fusion.1.r_1_ = bf16[832,3456]{1,0:T(8,128)(2,1)} fusion(bf16[832,1152]{1,0:T(8,128)(2,1)S(1)} %add_convert_fusion.7.a_ref, bf16[1152,3456]{1,0:T(8,128)(2,1)S(1)} %get-tuple-element.238), kind=kOutput, calls=%fused_computation.1 | convolution fusion | flops 6627778560 | bytes 15630336 | tf_op jit(solution)/shard_map/dot_general | solution.py:494
  175.0 31.2 %attn_fwd.1 = (bf16[832,1152]{1,0:T(8,128)(2,1)}, f32[832,128]{1,0:T(8,128)}) custom-call(s32[1]{0:T(128)} %bitcast.3.r_0_, bf16[832,3456]{1,0:T(8,128)(2,1)} %convolution_convert_fusion.1.r_1_, bf16[576,2304]{1,0:T(8,128)(2,1)} %fusion.4.r_2_), custom_call_target="tpu_custom_call" | custom-call | flops 19200000000 | bytes 12582912 | tf_op jit(solution)/shard_map/attn_fwd/pallas_call | solution.py:99
  212.0 6.5 %fusion.76 = (f32[832]{0:T(1024)S(1)}, f32[832,1152]{1,0:T(8,128)S(1)}) fusion(f32[1152]{0:T(1024)S(1)} %copy-done.79, f32[832,1152]{1,0:T(8,128)} %copy-done.26, bf16[832,1152]{1,0:T(8,128)(2,1)} %get-tuple-element.246, bf16[1152,1152]{1,0:T(8,128)(2,1)} %copy-done.22), kind=kOutput, calls=%fused_computation.167 | convolution fusion | flops 2211175680 | bytes 12246784 | tf_op jit(solution)/shard_map/dot_general | solution.py:494
  232.7 42.5 %mlp_up.1 = (bf16[832,4608]{1,0:T(8,128)(2,1)}, bf16[832,4608]{1,0:T(8,128)(2,1)}, bf16[2,2,4,144,1152]{4,3,2,1,0:T(8,128)(2,1)}, bf16[2,2,4,144,1152]{4,3,2,1,0:T(8,128)(2,1)}) custom-call(s32[4]{0:T(128)} %copy-done.19, bf16[832,1152]{1,0:T(8,128)(2,1)} %get-tuple-element.402.a_ref, bf16[1152,4608]{1,0:T(8,128)(2,1)} %copy-done, ...), custom_call_target="tpu_custom_call" | custom-call | flops 17666408448 | bytes 26542080 | tf_op jit(solution)/shard_map/mlp_up/pallas_call | solution.py:274
  275.4 51.7 %mlp_back.1 = (bf16[2,4,72,4608]{3,2,1,0:T(8,128)(2,1)}, bf16[2,4,72,4608]{3,2,1,0:T(8,128)(2,1)}, f32[832,1152]{1,0:T(8,128)}, f32[832,1152]{1,0:T(8,128)}, f32[1,4608]{1,0:T(1,128)}) custom-call(s32[4]{0:T(128)} %copy-done.19, bf16[832,1152]{1,0:T(8,128)(2,1)} %get-tuple-element.402.a_ref, bf16[832,1152]{1,0:T(8,128)(2,1)} %get-tuple-element.401.e_ref, ...), custom_call_target="tpu_custom_call" | custom-call | flops 35332816896 | bytes 52428800 | tf_op jit(solution)/shard_map/mlp_back/pallas_call | solution.py:348
  328.3 6.7 %fusion.21 = (bf16[2,4,144,1152]{3,2,1,0:T(8,128)(2,1)}, bf16[2,4,144,1152]{3,2,1,0:T(8,128)(2,1)}) fusion(bf16[2,2,4,144,1152]{4,3,2,1,0:T(8,128)(2,1)} %collective-permute-done.49, bf16[2,2,4,144,1152]{4,3,2,1,0:T(8,128)(2,1)} %get-tuple-element.270), kind=kLoop, calls=%fused_computation.45 | loop fusion | flops 10616832 | bytes 15925248 | tf_op jit(solution)/shard_map/convert_element_type | solution.py:722
  348.3 6.3 convolution_convert_fusion.2.r_3_
  354.7 6.7 %fusion.23 = (bf16[4,72,4608]{2,1,0:T(8,128)(2,1)}, bf16[4,72,4608]{2,1,0:T(8,128)(2,1)}) fusion(bf16[2,4,72,4608]{3,2,1,0:T(8,128)(2,1)} %collective-permute-done.50, bf16[2,4,72,4608]{3,2,1,0:T(8,128)(2,1)} %get-tuple-element.278), kind=kLoop, calls=%fused_computation.47 | loop fusion | flops 10616832 | bytes 15925248 | tf_op jit(solution)/shard_map/convert_element_type | solution.py:722
  365.4 56.8 %attn_bwd.1 = (bf16[832,3456]{1,0:T(8,128)(2,1)}, bf16[576,2304]{1,0:T(8,128)(2,1)}) custom-call(s32[1]{0:T(128)} %bitcast.3.r_0_, bf16[832,3456]{1,0:T(8,128)(2,1)} %convolution_convert_fusion.1.r_1_, bf16[576,2304]{1,0:T(8,128)(2,1)} %fusion.4.r_2_, bf16[832,1152]{1,0:T(8,128)(2,1)} %convolution_convert_fusion.2.r_3_, f32[16,832]{1,0:T(8,128)} %slice_bitcast_fusion.r_4_, ...), custom_call_target="tpu_custom_call" | custom-call | flops 40000000000 | bytes 20971520 | tf_op jit(solution)/shard_map/attn_bwd/pallas_call | solution.py:175
  422.2 8.2 %fusion.17 = bf16[576,1152]{1,0:T(8,128)(2,1)} fusion(bf16[576,2304]{1,0:T(8,128)(2,1)} %get-tuple-element.289.h_ref, bf16[1152,3456]{1,0:T(8,128)(2,1)} %copy-done.21), kind=kOutput, calls=%fused_computation.43 | convolution fusion | flops 3058311168 | bytes 9289728 | tf_op jit(solution)/shard_map/dot_general | solution.py:504
  441.9 22.4 %qkv_grad.1 = (bf16[2,4,72,3456]{3,2,1,0:T(8,128)(2,1)}, bf16[2,4,72,3456]{3,2,1,0:T(8,128)(2,1)}) custom-call(s32[4]{0:T(128)} %copy-done.19, bf16[832,1152]{1,0:T(8,128)(2,1)} %copy-done.38, bf16[576,1152]{1,0:T(8,128)(2,1)} %copy-done.77, bf16[832,3456]{1,0:T(8,128)(2,1)} %get-tuple-element.296.g_ref, bf16[576,2304]{1,0:T(8,128)(2,1)} %get-tuple-element.289.h_ref), custom_call_target="tpu_custom_call" | custom-call | flops 11041505280 | bytes 41943040 | tf_op jit(solution)/shard_map/qkv_grad/pallas_call | solution.py:410
  467.0 12.1 %fusion.77 = f32[832,1152]{1,0:T(8,128)S(1)} fusion(bf16[832,3456]{1,0:T(8,128)(2,1)} %get-tuple-element.296.g_ref, bf16[1152,3456]{1,0:T(8,128)(2,1)} %copy-done.21), kind=kOutput, calls=%fused_computation.168 | convolution fusion | flops 6624903168 | bytes 17547264 | tf_op jit(solution)/shard_map/dot_general | solution.py:504
  497.5 9.6 %skip_back.1 = (bf16[2,4,144,1152]{3,2,1,0:T(8,128)(2,1)S(1)}, bf16[2,4,144,1152]{3,2,1,0:T(8,128)(2,1)}) custom-call(s32[4]{0:T(128)S(1)} %copy-done.20, bf16[832,1152]{1,0:T(8,128)(2,1)S(1)} %bitcast.121, bf16[832,1152]{1,0:T(8,128)(2,1)S(1)} %copy-done.5, bf16[832,1152]{1,0:T(8,128)(2,1)S(1)} %get-tuple-element.321.g_ref), custom_call_target="tpu_custom_call" | custom-call | flops 4416602112 | bytes 12582912 | tf_op jit(solution)/shard_map/skip_back/pallas_call | solution.py:460
  515.3 6.5 %convolution_bitcast_fusion.2 = f32[1,832,1152]{2,1,0:T(8,128)} fusion(bf16[832,1152]{1,0:T(8,128)(2,1)S(1)} %get-tuple-element.321.g_ref, bf16[2304,1152]{1,0:T(8,128)(2,1)} %copy-done.1), kind=kOutput, calls=%fused_computation.21 | convolution fusion | flops 2208301056 | bytes 8404992 | tf_op jit(solution)/shard_map/dot_general | solution.py:504
  521.9 7.7 %collective-permute-done.60 = bf16[72,3456]{1,0:T(8,128)(2,1)S(1)} collective-permute-done((bf16[72,3456]{1,0:T(8,128)(2,1)S(1)}, bf16[72,3456]{1,0:T(8,128)(2,1)S(1)}, u32[]{:S(2)}, u32[]{:S(2)}) %collective-permute-start.60) | collective-permute-done | bytes 497696 | tf_op jit(solution)/shard_map/ppermute | solution.py:705
  529.6 7.8 %collective-permute-done.62 = bf16[72,3456]{1,0:T(8,128)(2,1)S(1)} collective-permute-done((bf16[72,3456]{1,0:T(8,128)(2,1)S(1)}, bf16[72,3456]{1,0:T(8,128)(2,1)S(1)}, u32[]{:S(2)}, u32[]{:S(2)}) %collective-permute-start.62) | collective-permute-done | bytes 497696 | tf_op jit(solution)/shard_map/ppermute | solution.py:697
  566.1 16.4 %collective-permute-done.70 = bf16[144,1152]{1,0:T(8,128)(2,1)} collective-permute-done((bf16[144,1152]{1,0:T(8,128)(2,1)}, bf16[144,1152]{1,0:T(8,128)(2,1)}, u32[]{:S(2)}, u32[]{:S(2)}) %collective-permute-start.70) | collective-permute-done | bytes 331808 | tf_op jit(solution)/shard_map/ppermute | solution.py:705
  593.9 19.6 %collective-permute-done.76 = bf16[72,1152]{1,0:T(8,128)(2,1)} collective-permute-done((bf16[72,1152]{1,0:T(8,128)(2,1)}, bf16[72,1152]{1,0:T(8,128)(2,1)}, u32[]{:S(2)}, u32[]{:S(2)}) %collective-permute-start.76) | collective-permute-done | bytes 165920 | tf_op jit(solution)/shard_map/ppermute | solution.py:709
  (420 shorter events, 242.0 us)
Async XLA Ops:
  7.2 268.1 %all-gather.2.cloned.1.call-start = ((), (), s32[]{:S(2)}) async-start(), calls=%async_computation.3 | async-start | bytes 11280384 | tf_op jit(solution)/shard_map/all_gather | solution.py:925
  16.1 44.5 %collective-permute-start.17 = (bf16[832,1152]{1,0:T(8,128)(2,1)}, bf16[832,1152]{1,0:T(8,128)(2,1)}, u32[]{:S(2)}, u32[]{:S(2)}) collective-permute-start(bf16[832,1152]{1,0:T(8,128)(2,1)} %dynamic-slice_bitcast_fusion), channel_id=1, source_target_pairs={{0,1},{1,0},{2,3},{3,2},{4,5},{5,4},{6,7},{7,6},{8,9},{9,8},{10,11... | collective-permute-start | bytes 5750792 | tf_op jit(solution)/shard_map/ppermute | solution.py:709
  44.0 23.6 %collective-permute-start.11 = (bf16[144,2304]{1,0:T(8,128)(2,1)S(1)}, bf16[144,2304]{1,0:T(8,128)(2,1)S(1)}, u32[]{:S(2)}, u32[]{:S(2)}) collective-permute-start(bf16[144,2304]{1,0:T(8,128)(2,1)S(1)} %maximum_select_fusion.1.refs_0_), channel_id=1, source_target_pairs={{0,8},{2,10},{4,12},{6,14},{8,16},{10,18},{12,20},{14,22},{16,24},... | collective-permute-start | bytes 1990664 | tf_op jit(solution)/shard_map/ppermute | solution.py:705
  46.3 23.5 %collective-permute-start.10 = (bf16[144,2304]{1,0:T(8,128)(2,1)S(1)}, bf16[144,2304]{1,0:T(8,128)(2,1)S(1)}, u32[]{:S(2)}, u32[]{:S(2)}) collective-permute-start(bf16[144,2304]{1,0:T(8,128)(2,1)S(1)} %maximum_select_fusion.1.refs_0_), channel_id=1, source_target_pairs={{0,4},{2,6},{4,0},{6,2},{8,12},{10,14},{12,8},{14,10},{16,20},{18,... | collective-permute-start | bytes 1990664 | tf_op jit(solution)/shard_map/ppermute | solution.py:697
  111.3 35.1 %collective-permute-start.36 = (bf16[576,1152]{1,0:T(8,128)(2,1)S(1)}, bf16[576,1152]{1,0:T(8,128)(2,1)S(1)}, u32[]{:S(2)}, u32[]{:S(2)}) collective-permute-start(bf16[576,1152]{1,0:T(8,128)(2,1)S(1)} %constant_dynamic-slice_fusion), channel_id=1, source_target_pairs={{0,1},{1,0},{2,3},{3,2},{4,5},{5,4},{6,7},{7,6},{8,9},{9,8},{10,11... | collective-permute-start | bytes 3981320 | tf_op jit(solution)/shard_map/ppermute | solution.py:709
  170.6 259.7 %reduce-scatter.10.cloned.1.call-start = ((), (), s32[]{:S(2)}) async-start(), calls=%async_computation.6 | async-start | bytes 2820096
  172.6 33.6 %collective-permute-start.44 = (bf16[144,2304]{1,0:T(8,128)(2,1)S(1)}, bf16[144,2304]{1,0:T(8,128)(2,1)}, u32[]{:S(2)}, u32[]{:S(2)}) collective-permute-start(bf16[144,2304]{1,0:T(8,128)(2,1)S(1)} %collective-permute-done.33.refs_2_), channel_id=1, source_target_pairs={{0,2},{2,0},{4,6},{6,4},{8,10},{10,8},{12,14},{14,12},{16,18},{18,... | collective-permute-start | bytes 1990664 | tf_op jit(solution)/shard_map/ppermute | solution.py:701
  172.7 33.6 %collective-permute-start.42 = (bf16[144,2304]{1,0:T(8,128)(2,1)S(1)}, bf16[144,2304]{1,0:T(8,128)(2,1)}, u32[]{:S(2)}, u32[]{:S(2)}) collective-permute-start(bf16[144,2304]{1,0:T(8,128)(2,1)S(1)} %collective-permute-done.33.refs_2_), channel_id=1, source_target_pairs={{0,4},{2,6},{4,0},{6,2},{8,12},{10,14},{12,8},{14,10},{16,20},{18,... | collective-permute-start | bytes 1990664 | tf_op jit(solution)/shard_map/ppermute | solution.py:697
  173.6 32.7 %collective-permute-start.45 = (bf16[144,2304]{1,0:T(8,128)(2,1)}, bf16[144,2304]{1,0:T(8,128)(2,1)}, u32[]{:S(2)}, u32[]{:S(2)}) collective-permute-start(bf16[144,2304]{1,0:T(8,128)(2,1)} %collective-permute-done.37.refs_3_), channel_id=1, source_target_pairs={{0,2},{2,0},{4,6},{6,4},{8,10},{10,8},{12,14},{14,12},{16,18},{18,... | collective-permute-start | bytes 1990664 | tf_op jit(solution)/shard_map/ppermute | solution.py:701
  173.7 37.7 %collective-permute-start.43 = (bf16[144,2304]{1,0:T(8,128)(2,1)}, bf16[144,2304]{1,0:T(8,128)(2,1)}, u32[]{:S(2)}, u32[]{:S(2)}) collective-permute-start(bf16[144,2304]{1,0:T(8,128)(2,1)} %collective-permute-done.37.refs_3_), channel_id=1, source_target_pairs={{0,4},{2,6},{4,0},{6,2},{8,12},{10,14},{12,8},{14,10},{16,20},{18,... | collective-permute-start | bytes 1990664 | tf_op jit(solution)/shard_map/ppermute | solution.py:697
  174.9 31.3 %collective-permute-start.46 = (bf16[144,2304]{1,0:T(8,128)(2,1)}, bf16[144,2304]{1,0:T(8,128)(2,1)}, u32[]{:S(2)}, u32[]{:S(2)}) collective-permute-start(bf16[144,2304]{1,0:T(8,128)(2,1)} %collective-permute-done.38.refs_5_), channel_id=1, source_target_pairs={{0,2},{2,0},{4,6},{6,4},{8,10},{10,8},{12,14},{14,12},{16,18},{18,... | collective-permute-start | bytes 1990664 | tf_op jit(solution)/shard_map/ppermute | solution.py:701
  275.3 51.8 %collective-permute-start.49 = (bf16[2,2,4,144,1152]{4,3,2,1,0:T(8,128)(2,1)}, bf16[2,2,4,144,1152]{4,3,2,1,0:T(8,128)(2,1)}, u32[]{:S(2)}, u32[]{:S(2)}) collective-permute-start(bf16[2,2,4,144,1152]{4,3,2,1,0:T(8,128)(2,1)} %get-tuple-element.261), channel_id=1, source_target_pairs={{0,2},{2,0},{4,6},{6,4},{8,10},{10,8},{12,14},{14,12},{16,18},{18,... | collective-permute-start | bytes 15925256 | tf_op jit(solution)/shard_map/ppermute | solution.py:701
  327.0 27.5 %collective-permute-start.50 = (bf16[2,4,72,4608]{3,2,1,0:T(8,128)(2,1)}, bf16[2,4,72,4608]{3,2,1,0:T(8,128)(2,1)}, u32[]{:S(2)}, u32[]{:S(2)}) collective-permute-start(bf16[2,4,72,4608]{3,2,1,0:T(8,128)(2,1)} %get-tuple-element.268), channel_id=1, source_target_pairs={{0,2},{2,0},{4,6},{6,4},{8,10},{10,8},{12,14},{14,12},{16,18},{18,... | collective-permute-start | bytes 15925256 | tf_op jit(solution)/shard_map/ppermute | solution.py:701
  335.0 95.3 %collective-permute-start.51 = (bf16[2,4,144,1152]{3,2,1,0:T(8,128)(2,1)}, bf16[2,4,144,1152]{3,2,1,0:T(8,128)(2,1)}, u32[]{:S(2)}, u32[]{:S(2)}) collective-permute-start(bf16[2,4,144,1152]{3,2,1,0:T(8,128)(2,1)} %get-tuple-element.370), channel_id=1, source_target_pairs={{0,1},{1,0},{2,3},{3,2},{4,5},{5,4},{6,7},{7,6},{8,9},{9,8},{10,11... | collective-permute-start | bytes 7962632 | tf_op jit(solution)/shard_map/ppermute | solution.py:709
  354.6 211.5 %reduce-scatter.6.cloned.1.call-start = ((), (), s32[]{:S(2)}) async-start(), calls=%async_computation.4 | async-start | bytes 3317760 | tf_op jit(solution)/shard_map/reduce_scatter | solution.py:841
  361.4 68.9 %collective-permute-start.52 = (bf16[4,72,4608]{2,1,0:T(8,128)(2,1)}, bf16[4,72,4608]{2,1,0:T(8,128)(2,1)}, u32[]{:S(2)}, u32[]{:S(2)}) collective-permute-start(bf16[4,72,4608]{2,1,0:T(8,128)(2,1)} %get-tuple-element.368), channel_id=1, source_target_pairs={{0,4},{2,6},{4,0},{6,2},{8,12},{10,14},{12,8},{14,10},{16,20},{18,... | collective-permute-start | bytes 7962632 | tf_op jit(solution)/shard_map/ppermute | solution.py:697
  439.9 24.3 %collective-permute-start.53 = (bf16[288,1152]{1,0:T(8,128)(2,1)S(1)}, bf16[288,1152]{1,0:T(8,128)(2,1)S(1)}, u32[]{:S(2)}, u32[]{:S(2)}) collective-permute-start(bf16[288,1152]{1,0:T(8,128)(2,1)S(1)} %slice.229), channel_id=1, source_target_pairs={{0,1},{1,0},{2,3},{3,2},{4,5},{5,4},{6,7},{7,6},{8,9},{9,8},{10,11... | collective-permute-start | bytes 1990664 | tf_op jit(solution)/shard_map/ppermute | solution.py:709
  464.5 129.4 %reduce-scatter.8.cloned.1.call-start = ((), (), s32[]{:S(2)}) async-start(), calls=%async_computation.5 | async-start | bytes 1658880 | tf_op jit(solution)/shard_map/reduce_scatter | solution.py:841
  509.6 27.8 %collective-permute-start.63 = (bf16[2,4,144,1152]{3,2,1,0:T(8,128)(2,1)}, bf16[2,4,144,1152]{3,2,1,0:T(8,128)(2,1)}, u32[]{:S(2)}, u32[]{:S(2)}) collective-permute-start(bf16[2,4,144,1152]{3,2,1,0:T(8,128)(2,1)} %get-tuple-element.312), channel_id=1, source_target_pairs={{0,2},{2,0},{4,6},{6,4},{8,10},{10,8},{12,14},{14,12},{16,18},{18,... | collective-permute-start | bytes 7962632 | tf_op jit(solution)/shard_map/ppermute | solution.py:701
  514.0 23.4 %collective-permute-start.62 = (bf16[72,3456]{1,0:T(8,128)(2,1)S(1)}, bf16[72,3456]{1,0:T(8,128)(2,1)S(1)}, u32[]{:S(2)}, u32[]{:S(2)}) collective-permute-start(bf16[72,3456]{1,0:T(8,128)(2,1)S(1)} %copy-done.52), channel_id=1, source_target_pairs={{0,4},{2,6},{4,0},{6,2},{8,12},{10,14},{12,8},{14,10},{16,20},{18,... | collective-permute-start | bytes 1493000 | tf_op jit(solution)/shard_map/ppermute | solution.py:697
  583.8 29.7 %collective-permute-start.73 = (bf16[72,3456]{1,0:T(8,128)(2,1)S(1)}, bf16[72,3456]{1,0:T(8,128)(2,1)}, u32[]{:S(2)}, u32[]{:S(2)}) collective-permute-start(bf16[72,3456]{1,0:T(8,128)(2,1)S(1)} %fusion.35), channel_id=1, source_target_pairs={{0,1},{1,0},{2,3},{3,2},{4,5},{5,4},{6,7},{7,6},{8,9},{9,8},{10,11... | collective-permute-start | bytes 1493000 | tf_op jit(solution)/shard_map/ppermute | solution.py:709
  584.6 28.9 %collective-permute-start.77 = (bf16[72,4608]{1,0:T(8,128)(2,1)}, bf16[72,4608]{1,0:T(8,128)(2,1)S(1)}, u32[]{:S(2)}, u32[]{:S(2)}) collective-permute-start(bf16[72,4608]{1,0:T(8,128)(2,1)} %reduce-scatter.6.cloned.1.call-done), channel_id=1, source_target_pairs={{0,1},{1,0},{2,3},{3,2},{4,5},{5,4},{6,7},{7,6},{8,9},{9,8},{10,11... | collective-permute-start | bytes 1990664 | tf_op jit(solution)/shard_map/ppermute | solution.py:709
  587.9 25.6 %collective-permute-start.74 = (bf16[144,1152]{1,0:T(8,128)(2,1)}, bf16[144,1152]{1,0:T(8,128)(2,1)S(1)}, u32[]{:S(2)}, u32[]{:S(2)}) collective-permute-start(bf16[144,1152]{1,0:T(8,128)(2,1)} %fusion.44), channel_id=1, source_target_pairs={{0,8},{2,10},{4,12},{6,14},{8,16},{10,18},{12,20},{14,22},{16,24},... | collective-permute-start | bytes 995336 | tf_op jit(solution)/shard_map/ppermute | solution.py:705
  587.9 25.6 %collective-permute-start.76 = (bf16[72,1152]{1,0:T(8,128)(2,1)}, bf16[72,1152]{1,0:T(8,128)(2,1)}, u32[]{:S(2)}, u32[]{:S(2)}) collective-permute-start(bf16[72,1152]{1,0:T(8,128)(2,1)} %reduce-scatter.10.cloned.1.call-done), channel_id=1, source_target_pairs={{0,1},{1,0},{2,3},{3,2},{4,5},{5,4},{6,7},{7,6},{8,9},{9,8},{10,11... | collective-permute-start | bytes 497672 | tf_op jit(solution)/shard_map/ppermute | solution.py:709
  (146 other events, 1720.3 us)
Sparse Core Ops, SparseCore 0:
  170.7 89.6 all-gather.1
  354.7 70.7 reduce-scatter.9
  464.6 50.5 reduce-scatter.5
  518.0 35.1 reduce-scatter.7

commit v4 on v3

--- a/solution.py
+++ b/solution.py
@@ -13,190 +13,209 @@
 ROWS = 16
 EPS = 1e-05
 
-SCALE=HD**-0.5
-C2=SCALE*math.log2(math.e)
-REM=576
-TILES={
- 0:[(256,576,258,832,[(0,256,576,258,832),(1,0,464,0,452)]),
-    (0,272,0,258,[(0,0,272,0,258)])],
- 1:[(0,464,0,452,[(0,0,464,0,452),(1,0,576,2,576)]),
-    (448,272,452,710,[(0,448,272,452,710)]),
-    (704,128,710,832,[(0,704,128,710,832)])],
+SCALE = HD**-0.5
+C2 = SCALE * math.log2(math.e)
+REM = 576
+TILES = {
+    0: [
+        (256, 576, 258, 832, [(False, 256, 576, 258, 832), (True, 0, 464, 0, 452)]),
+        (0, 272, 0, 258, [(False, 0, 272, 0, 258)]),
+    ],
+    1: [
+        (0, 464, 0, 452, [(False, 0, 464, 0, 452), (True, 0, 576, 2, 576)]),
+        (448, 272, 452, 710, [(False, 448, 272, 452, 710)]),
+        (704, 128, 710, 832, [(False, 704, 128, 710, 832)]),
+    ],
 }
-NT=(((1,),(1,)),((),()))
-TN=(((0,),(0,)),((),()))
-def dot(a,b,dims=(((1,),(0,)),((),()))):
-    return lax.dot_general(a,b,dims,preferred_element_type=jnp.float32)
-
-def split(n,step):
-    out=[];i=0
-    while i<n:
-        out.append((i,min(step,n-i))); i+=step
-    return out
-
-def fwd_kernel(s_ref, qkv_ref, kvr_ref, *refs, qstep, first):
-    o_ref, l_ref = refs[-2:]
-    h = pl.program_id(0) + first
-
-    @pl.when(h == first)
+NT = (((1,), (1,)), ((), ()))
+
+
+def dot(a, b, dims=(((1,), (0,)), ((), ()))):
+    return lax.dot_general(a, b, dims, preferred_element_type=jnp.float32)
+
+
+def split(n, step):
+    return [(i, min(step, n - i)) for i in range(0, n, step)]
+
+
+def full(shape):
+    return pl.BlockSpec(shape, lambda h, s: (0,) * len(shape), pipeline_mode=pl.Buffered(1))
+
+
+def pair_window(pair):
+    tile = (2 * HD * pair) // 128
+    first = 2 * HD * pair - 128 * tile
+    lane = lax.broadcasted_iota(jnp.int32, (1, 256), 1)
+    left = (lane >= first) & (lane < first + HD)
+    right = (lane >= first + HD) & (lane < first + 2 * HD)
+    base = pl.multiple_of(tile * 128, 128)
+
+    def at(offset, row, count):
+        return slice(row, row + count), pl.ds(pl.multiple_of(base + offset, 128), 256)
+
+    return at, left, right
+
+
+def stacked(value, left, right):
+    zero = jnp.zeros_like(value)
+    return jnp.concatenate([jnp.where(left, value, zero), jnp.where(right, value, zero)], 0)
+
+
+def fwd_kernel(s_ref, qkv_ref, kvr_ref, o_ref, l_ref, *, qstep):
+    pair = pl.program_id(0)
+
+    @pl.when(pair == 0)
     def _():
-        for ref, old in zip((o_ref, l_ref), refs[:-2] or (None, None)):
-            ref[...] = jnp.zeros_like(ref) if old is None else old[...]
-
-    t=jnp.minimum((72*h)//128, 7)
-    lo=72*h-128*t
-    base=pl.multiple_of(t*128,128)
-    def win(ref,off,r0,n):
-        return ref[r0:r0+n, pl.ds(pl.multiple_of(base+off,128),256)]
-    def tile(q0,nq,qv0,qv1,keys):
-        lane=lax.broadcasted_iota(jnp.int32,(1,256),1)
-        hm=(lane>=lo)&(lane<lo+72)
-        for (a,n) in split(nq,qstep):
-            r0=q0+a
-            q=win(qkv_ref,0,r0,n)
-            qm=jnp.where(hm,q,jnp.zeros_like(q))
-            ss=[]
-            for (src,k0,kc,kv0,kv1) in keys:
-                k=win(qkv_ref,D,k0,kc) if src==0 else win(kvr_ref,0,k0,kc)
-                s=dot(qm,k,NT)
-                if kv0>k0 or kv1<k0+kc:
-                    kp=k0+lax.broadcasted_iota(jnp.int32,(1,kc),1)
-                    s=jnp.where((kp>=kv0)&(kp<kv1),s,-1e30)
-                ss.append(s)
-            m=jnp.max(ss[0],axis=1,keepdims=True)
-            for s in ss[1:]: m=jnp.maximum(m,jnp.max(s,axis=1,keepdims=True))
-            mc=m*C2
-            l=None; o=None
-            for s,(src,k0,kc,kv0,kv1) in zip(ss,keys):
-                p=jnp.exp2(s*C2-mc)
-                lp=jnp.sum(p,axis=1,keepdims=True)
-                v=win(qkv_ref,2*D,k0,kc) if src==0 else win(kvr_ref,D,k0,kc)
-                op=dot(p.astype(jnp.bfloat16),v)
-                l=lp if l is None else l+lp
-                o=op if o is None else o+op
-            o=o*(1.0/l)
-            lse=mc+jnp.log2(l)
-            sl=(slice(r0,r0+n),pl.ds(base,256))
-            old=o_ref[sl]; ob=o.astype(jnp.bfloat16)
-            hl=lax.broadcasted_iota(jnp.int32,(1,128),1)==h
-            oldl=l_ref[r0:r0+n,:]
-            if r0<qv0 or r0+n>qv1:
-                row=r0+lax.broadcasted_iota(jnp.int32,(n,1),0)
-                rv=(row>=qv0)&(row<qv1)
-                o_ref[sl]=jnp.where(hm&rv,ob,old)
-                l_ref[r0:r0+n,:]=jnp.where(hl&rv,lse,oldl)
-            else:
-                o_ref[sl]=jnp.where(hm,ob,old)
-                l_ref[r0:r0+n,:]=jnp.where(hl,lse,oldl)
-    for sidx in (0,1):
-        @pl.when(s_ref[0]==sidx)
+        o_ref[...] = jnp.zeros_like(o_ref)
+        l_ref[...] = jnp.zeros_like(l_ref)
+
+    at, left, right = pair_window(pair)
+
+    def chunk(r0, n, qv0, qv1, keys):
+        q2 = stacked(qkv_ref[at(0, r0, n)], left, right)
+        scores = []
+        for far, k0, kc, kv0, kv1 in keys:
+            k = kvr_ref[at(0, k0, kc)] if far else qkv_ref[at(D, k0, kc)]
+            s = dot(q2, k, NT)
+            if kv0 > k0 or kv1 < k0 + kc:
+                kp = k0 + lax.broadcasted_iota(jnp.int32, (1, kc), 1)
+                s = jnp.where((kp >= kv0) & (kp < kv1), s, -1e30)
+            scores.append(s)
+        top = jnp.max(scores[0], axis=1, keepdims=True)
+        for s in scores[1:]:
+            top = jnp.maximum(top, jnp.max(s, axis=1, keepdims=True))
+        top = top * C2
+        total, out = 0.0, 0.0
+        for s, (far, k0, kc, _, _) in zip(scores, keys):
+            p = jnp.exp2(s * C2 - top)
+            total = total + jnp.sum(p, axis=1, keepdims=True)
+            v = kvr_ref[at(D, k0, kc)] if far else qkv_ref[at(2 * D, k0, kc)]
+            out = out + dot(p.astype(jnp.bfloat16), v)
+        out = out * (1.0 / total)
+        lse = top + jnp.log2(total)
+        out = jnp.where(left, out[:n], out[n:]).astype(jnp.bfloat16)
+        head = lax.broadcasted_iota(jnp.int32, (1, 128), 1) - 2 * pair
+        lse = jnp.where(head == 0, lse[:n], lse[n:])
+        keep, keep_l = left | right, (head == 0) | (head == 1)
+        if r0 < qv0 or r0 + n > qv1:
+            row = r0 + lax.broadcasted_iota(jnp.int32, (n, 1), 0)
+            valid = (row >= qv0) & (row < qv1)
+            keep, keep_l = keep & valid, keep_l & valid
+        o_ref[at(0, r0, n)] = jnp.where(keep, out, o_ref[at(0, r0, n)])
+        l_ref[r0 : r0 + n, :] = jnp.where(keep_l, lse, l_ref[r0 : r0 + n, :])
+
+    for side in (0, 1):
+
+        @pl.when(s_ref[0] == side)
         def _():
-            for tl in TILES[sidx]: tile(*tl)
-
-def full(shape,n=1):
-    return pl.BlockSpec(shape,lambda h,s:(0,)*len(shape),pipeline_mode=pl.Buffered(1))
-def attn_fwd(sidx, qkv, kvr, first, count, prev=(), qstep=288):
+            for q0, nq, qv0, qv1, keys in TILES[side]:
+                for a, n in split(nq, qstep):
+                    chunk(q0 + a, n, qv0, qv1, keys)
+
+
+def attn_fwd(sidx, qkv, kvr, qstep=288):
     return pl.pallas_call(
-        lambda *r: fwd_kernel(*r, qstep=qstep, first=first),
+        lambda *r: fwd_kernel(*r, qstep=qstep),
         out_shape=(
             jax.ShapeDtypeStruct((832, D), jnp.bfloat16),
             jax.ShapeDtypeStruct((832, 128), jnp.float32),
         ),
         grid_spec=pltpu.PrefetchScalarGridSpec(
             num_scalar_prefetch=1,
-            grid=(count,),
-            in_specs=[full((832, 3 * D)), full((REM, 2 * D))] + [full(v.shape) for v in prev],
+            grid=(HEADS // 2,),
+            in_specs=[full((832, 3 * D)), full((REM, 2 * D))],
             out_specs=(full((832, D)), full((832, 128))),
         ),
         compiler_params=pltpu.CompilerParams(vmem_limit_bytes=60 * 2**20),
         cost_estimate=pl.CostEstimate(
-            flops=count * 1200 * 10**6, bytes_accessed=12 * 2**20, transcendentals=0
+            flops=20 * 10**9, bytes_accessed=12 * 2**20, transcendentals=0
         ),
         name="attn_fwd",
-    )(sidx, qkv, kvr, *prev)
-
-
-def bwd_kernel(s_ref, qkv_ref, kvr_ref, do_ref, lt_ref, dt_ref, *refs, kstep, expl, first):
-    dqkv_ref, dkvr_ref = refs[-2:]
-    h = pl.program_id(0) + first
-
-    @pl.when(h == first)
+    )(sidx, qkv, kvr)
+
+
+def bwd_kernel(s_ref, qkv_ref, kvr_ref, do_ref, lt_ref, dt_ref, dqkv_ref, dkvr_ref, *, kstep):
+    pair = pl.program_id(0)
+
+    @pl.when(pair == 0)
     def _():
-        for ref, old in zip((dqkv_ref, dkvr_ref), refs[:-2] or (None, None)):
-            ref[...] = jnp.zeros_like(ref) if old is None else old[...]
-
-    t=jnp.minimum((72*h)//128, 7)
-    lo=72*h-128*t
-    base=pl.multiple_of(t*128,128)
-    def ws(off,r0,n):
-        return (slice(r0,r0+n), pl.ds(pl.multiple_of(base+off,128),256))
-    def tile(q0,nq,qv0,qv1,keys):
-        lane=lax.broadcasted_iota(jnp.int32,(1,256),1)
-        hm=(lane>=lo)&(lane<lo+72)
-        q=qkv_ref[ws(0,q0,nq)]; qm=jnp.where(hm,q,jnp.zeros_like(q))
-        do=do_ref[ws(0,q0,nq)]; dom=jnp.where(hm,do,jnp.zeros_like(do))
-        lrow=lt_ref[pl.ds(h,1),:][:,q0:q0+nq]; drow=dt_ref[pl.ds(h,1),:][:,q0:q0+nq]
-        if qv0>q0 or qv1<q0+nq:
-            qp=q0+lax.broadcasted_iota(jnp.int32,(1,nq),1)
-            lrow=jnp.where((qp>=qv0)&(qp<qv1),lrow,1e30)
-        dqt=None
-        for (src,k00,kcc,kv0,kv1) in keys:
-            for (a,kc) in split(kcc,kstep):
-                k0=k00+a
-                k=qkv_ref[ws(D,k0,kc)] if src==0 else kvr_ref[ws(0,k0,kc)]
-                v=qkv_ref[ws(2*D,k0,kc)] if src==0 else kvr_ref[ws(D,k0,kc)]
-                st=dot(k,qm,NT)
-                p=jnp.exp2(st*C2-lrow)
-                if kv0>k0 or kv1<k0+kc:
-                    kp=k0+lax.broadcasted_iota(jnp.int32,(kc,1),0)
-                    p=jnp.where((kp>=kv0)&(kp<kv1),p,0.0)
-                dp=dot(v,dom,NT)
-                ds=(p*(dp-drow)).astype(jnp.bfloat16)
-                dv=dot(p.astype(jnp.bfloat16),dom)
-                dk=dot(ds,qm)*SCALE
-                if src==0:
-                    dqkv_ref[ws(D,k0,kc)]+=dk.astype(jnp.bfloat16)
-                    dqkv_ref[ws(2*D,k0,kc)]+=dv.astype(jnp.bfloat16)
+        dqkv_ref[...] = jnp.zeros_like(dqkv_ref)
+        dkvr_ref[...] = jnp.zeros_like(dkvr_ref)
+
+    at, left, right = pair_window(pair)
+
+    def tile(q0, nq, qv0, qv1, keys):
+        q2 = stacked(qkv_ref[at(0, q0, nq)], left, right)
+        do2 = stacked(do_ref[at(0, q0, nq)], left, right)
+
+        def both(ref, mask):
+            rows = []
+            for h in (0, 1):
+                row = ref[pl.ds(2 * pair + h, 1), :][:, q0 : q0 + nq]
+                if mask and (qv0 > q0 or qv1 < q0 + nq):
+                    qp = q0 + lax.broadcasted_iota(jnp.int32, (1, nq), 1)
+                    row = jnp.where((qp >= qv0) & (qp < qv1), row, 1e30)
+                rows.append(row)
+            return jnp.concatenate(rows, 1)
+
+        lse, row_dot = both(lt_ref, True), both(dt_ref, False)
+        dqt = 0.0
+        for far, first, count, kv0, kv1 in keys:
+            for a, kc in split(count, kstep):
+                k0 = first + a
+                k = kvr_ref[at(0, k0, kc)] if far else qkv_ref[at(D, k0, kc)]
+                v = kvr_ref[at(D, k0, kc)] if far else qkv_ref[at(2 * D, k0, kc)]
+                p = jnp.exp2(dot(k, q2, NT) * C2 - lse)
+                if kv0 > k0 or kv1 < k0 + kc:
+                    kp = k0 + lax.broadcasted_iota(jnp.int32, (kc, 1), 0)
+                    p = jnp.where((kp >= kv0) & (kp < kv1), p, 0.0)
+                ds = (p * (dot(v, do2, NT) - row_dot)).astype(jnp.bfloat16)
+                dv = dot(p.astype(jnp.bfloat16), do2).astype(jnp.bfloat16)
+                dk = (dot(ds, q2) * SCALE).astype(jnp.bfloat16)
+                if far:
+                    dkvr_ref[at(0, k0, kc)] += dk
+                    dkvr_ref[at(D, k0, kc)] += dv
                 else:
-                    dkvr_ref[ws(0,k0,kc)]+=dk.astype(jnp.bfloat16)
-                    dkvr_ref[ws(D,k0,kc)]+=dv.astype(jnp.bfloat16)
-                if expl: d=dot(k.T,ds)
-                else: d=dot(k,ds,TN)
-                dqt=d if dqt is None else dqt+d
-        dq=(dqt*SCALE).T
-        sl=ws(0,q0,nq)
-        dqkv_ref[sl]=dqkv_ref[sl]+jnp.where(hm,dq,0.0).astype(jnp.bfloat16)
-    for sidx in (0,1):
-        @pl.when(s_ref[0]==sidx)
+                    dqkv_ref[at(D, k0, kc)] += dk
+                    dqkv_ref[at(2 * D, k0, kc)] += dv
+                dqt = dqt + dot(k.T, ds)
+        dq = (dqt * SCALE).T
+        dq = jnp.where(left, dq[:nq], jnp.where(right, dq[nq:], 0.0)).astype(jnp.bfloat16)
+        dqkv_ref[at(0, q0, nq)] += dq
+
+    for side in (0, 1):
+
+        @pl.when(s_ref[0] == side)
         def _():
-            for tl in TILES[sidx]: tile(*tl)
-
-def attn_bwd(sidx, qkv, kvr, do, lt, dt, first, count, prev=(), kstep=1024, expl=True):
+            for parts in TILES[side]:
+                tile(*parts)
+
+
+def attn_bwd(sidx, qkv, kvr, do, lt, dt, kstep=1024):
     return pl.pallas_call(
-        lambda *r: bwd_kernel(*r, kstep=kstep, expl=expl, first=first),
+        lambda *r: bwd_kernel(*r, kstep=kstep),
         out_shape=(
             jax.ShapeDtypeStruct((832, 3 * D), jnp.bfloat16),
             jax.ShapeDtypeStruct((REM, 2 * D), jnp.bfloat16),
         ),
         grid_spec=pltpu.PrefetchScalarGridSpec(
             num_scalar_prefetch=1,
-            grid=(count,),
+            grid=(HEADS // 2,),
             in_specs=[
                 full((832, 3 * D)),
                 full((REM, 2 * D)),
                 full((832, D)),
                 full((16, 832)),
                 full((16, 832)),
-            ]
-            + [full(v.shape) for v in prev],
+            ],
             out_specs=(full((832, 3 * D)), full((REM, 2 * D))),
         ),
         compiler_params=pltpu.CompilerParams(vmem_limit_bytes=60 * 2**20),
         cost_estimate=pl.CostEstimate(
-            flops=count * 2500 * 10**6, bytes_accessed=20 * 2**20, transcendentals=0
+            flops=40 * 10**9, bytes_accessed=20 * 2**20, transcendentals=0
         ),
         name="attn_bwd",
-    )(sidx, qkv, kvr, do, lt, dt, *prev)
+    )(sidx, qkv, kvr, do, lt, dt)
 
 
 ERFC = (0.5 * 1.061405429, -0.5 * 1.453152027, 0.5 * 1.421413741, -0.5 * 0.284496736, 0.5 * 0.254829592)
@@ -890,19 +909,18 @@
     s3, t2, s2, q0, t1, s1c, t0c = tied(s3, t2, s2, q0, t1, s1c, t0c)
     t3, r0 = swap_y(s3), swap_y(q0)
     s2c, s3c, t1c, t2c = swap_core(s2), swap_core(s3), swap_core(t1), swap_core(t2)
-    s2c, s3c, t1c, t2c, t3, skip_far = tied(s2c, s3c, t1c, t2c, t3, skip_far)
+    s2c, s3c, t1c, t2c, t3, skip_far, q1, q0 = tied(s2c, s3c, t1c, t2c, t3, skip_far, q1, q0)
+    q2, r1 = next_z(q1), swap_y(q1)
     w_skip = assemble(
         [s0, s1, s2, s3, t0, t1, t2, t3, s0c, s1c, s2c, s3c, t0c, t1c, t2c, swap_core(t3)], "rows"
     )
-    r0, q1, w_skip, q0 = tied(r0, q1, w_skip, q0)
-    q2, r1 = next_z(q1), swap_y(q1)
     skip_flat = b16(f32(take(parts, 0, side)) + f32(skip_far))
     h_zero = fwd_dot(tok_flat, w_skip[:D]) + fwd_dot(skip_flat, w_skip[D:]) + skip_bias
     normed_one, ln1_back = jax.vjp(layer_norm, h_zero, ln1_gain, ln1_bias)
     act_one = b16(normed_one)
     act_send = lax.dynamic_slice(act_one, (shared, 0), (REM, D))
     u0 = core_pair(fc1_w)
-    q2, r1, act_one, act_send, u0, q1 = tied(q2, r1, act_one, act_send, u0, q1)
+    q2, r1, r0, act_one, act_send, u0, q1 = tied(q2, r1, r0, act_one, act_send, u0, q1)
     act_far = swap_seq(act_send)
     q3, r2 = next_z(q2), swap_y(q2)
     q0c, q1c, r0c = swap_core(q0), swap_core(q1), swap_core(r0)
@@ -925,7 +943,7 @@
     w_down = lax.all_gather(fc2_w, "batch", axis=0, tiled=True)
     v2, v3 = swap_y(u2), swap_y(u3)
     u2c, u3c, v1c = swap_core(u2), swap_core(u3), swap_core(v1)
-    att, lse = attn_fwd(index, qkv, kv_far, 0, HEADS)
+    att, lse = attn_fwd(index, qkv, kv_far)
     v2, v3, u2c, u3c, v1c, att = tied(v2, v3, u2c, u3c, v1c, att)
     v2c, v3c = swap_core(v2), swap_core(v3)
     h_one = h_zero + fwd_dot(att, w_proj) + proj_bias
@@ -951,12 +969,13 @@
     d_h_one, d_ln2_gain, d_ln2_bias = ln2_back(d_act_two)
     d_h_one = d_h_one + grad_two
     proj_low = b16(d_h_one)
+    up_got, proj_low, dn = tied(up_got, proj_low, dn)
+    up_far = swap_y(added(up[1], up_got[1]))
+    up = added(up[0], up_got[0])
     d_proj = b16(contract_rows(att, proj_low))
     d_att = b16(back_dot(proj_low, w_proj))
-    d_att, d_proj, up_got, output, dn = tied(d_att, d_proj, up_got, output, dn)
+    d_att, d_proj, output, up = tied(d_att, d_proj, output, up)
     proj_part = sc_sum(d_proj)
-    up_far = swap_y(added(up[1], up_got[1]))
-    up = added(up[0], up_got[0])
     pick = (
         lax.broadcasted_iota(jnp.int32, (D, HEADS), 0) // HD
         == lax.broadcasted_iota(jnp.int32, (D, HEADS), 1)
@@ -965,7 +984,7 @@
         pick, f32(d_att) * f32(att), (((0,), (1,)), ((), ())), precision=lax.Precision.HIGHEST
     )
     lse = lse[:, :HEADS].T
-    d_qkv, d_far = attn_bwd(index, qkv, kv_far, d_att, lse, row_dot, 0, HEADS)
+    d_qkv, d_far = attn_bwd(index, qkv, kv_far, d_att, lse, row_dot)
     far = b16(back_dot(d_far, w_qkv[:, D:]))
     far, d_qkv, d_far, dn, dn_far, up, up_far, proj_part = tied(
         far, d_qkv, d_far, dn, dn_far, up, up_far, proj_part
@@ -1011,42 +1030,44 @@
             jnp.sum(grad_two, axis=0),
         ]
     ).reshape(-1, 128)
-    q_y[3], q_y[2], q, q_send, k, k_got, zero_low, sums = tied(
-        q_y[3], q_y[2], q, q_send, k, k_got, zero_low, sums
+    q_y[3], q_y[2], q, q_send, k, k_got, zero_low, sums, proj_part = tied(
+        q_y[3], q_y[2], q, q_send, k, k_got, zero_low, sums, proj_part
     )
     k_got = swap_core(k_got)
     q_next = next_z(added(q[3], q_y[3]))
-    q_y[1], q_y[0] = swap_y(q_send[1]), swap_y(q_send[0])
+    q_y[1] = swap_y(q_send[1])
+    proj_far = swap_seq(proj_part)
     d_tokens = back_dot(zero_low, w_skip[:D]).reshape(1, count, D)
     sums = vector_step(sums, 1)
-    q_next, q_y, k, k_got, sums, zero_low, d_tokens = tied(
-        q_next, q_y, k, k_got, sums, zero_low, d_tokens
+    q_next, q_y, k, k_got, sums, zero_low, d_tokens, proj_far, up_part = tied(
+        q_next, q_y, k, k_got, sums, zero_low, d_tokens, proj_far, up_part
     )
     q_next = onward(q[2], q_y[2], q_next)
     k_send = [added(k[1, i], k_got[1, i]) for i in range(4)]
-    k_y = {i: swap_y(k_send[i]) for i in (3, 2)}
+    q_y[0] = swap_y(q_send[0])
+    k_y = {3: swap_y(k_send[3])}
     k = added(k[0], k_got[0])
-    sums = vector_step(sums, 0, "seq")
+    up_far = swap_seq(up_part)
+    out_proj = f32(proj_part) + f32(proj_far)
     d_skip = back_dot(zero_low, w_skip[D:]).reshape(1, count, D)
-    q_next, k_y, k, k_send, sums, d_skip = tied(q_next, k_y, k, k_send, sums, d_skip)
+    q_next, q_y, k_y, k, k_send, sums, d_skip, up_far = tied(
+        q_next, q_y, k_y, k, k_send, sums, d_skip, up_far
+    )
     q_next = onward(q[1], q_y[1], q_next)
     k_next = next_z(added(k[3], k_y[3]))
-    k_y[1], k_y[0] = swap_y(k_send[1]), swap_y(k_send[0])
-    q_next, k_next, k_y, up_part, proj_part = tied(q_next, k_next, k_y, up_part, proj_part)
-    up_far = swap_seq(up_part)
-    proj_far = swap_seq(proj_part)
+    k_y[2], k_y[1] = swap_y(k_send[2]), swap_y(k_send[1])
+    out_up = f32(up_part) + f32(up_far)
+    sums = vector_step(sums, 0, "seq")
+    q_next, k_next, k_y, sums, dn_part = tied(q_next, k_next, k_y, sums, dn_part)
     q_sum = b16(f32(q[0]) + f32(q_y[0]) + f32(q_next))
     q_got = swap_seq(q_sum)
     k_next = onward(k[2], k_y[2], k_next)
-    sums = vector_step(sums, 2)
-    q_got, k_next, k_y, sums, dn_part, proj_far, up_far = tied(
-        q_got, k_next, k_y, sums, dn_part, proj_far, up_far
-    )
+    k_y[0] = swap_y(k_send[0])
+    q_got, k_next, k_y, dn_part, sums = tied(q_got, k_next, k_y, dn_part, sums)
     dn_got = swap_seq(dn_part)
-    out_up = f32(up_part) + f32(up_far)
-    out_proj = f32(proj_part) + f32(proj_far)
     out_qkv = f32(q_sum) + f32(q_got)
     k_next = onward(k[1], k_y[1], k_next)
+    sums = vector_step(sums, 2)
     k_next, k_y, sums, dn_got = tied(k_next, k_y, sums, dn_got)
     out_down = by_side(side, dn_part, dn_got)
     k_sum = b16(f32(k[0]) + f32(k_y[0]) + f32(k_next))

time: 654 us -> 639 us (0.977)
  Pallas kernels: 229 us -> 216 us
    ppermute x15, waiting for transfers between devices: 52.9 us -> 75.8 us  [next_z(): return lax.ppermute(v, 'batch', ZUP)]
    ppermute x11, waiting for transfers between devices: 25.1 us -> 7.16 us  [swap_seq(): return lax.ppermute(v, 'seq', [(0, 1), (1, 0)])]
    pallas_call x2, Pallas kernels: 88 us -> 74.7 us  [the longest x1 46.7 us: attn_bwd(): pl.pallas_call(lambda *r: bwd_kernel(*r, kstep=kstep), out_shape=(jax.Sha...]
    ppermute x23, waiting for transfers between devices: 89.9 us -> 77.7 us  [swap_y(): return lax.ppermute(v, 'batch', YSW)]
    convert_element_type x21 -> x22, other arithmetic: 49.2 us -> 54.6 us  [b16(): return v.astype(jnp.bfloat16)]
    unnamed x173 -> x167, local copies, waits for them, and re-layouts: 17.3 us -> 18.3 us
  transfers between devices with their start and end apart: 87 -> 87, of which waited for: 40 -> 42; matrix products, arithmetic and copies ran while one was open for 22% -> 23% of each run, Pallas kernels for 35% -> 34%
where the time goes in v4:
time: 639 us; the launch traced here: 628 us
  Pallas kernels  216 us (34%)
  waiting for transfers between devices  176 us (28%)
  other arithmetic  77.9 us (12%)
  matrix products  72.7 us (11%)
  starting transfers between devices  45.8 us (7%)
  local copies, waits for them, and re-layouts  25.1 us (4%)
  between operations  15.1 us (2%)
    ppermute x23, waiting for transfers between devices, swap_y(): return lax.ppermute(v, 'batch', YSW)  77.7 us
    ppermute x15, waiting for transfers between devices, next_z(): return lax.ppermute(v, 'batch', ZUP)  75.8 us
    convert_element_type x22, other arithmetic, b16(): return v.astype(jnp.bfloat16)  54.6 us
    pallas_call x1, Pallas kernels, mlp_back(): pl.pallas_call(kernel, out_shape=(split, split, whole, whole, jax.ShapeDt...  51.7 us
    pallas_call x1, Pallas kernels, attn_bwd(): pl.pallas_call(lambda *r: bwd_kernel(*r, kstep=kstep), out_shape=(jax.Sha...  46.7 us
    pallas_call x1, Pallas kernels, mlp_up(): pl.pallas_call(kernel, out_shape=(out, out, split, split), grid_spec=pltp...  42.8 us
    dot_general x5, matrix products, back_dot(): lax.dot_general(grad_rows, weight, (((1,), (1,)), ((), ())), preferred_el...  35.4 us
    pallas_call x1, Pallas kernels, attn_fwd(): pl.pallas_call(lambda *r: fwd_kernel(*r, qstep=qstep), out_shape=(jax.Sha...  28 us
  transfers between devices with their start and end apart: 87, of which 42 were waited for; matrix products, arithmetic and copies ran while one was open for 23% of the time, Pallas kernels for 34%

profile of v4, /device:TPU:0, one launch (start us, length us, event | category | flops | bytes accessed | tf_op | source)
XLA Modules:
  0.0 627.9 jit_solution(12518995421067119057)
XLA Ops:
  22.3 7.8 %collective-permute-done.3.refs_5_ = bf16[144,1152]{1,0:T(8,128)(2,1)S(1)} collective-permute-done((bf16[144,1152]{1,0:T(8,128)(2,1)S(1)}, bf16[144,1152]{1,0:T(8,128)(2,1)S(1)}, u32[]{:S(2)}, u32[]{:S(2)}) %collective-permute-start.3) | collective-permute-done | bytes 331808 | tf_op jit(solution)/shard_map/ppermute | solution.py:716
  47.8 6.5 %collective-permute-done.14.refs_7_ = bf16[144,1152]{1,0:T(8,128)(2,1)S(1)} collective-permute-done((bf16[144,1152]{1,0:T(8,128)(2,1)}, bf16[144,1152]{1,0:T(8,128)(2,1)S(1)}, u32[]{:S(2)}, u32[]{:S(2)}) %collective-permute-start.14) | collective-permute-done | bytes 331808 | tf_op jit(solution)/shard_map/ppermute | solution.py:716
  54.2 8.2 %collective-permute-done.16.refs_1_ = bf16[144,2304]{1,0:T(8,128)(2,1)S(1)} collective-permute-done((bf16[144,2304]{1,0:T(8,128)(2,1)S(1)}, bf16[144,2304]{1,0:T(8,128)(2,1)S(1)}, u32[]{:S(2)}, u32[]{:S(2)}) %collective-permute-start.16) | collective-permute-done | bytes 663584 | tf_op jit(solution)/shard_map/ppermute | solution.py:724
  85.3 14.3 %collective-permute-done.23.refs_6_ = bf16[144,2304]{1,0:T(8,128)(2,1)S(1)} collective-permute-done((bf16[144,2304]{1,0:T(8,128)(2,1)S(1)}, bf16[144,2304]{1,0:T(8,128)(2,1)S(1)}, u32[]{:S(2)}, u32[]{:S(2)}) %collective-permute-start.23) | collective-permute-done | bytes 663584 | tf_op jit(solution)/shard_map/ppermute | solution.py:716
  106.9 12.9 %collective-permute-done.27.refs_7_ = bf16[144,2304]{1,0:T(8,128)(2,1)S(1)} collective-permute-done((bf16[144,2304]{1,0:T(8,128)(2,1)S(1)}, bf16[144,2304]{1,0:T(8,128)(2,1)S(1)}, u32[]{:S(2)}, u32[]{:S(2)}) %collective-permute-start.27) | collective-permute-done | bytes 663584 | tf_op jit(solution)/shard_map/ppermute | solution.py:716
  133.5 6.7 %collective-permute-done.34.refs_4_ = bf16[144,2304]{1,0:T(8,128)(2,1)S(1)} collective-permute-done((bf16[144,2304]{1,0:T(8,128)(2,1)S(1)}, bf16[144,2304]{1,0:T(8,128)(2,1)S(1)}, u32[]{:S(2)}, u32[]{:S(2)}) %collective-permute-start.34) | collective-permute-done | bytes 663584 | tf_op jit(solution)/shard_map/ppermute | solution.py:716
  144.3 9.8 %convolution_convert_fusion.1.r_1_ = bf16[832,3456]{1,0:T(8,128)(2,1)} fusion(bf16[832,1152]{1,0:T(8,128)(2,1)S(1)} %add_convert_fusion.7.a_ref, bf16[1152,3456]{1,0:T(8,128)(2,1)S(1)} %get-tuple-element.240), kind=kOutput, calls=%fused_computation.1 | convolution fusion | flops 6627778560 | bytes 15630336 | tf_op jit(solution)/shard_map/dot_general | solution.py:513
  168.7 28.0 %attn_fwd.1 = (bf16[832,1152]{1,0:T(8,128)(2,1)}, f32[832,128]{1,0:T(8,128)}) custom-call(s32[1]{0:T(128)} %bitcast.3.r_0_, bf16[832,3456]{1,0:T(8,128)(2,1)} %convolution_convert_fusion.1.r_1_, bf16[576,2304]{1,0:T(8,128)(2,1)} %fusion.4.r_2_), custom_call_target="tpu_custom_call" | custom-call | flops 20000000000 | bytes 12582912 | tf_op jit(solution)/shard_map/attn_fwd/pallas_call | solution.py:117
  196.8 8.4 %collective-permute-done.43.refs_7_ = bf16[144,2304]{1,0:T(8,128)(2,1)} collective-permute-done((bf16[144,2304]{1,0:T(8,128)(2,1)}, bf16[144,2304]{1,0:T(8,128)(2,1)}, u32[]{:S(2)}, u32[]{:S(2)}) %collective-permute-start.43) | collective-permute-done | bytes 663584 | tf_op jit(solution)/shard_map/ppermute | solution.py:716
  205.7 6.5 %fusion.77 = (f32[832]{0:T(1024)S(1)}, f32[832,1152]{1,0:T(8,128)S(1)}) fusion(f32[1152]{0:T(1024)S(1)} %copy-done.76, f32[832,1152]{1,0:T(8,128)} %copy-done.32, bf16[832,1152]{1,0:T(8,128)(2,1)} %get-tuple-element.248, bf16[1152,1152]{1,0:T(8,128)(2,1)} %copy-done.28), kind=kOutput, calls=%fused_computation.167 | convolution fusion | flops 2211175680 | bytes 12246784 | tf_op jit(solution)/shard_map/dot_general | solution.py:513
  226.1 42.8 %mlp_up.1 = (bf16[832,4608]{1,0:T(8,128)(2,1)}, bf16[832,4608]{1,0:T(8,128)(2,1)}, bf16[2,2,4,144,1152]{4,3,2,1,0:T(8,128)(2,1)}, bf16[2,2,4,144,1152]{4,3,2,1,0:T(8,128)(2,1)}) custom-call(s32[4]{0:T(128)} %copy-done.25, bf16[832,1152]{1,0:T(8,128)(2,1)} %get-tuple-element.407.a_ref, bf16[1152,4608]{1,0:T(8,128)(2,1)} %copy-done, ...), custom_call_target="tpu_custom_call" | custom-call | flops 17666408448 | bytes 26542080 | tf_op jit(solution)/shard_map/mlp_up/pallas_call | solution.py:293
  269.0 51.7 %mlp_back.1 = (bf16[2,4,72,4608]{3,2,1,0:T(8,128)(2,1)}, bf16[2,4,72,4608]{3,2,1,0:T(8,128)(2,1)}, f32[832,1152]{1,0:T(8,128)}, f32[832,1152]{1,0:T(8,128)}, f32[1,4608]{1,0:T(1,128)}) custom-call(s32[4]{0:T(128)} %copy-done.25, bf16[832,1152]{1,0:T(8,128)(2,1)} %get-tuple-element.407.a_ref, bf16[832,1152]{1,0:T(8,128)(2,1)} %get-tuple-element.406.e_ref, ...), custom_call_target="tpu_custom_call" | custom-call | flops 35332816896 | bytes 52428800 | tf_op jit(solution)/shard_map/mlp_back/pallas_call | solution.py:367
  321.9 6.3 %fusion.23 = (bf16[2,4,144,1152]{3,2,1,0:T(8,128)(2,1)}, bf16[2,4,144,1152]{3,2,1,0:T(8,128)(2,1)}) fusion(bf16[2,2,4,144,1152]{4,3,2,1,0:T(8,128)(2,1)} %collective-permute-done.49, bf16[2,2,4,144,1152]{4,3,2,1,0:T(8,128)(2,1)} %get-tuple-element.271), kind=kLoop, calls=%fused_computation.46 | loop fusion | flops 10616832 | bytes 15925248 | tf_op jit(solution)/shard_map/convert_element_type | solution.py:741
  346.6 6.2 fusion.24
  359.6 46.7 %attn_bwd.1 = (bf16[832,3456]{1,0:T(8,128)(2,1)}, bf16[576,2304]{1,0:T(8,128)(2,1)}) custom-call(s32[1]{0:T(128)} %bitcast.3.r_0_, bf16[832,3456]{1,0:T(8,128)(2,1)} %convolution_convert_fusion.1.r_1_, bf16[576,2304]{1,0:T(8,128)(2,1)} %fusion.4.r_2_, bf16[832,1152]{1,0:T(8,128)(2,1)} %convolution_convert_fusion.2.r_3_, f32[16,832]{1,0:T(8,128)} %slice_bitcast_fusion.r_4_, ...), custom_call_target="tpu_custom_call" | custom-call | flops 40000000000 | bytes 20971520 | tf_op jit(solution)/shard_map/attn_bwd/pallas_call | solution.py:195
  406.3 6.9 %fusion.18 = bf16[576,1152]{1,0:T(8,128)(2,1)S(1)} fusion(bf16[576,2304]{1,0:T(8,128)(2,1)} %get-tuple-element.293.h_ref, bf16[1152,3456]{1,0:T(8,128)(2,1)} %copy-done.27), kind=kOutput, calls=%fused_computation.43 | convolution fusion | flops 3058311168 | bytes 9289728 | tf_op jit(solution)/shard_map/dot_general | solution.py:523
  413.3 8.5 %collective-permute-done.52 = bf16[4,72,4608]{2,1,0:T(8,128)(2,1)} collective-permute-done((bf16[4,72,4608]{2,1,0:T(8,128)(2,1)}, bf16[4,72,4608]{2,1,0:T(8,128)(2,1)}, u32[]{:S(2)}, u32[]{:S(2)}) %collective-permute-start.52) | collective-permute-done | bytes 2654240 | tf_op jit(solution)/shard_map/ppermute | solution.py:716
  437.3 22.4 %qkv_grad.1 = (bf16[2,4,72,3456]{3,2,1,0:T(8,128)(2,1)}, bf16[2,4,72,3456]{3,2,1,0:T(8,128)(2,1)}) custom-call(s32[4]{0:T(128)} %copy-done.25, bf16[832,1152]{1,0:T(8,128)(2,1)} %copy-done.44, bf16[576,1152]{1,0:T(8,128)(2,1)} %copy-done.74, bf16[832,3456]{1,0:T(8,128)(2,1)} %get-tuple-element.300.g_ref, bf16[576,2304]{1,0:T(8,128)(2,1)} %get-tuple-element.293.h_ref), custom_call_target="tpu_custom_call" | custom-call | flops 11041505280 | bytes 41943040 | tf_op jit(solution)/shard_map/qkv_grad/pallas_call | solution.py:429
  462.2 12.2 %fusion.78 = f32[832,1152]{1,0:T(8,128)S(1)} fusion(bf16[832,3456]{1,0:T(8,128)(2,1)} %get-tuple-element.300.g_ref, bf16[1152,3456]{1,0:T(8,128)(2,1)} %copy-done.27), kind=kOutput, calls=%fused_computation.168 | convolution fusion | flops 6624903168 | bytes 17547264 | tf_op jit(solution)/shard_map/dot_general | solution.py:523
  495.0 9.6 %skip_back.1 = (bf16[2,4,144,1152]{3,2,1,0:T(8,128)(2,1)S(1)}, bf16[2,4,144,1152]{3,2,1,0:T(8,128)(2,1)}) custom-call(s32[4]{0:T(128)S(1)} %copy-done.26, bf16[832,1152]{1,0:T(8,128)(2,1)S(1)} %bitcast.137, bf16[832,1152]{1,0:T(8,128)(2,1)S(1)} %copy-done.3, bf16[832,1152]{1,0:T(8,128)(2,1)S(1)} %get-tuple-element.329.g_ref), custom_call_target="tpu_custom_call" | custom-call | flops 4416602112 | bytes 12582912 | tf_op jit(solution)/shard_map/skip_back/pallas_call | solution.py:479
  511.8 7.1 %convolution_bitcast_fusion.2 = f32[1,832,1152]{2,1,0:T(8,128)} fusion(bf16[832,1152]{1,0:T(8,128)(2,1)} %copy-done.4, bf16[2304,1152]{1,0:T(8,128)(2,1)} %copy-done.1), kind=kOutput, calls=%fused_computation.21 | convolution fusion | flops 2208301056 | bytes 8404992 | tf_op jit(solution)/shard_map/dot_general | solution.py:523
  520.3 8.6 %collective-permute-done.60 = bf16[72,3456]{1,0:T(8,128)(2,1)} collective-permute-done((bf16[72,3456]{1,0:T(8,128)(2,1)}, bf16[72,3456]{1,0:T(8,128)(2,1)}, u32[]{:S(2)}, u32[]{:S(2)}) %collective-permute-start.60) | collective-permute-done | bytes 497696 | tf_op jit(solution)/shard_map/ppermute | solution.py:724
  544.1 14.1 %collective-permute-done.65 = bf16[72,3456]{1,0:T(8,128)(2,1)S(1)} collective-permute-done((bf16[72,3456]{1,0:T(8,128)(2,1)S(1)}, bf16[72,3456]{1,0:T(8,128)(2,1)S(1)}, u32[]{:S(2)}, u32[]{:S(2)}) %collective-permute-start.65) | collective-permute-done | bytes 497696 | tf_op jit(solution)/shard_map/ppermute | solution.py:724
  567.0 15.7 %collective-permute-done.70 = bf16[144,1152]{1,0:T(8,128)(2,1)} collective-permute-done((bf16[144,1152]{1,0:T(8,128)(2,1)}, bf16[144,1152]{1,0:T(8,128)(2,1)}, u32[]{:S(2)}, u32[]{:S(2)}) %collective-permute-start.70) | collective-permute-done | bytes 331808 | tf_op jit(solution)/shard_map/ppermute | solution.py:724
  (414 shorter events, 244.9 us)
Async XLA Ops:
  7.2 261.7 %all-gather.2.cloned.1.call-start = ((), (), s32[]{:S(2)}) async-start(), calls=%async_computation.3 | async-start | bytes 11280384 | tf_op jit(solution)/shard_map/all_gather | solution.py:943
  16.1 46.3 %collective-permute-start.15 = (bf16[832,1152]{1,0:T(8,128)(2,1)}, bf16[832,1152]{1,0:T(8,128)(2,1)}, u32[]{:S(2)}, u32[]{:S(2)}) collective-permute-start(bf16[832,1152]{1,0:T(8,128)(2,1)} %dynamic-slice_bitcast_fusion), channel_id=1, source_target_pairs={{0,1},{1,0},{2,3},{3,2},{4,5},{5,4},{6,7},{7,6},{8,9},{9,8},{10,11... | collective-permute-start | bytes 5750792 | tf_op jit(solution)/shard_map/ppermute | solution.py:728
  46.9 31.9 %collective-permute-start.20 = (bf16[144,2304]{1,0:T(8,128)(2,1)S(1)}, bf16[144,2304]{1,0:T(8,128)(2,1)S(1)}, u32[]{:S(2)}, u32[]{:S(2)}) collective-permute-start(bf16[144,2304]{1,0:T(8,128)(2,1)S(1)} %maximum_select_fusion.1.refs_0_), channel_id=1, source_target_pairs={{0,4},{2,6},{4,0},{6,2},{8,12},{10,14},{12,8},{14,10},{16,20},{18,... | collective-permute-start | bytes 1990664 | tf_op jit(solution)/shard_map/ppermute | solution.py:716
  105.0 35.1 %collective-permute-start.36 = (bf16[576,1152]{1,0:T(8,128)(2,1)S(1)}, bf16[576,1152]{1,0:T(8,128)(2,1)S(1)}, u32[]{:S(2)}, u32[]{:S(2)}) collective-permute-start(bf16[576,1152]{1,0:T(8,128)(2,1)S(1)} %constant_dynamic-slice_fusion), channel_id=1, source_target_pairs={{0,1},{1,0},{2,3},{3,2},{4,5},{5,4},{6,7},{7,6},{8,9},{9,8},{10,11... | collective-permute-start | bytes 3981320 | tf_op jit(solution)/shard_map/ppermute | solution.py:728
  142.9 21.4 %collective-permute-start.38 = (bf16[144,2304]{1,0:T(8,128)(2,1)S(1)}, bf16[144,2304]{1,0:T(8,128)(2,1)}, u32[]{:S(2)}, u32[]{:S(2)}) collective-permute-start(bf16[144,2304]{1,0:T(8,128)(2,1)S(1)} %collective-permute-done.28.refs_1_), channel_id=1, source_target_pairs={{0,4},{2,6},{4,0},{6,2},{8,12},{10,14},{12,8},{14,10},{16,20},{18,... | collective-permute-start | bytes 1990664 | tf_op jit(solution)/shard_map/ppermute | solution.py:716
  164.3 260.2 %reduce-scatter.10.cloned.1.call-start = ((), (), s32[]{:S(2)}) async-start(), calls=%async_computation.6 | async-start | bytes 2820096
  166.3 30.4 %collective-permute-start.44 = (bf16[144,2304]{1,0:T(8,128)(2,1)S(1)}, bf16[144,2304]{1,0:T(8,128)(2,1)}, u32[]{:S(2)}, u32[]{:S(2)}) collective-permute-start(bf16[144,2304]{1,0:T(8,128)(2,1)S(1)} %collective-permute-done.33.refs_2_), channel_id=1, source_target_pairs={{0,2},{2,0},{4,6},{6,4},{8,10},{10,8},{12,14},{14,12},{16,18},{18,... | collective-permute-start | bytes 1990664 | tf_op jit(solution)/shard_map/ppermute | solution.py:720
  166.4 30.3 %collective-permute-start.42 = (bf16[144,2304]{1,0:T(8,128)(2,1)S(1)}, bf16[144,2304]{1,0:T(8,128)(2,1)}, u32[]{:S(2)}, u32[]{:S(2)}) collective-permute-start(bf16[144,2304]{1,0:T(8,128)(2,1)S(1)} %collective-permute-done.33.refs_2_), channel_id=1, source_target_pairs={{0,4},{2,6},{4,0},{6,2},{8,12},{10,14},{12,8},{14,10},{16,20},{18,... | collective-permute-start | bytes 1990664 | tf_op jit(solution)/shard_map/ppermute | solution.py:716
  167.7 29.1 %collective-permute-start.45 = (bf16[144,2304]{1,0:T(8,128)(2,1)}, bf16[144,2304]{1,0:T(8,128)(2,1)}, u32[]{:S(2)}, u32[]{:S(2)}) collective-permute-start(bf16[144,2304]{1,0:T(8,128)(2,1)} %copy-done.6), channel_id=1, source_target_pairs={{0,2},{2,0},{4,6},{6,4},{8,10},{10,8},{12,14},{14,12},{16,18},{18,... | collective-permute-start | bytes 1990664 | tf_op jit(solution)/shard_map/ppermute | solution.py:720
  167.8 37.3 %collective-permute-start.43 = (bf16[144,2304]{1,0:T(8,128)(2,1)}, bf16[144,2304]{1,0:T(8,128)(2,1)}, u32[]{:S(2)}, u32[]{:S(2)}) collective-permute-start(bf16[144,2304]{1,0:T(8,128)(2,1)} %copy-done.6), channel_id=1, source_target_pairs={{0,4},{2,6},{4,0},{6,2},{8,12},{10,14},{12,8},{14,10},{16,20},{18,... | collective-permute-start | bytes 1990664 | tf_op jit(solution)/shard_map/ppermute | solution.py:716
  168.7 28.1 %collective-permute-start.46 = (bf16[144,2304]{1,0:T(8,128)(2,1)}, bf16[144,2304]{1,0:T(8,128)(2,1)}, u32[]{:S(2)}, u32[]{:S(2)}) collective-permute-start(bf16[144,2304]{1,0:T(8,128)(2,1)} %collective-permute-done.38.refs_5_), channel_id=1, source_target_pairs={{0,2},{2,0},{4,6},{6,4},{8,10},{10,8},{12,14},{14,12},{16,18},{18,... | collective-permute-start | bytes 1990664 | tf_op jit(solution)/shard_map/ppermute | solution.py:720
  268.9 51.7 %collective-permute-start.49 = (bf16[2,2,4,144,1152]{4,3,2,1,0:T(8,128)(2,1)}, bf16[2,2,4,144,1152]{4,3,2,1,0:T(8,128)(2,1)}, u32[]{:S(2)}, u32[]{:S(2)}) collective-permute-start(bf16[2,2,4,144,1152]{4,3,2,1,0:T(8,128)(2,1)} %get-tuple-element.263), channel_id=1, source_target_pairs={{0,2},{2,0},{4,6},{6,4},{8,10},{10,8},{12,14},{14,12},{16,18},{18,... | collective-permute-start | bytes 15925256 | tf_op jit(solution)/shard_map/ppermute | solution.py:720
  328.2 85.0 %collective-permute-start.51 = (bf16[2,4,144,1152]{3,2,1,0:T(8,128)(2,1)}, bf16[2,4,144,1152]{3,2,1,0:T(8,128)(2,1)}, u32[]{:S(2)}, u32[]{:S(2)}) collective-permute-start(bf16[2,4,144,1152]{3,2,1,0:T(8,128)(2,1)} %get-tuple-element.377), channel_id=1, source_target_pairs={{0,1},{1,0},{2,3},{3,2},{4,5},{5,4},{6,7},{7,6},{8,9},{9,8},{10,11... | collective-permute-start | bytes 7962632 | tf_op jit(solution)/shard_map/ppermute | solution.py:728
  352.9 167.4 %reduce-scatter.6.cloned.1.call-start = ((), (), s32[]{:S(2)}) async-start(), calls=%async_computation.4 | async-start | bytes 3317760 | tf_op jit(solution)/shard_map/reduce_scatter | solution.py:860
  352.9 68.9 %collective-permute-start.52 = (bf16[4,72,4608]{2,1,0:T(8,128)(2,1)}, bf16[4,72,4608]{2,1,0:T(8,128)(2,1)}, u32[]{:S(2)}, u32[]{:S(2)}) collective-permute-start(bf16[4,72,4608]{2,1,0:T(8,128)(2,1)} %get-tuple-element.375), channel_id=1, source_target_pairs={{0,4},{2,6},{4,0},{6,2},{8,12},{10,14},{12,8},{14,10},{16,20},{18,... | collective-permute-start | bytes 7962632 | tf_op jit(solution)/shard_map/ppermute | solution.py:716
  435.2 24.5 %collective-permute-start.53 = (bf16[288,1152]{1,0:T(8,128)(2,1)}, bf16[288,1152]{1,0:T(8,128)(2,1)}, u32[]{:S(2)}, u32[]{:S(2)}) collective-permute-start(bf16[288,1152]{1,0:T(8,128)(2,1)} %slice.229), channel_id=1, source_target_pairs={{0,1},{1,0},{2,3},{3,2},{4,5},{5,4},{6,7},{7,6},{8,9},{9,8},{10,11... | collective-permute-start | bytes 1990664 | tf_op jit(solution)/shard_map/ppermute | solution.py:728
  436.7 23.1 %collective-permute-start.54 = (bf16[2,144,1152]{2,1,0:T(8,128)(2,1)}, bf16[2,144,1152]{2,1,0:T(8,128)(2,1)}, u32[]{:S(2)}, u32[]{:S(2)}) collective-permute-start(bf16[2,144,1152]{2,1,0:T(8,128)(2,1)} %get-tuple-element.297), channel_id=1, source_target_pairs={{0,4},{2,6},{4,0},{6,2},{8,12},{10,14},{12,8},{14,10},{16,20},{18,... | collective-permute-start | bytes 1990664 | tf_op jit(solution)/shard_map/ppermute | solution.py:716
  460.0 107.0 %reduce-scatter.8.cloned.1.call-start = ((), (), s32[]{:S(2)}) async-start(), calls=%async_computation.5 | async-start | bytes 1658880 | tf_op jit(solution)/shard_map/reduce_scatter | solution.py:860
  481.4 23.3 %collective-permute-start.59 = (bf16[72,3456]{1,0:T(8,128)(2,1)S(1)}, bf16[72,3456]{1,0:T(8,128)(2,1)S(1)}, u32[]{:S(2)}, u32[]{:S(2)}) collective-permute-start(bf16[72,3456]{1,0:T(8,128)(2,1)S(1)} %get-tuple-element.382), channel_id=1, source_target_pairs={{0,4},{2,6},{4,0},{6,2},{8,12},{10,14},{12,8},{14,10},{16,20},{18,... | collective-permute-start | bytes 1493000 | tf_op jit(solution)/shard_map/ppermute | solution.py:716
  482.0 22.8 %collective-permute-start.58 = (bf16[72,3456]{1,0:T(8,128)(2,1)S(1)}, bf16[72,3456]{1,0:T(8,128)(2,1)S(1)}, u32[]{:S(2)}, u32[]{:S(2)}) collective-permute-start(bf16[72,3456]{1,0:T(8,128)(2,1)S(1)} %get-tuple-element.383), channel_id=1, source_target_pairs={{0,4},{2,6},{4,0},{6,2},{8,12},{10,14},{12,8},{14,10},{16,20},{18,... | collective-permute-start | bytes 1493000 | tf_op jit(solution)/shard_map/ppermute | solution.py:716
  504.8 24.1 %collective-permute-start.62 = (bf16[2,4,144,1152]{3,2,1,0:T(8,128)(2,1)}, bf16[2,4,144,1152]{3,2,1,0:T(8,128)(2,1)}, u32[]{:S(2)}, u32[]{:S(2)}) collective-permute-start(bf16[2,4,144,1152]{3,2,1,0:T(8,128)(2,1)} %get-tuple-element.316), channel_id=1, source_target_pairs={{0,2},{2,0},{4,6},{6,4},{8,10},{10,8},{12,14},{14,12},{16,18},{18,... | collective-permute-start | bytes 7962632 | tf_op jit(solution)/shard_map/ppermute | solution.py:720
  519.0 22.9 %collective-permute-start.66 = (bf16[72,3456]{1,0:T(8,128)(2,1)S(1)}, bf16[72,3456]{1,0:T(8,128)(2,1)}, u32[]{:S(2)}, u32[]{:S(2)}) collective-permute-start(bf16[72,3456]{1,0:T(8,128)(2,1)S(1)} %get-tuple-element.324), channel_id=1, source_target_pairs={{0,4},{2,6},{4,0},{6,2},{8,12},{10,14},{12,8},{14,10},{16,20},{18,... | collective-permute-start | bytes 1493000 | tf_op jit(solution)/shard_map/ppermute | solution.py:716
  529.0 29.3 %collective-permute-start.68 = (bf16[72,4608]{1,0:T(8,128)(2,1)}, bf16[72,4608]{1,0:T(8,128)(2,1)S(1)}, u32[]{:S(2)}, u32[]{:S(2)}) collective-permute-start(bf16[72,4608]{1,0:T(8,128)(2,1)} %reduce-scatter.6.cloned.1.call-done), channel_id=1, source_target_pairs={{0,1},{1,0},{2,3},{3,2},{4,5},{5,4},{6,7},{7,6},{8,9},{9,8},{10,11... | collective-permute-start | bytes 1990664 | tf_op jit(solution)/shard_map/ppermute | solution.py:728
  566.4 22.2 %collective-permute-start.76 = (bf16[144,1152]{1,0:T(8,128)(2,1)}, bf16[144,1152]{1,0:T(8,128)(2,1)}, u32[]{:S(2)}, u32[]{:S(2)}) collective-permute-start(bf16[144,1152]{1,0:T(8,128)(2,1)} %get-tuple-element.346), channel_id=1, source_target_pairs={{0,4},{2,6},{4,0},{6,2},{8,12},{10,14},{12,8},{14,10},{16,20},{18,... | collective-permute-start | bytes 995336 | tf_op jit(solution)/shard_map/ppermute | solution.py:716
  (143 other events, 1658.0 us)
Sparse Core Ops, SparseCore 0:
  164.5 90.0 all-gather.1
  353.0 71.4 reduce-scatter.9
  460.1 51.4 reduce-scatter.5
  514.5 41.5 reduce-scatter.7

commit v5 on v4

--- a/solution.py
+++ b/solution.py
@@ -127,9 +127,6 @@
             out_specs=(full((832, D)), full((832, 128))),
         ),
         compiler_params=pltpu.CompilerParams(vmem_limit_bytes=60 * 2**20),
-        cost_estimate=pl.CostEstimate(
-            flops=20 * 10**9, bytes_accessed=12 * 2**20, transcendentals=0
-        ),
         name="attn_fwd",
     )(sidx, qkv, kvr)
 
@@ -211,9 +208,6 @@
             out_specs=(full((832, 3 * D)), full((REM, 2 * D))),
         ),
         compiler_params=pltpu.CompilerParams(vmem_limit_bytes=60 * 2**20),
-        cost_estimate=pl.CostEstimate(
-            flops=40 * 10**9, bytes_accessed=20 * 2**20, transcendentals=0
-        ),
         name="attn_bwd",
     )(sidx, qkv, kvr, do, lt, dt)
 
@@ -306,11 +300,6 @@
             scratch_shapes=[pltpu.VMEM((tile, rows), jnp.bfloat16)],
         ),
         compiler_params=pltpu.CompilerParams(vmem_limit_bytes=60 * 2**20),
-        cost_estimate=pl.CostEstimate(
-            flops=4 * rows * D * width,
-            bytes_accessed=5 * D * width,
-            transcendentals=rows * width,
-        ),
         name="mlp_up",
     )(at, act, weight, bias.reshape(1, width), grad)
 
@@ -398,9 +387,6 @@
             ],
         ),
         compiler_params=pltpu.CompilerParams(vmem_limit_bytes=62 * 2**20),
-        cost_estimate=pl.CostEstimate(
-            flops=8 * rows * D * width, bytes_accessed=50 * 2**20, transcendentals=0
-        ),
         name="mlp_back",
     )(at, act, grad, gelu, slope, w_up, w_down)
 
@@ -447,9 +433,6 @@
             ],
         ),
         compiler_params=pltpu.CompilerParams(vmem_limit_bytes=60 * 2**20),
-        cost_estimate=pl.CostEstimate(
-            flops=10 * rows * D * D, bytes_accessed=40 * 2**20, transcendentals=0
-        ),
         name="qkv_grad",
     )(at, act, act_far, grad, grad_far)
 
@@ -487,9 +470,6 @@
             scratch_shapes=[pltpu.VMEM((2 * D, rows), jnp.bfloat16)],
         ),
         compiler_params=pltpu.CompilerParams(vmem_limit_bytes=40 * 2**20),
-        cost_estimate=pl.CostEstimate(
-            flops=4 * rows * D * D, bytes_accessed=12 * 2**20, transcendentals=0
-        ),
         name="skip_back",
     )(at, tok, skip, grad)
 
@@ -826,9 +806,6 @@
             pltpu.SemaphoreType.DMA((32,)),
         ],
         compiler_params=pltpu.CompilerParams(vmem_limit_bytes=16 * 2**20),
-        cost_estimate=pl.CostEstimate(
-            flops=0, bytes_accessed=64 * rows * cols, transcendentals=0
-        ),
         name="assemble",
     )(jnp.stack([*place(), lax.axis_index("seq").astype(jnp.int32)]), *pieces)
     return out if split else out[0]
@@ -1009,7 +986,9 @@
     q_send = [added(q[1, i], q_got[1, i]) for i in range(4)]
     q_y = {i: swap_y(q_send[i]) for i in (3, 2)}
     q = added(q[0], q_got[0])
-    dn_part = z_scatter(added(dn, jnp.concatenate([dn_low, dn_high], 0)).reshape(4 * 144, D))
+    dn = added(dn, jnp.concatenate([dn_low, dn_high], 0))
+    dn = [take(dn, 0, (place()[0] + i) % 4) for i in range(4)]
+    dn_next = next_z(dn[3])
     d_h_zero, d_ln1_gain, d_ln1_bias = ln1_back(d_act_one)
     d_h_zero = d_h_zero + d_h_one
     zero_low = b16(d_h_zero)
@@ -1030,18 +1009,20 @@
             jnp.sum(grad_two, axis=0),
         ]
     ).reshape(-1, 128)
-    q_y[3], q_y[2], q, q_send, k, k_got, zero_low, sums, proj_part = tied(
-        q_y[3], q_y[2], q, q_send, k, k_got, zero_low, sums, proj_part
-    )
+    q_y[3], q_y[2], q, q_send, k, k_got, zero_low, sums, proj_part, dn_next, dn = tied(
+        q_y[3], q_y[2], q, q_send, k, k_got, zero_low, sums, proj_part, dn_next, dn
+    )
+    dn_next = next_z(added(dn[2], dn_next))
     k_got = swap_core(k_got)
     q_next = next_z(added(q[3], q_y[3]))
     q_y[1] = swap_y(q_send[1])
     proj_far = swap_seq(proj_part)
     d_tokens = back_dot(zero_low, w_skip[:D]).reshape(1, count, D)
     sums = vector_step(sums, 1)
-    q_next, q_y, k, k_got, sums, zero_low, d_tokens, proj_far, up_part = tied(
-        q_next, q_y, k, k_got, sums, zero_low, d_tokens, proj_far, up_part
-    )
+    q_next, q_y, k, k_got, sums, zero_low, d_tokens, proj_far, up_part, dn_next = tied(
+        q_next, q_y, k, k_got, sums, zero_low, d_tokens, proj_far, up_part, dn_next
+    )
+    dn_next = next_z(added(dn[1], dn_next))
     q_next = onward(q[2], q_y[2], q_next)
     k_send = [added(k[1, i], k_got[1, i]) for i in range(4)]
     q_y[0] = swap_y(q_send[0])
@@ -1050,29 +1031,34 @@
     up_far = swap_seq(up_part)
     out_proj = f32(proj_part) + f32(proj_far)
     d_skip = back_dot(zero_low, w_skip[D:]).reshape(1, count, D)
-    q_next, q_y, k_y, k, k_send, sums, d_skip, up_far = tied(
-        q_next, q_y, k_y, k, k_send, sums, d_skip, up_far
-    )
+    sums = vector_step(sums, 0, "seq")
+    q_next, q_y, k_y, k, k_send, sums, d_skip, up_far, dn_next = tied(
+        q_next, q_y, k_y, k, k_send, sums, d_skip, up_far, dn_next
+    )
+    dn_part = added(dn[0], dn_next)
+    dn_got = swap_seq(dn_part)
     q_next = onward(q[1], q_y[1], q_next)
     k_next = next_z(added(k[3], k_y[3]))
     k_y[2], k_y[1] = swap_y(k_send[2]), swap_y(k_send[1])
     out_up = f32(up_part) + f32(up_far)
-    sums = vector_step(sums, 0, "seq")
-    q_next, k_next, k_y, sums, dn_part = tied(q_next, k_next, k_y, sums, dn_part)
+    sums = vector_step(sums, 2)
+    q_next, k_next, k_y, sums, dn_part, dn_got = tied(
+        q_next, k_next, k_y, sums, dn_part, dn_got
+    )
+    out_down = by_side(side, dn_part, dn_got)
     q_sum = b16(f32(q[0]) + f32(q_y[0]) + f32(q_next))
     q_got = swap_seq(q_sum)
     k_next = onward(k[2], k_y[2], k_next)
     k_y[0] = swap_y(k_send[0])
-    q_got, k_next, k_y, dn_part, sums = tied(q_got, k_next, k_y, dn_part, sums)
-    dn_got = swap_seq(dn_part)
+    sums = vector_step(sums, 4)
+    q_got, k_next, k_y, sums = tied(q_got, k_next, k_y, sums)
     out_qkv = f32(q_sum) + f32(q_got)
     k_next = onward(k[1], k_y[1], k_next)
-    sums = vector_step(sums, 2)
-    k_next, k_y, sums, dn_got = tied(k_next, k_y, sums, dn_got)
-    out_down = by_side(side, dn_part, dn_got)
+    sums = vector_step(sums, 8)
+    k_next, k_y, sums = tied(k_next, k_y, sums)
     k_sum = b16(f32(k[0]) + f32(k_y[0]) + f32(k_next))
     out_skip = f32(k_sum) + f32(swap_seq(k_sum))
-    sums = vector_step(vector_step(sums, 4), 8).reshape(-1)
+    sums = sums.reshape(-1)
     starts = [0, D, 2 * D, 3 * D, 4 * D, 5 * D, 6 * D, 10 * D, 11 * D]
     sums = [sums[a:b] for a, b in zip(starts, starts[1:])]
     grads = (out_skip, out_qkv, out_proj, out_up, out_down)

time: 639 us -> 632 us (0.989)
  waiting for transfers between devices: 176 us -> 169 us
    ppermute x15 -> x18, waiting for transfers between devices: 75.8 us -> 61.6 us  [next_z(): return lax.ppermute(v, 'batch', ZUP)]
    convert_element_type x22 -> x25, other arithmetic: 54.6 us -> 45.2 us  [b16(): return v.astype(jnp.bfloat16)]
    unnamed x167 -> x163, local copies, waits for them, and re-layouts: 18.3 us -> 17.4 us
  transfers between devices with their start and end apart: 87 -> 89, of which waited for: 42 -> 44; matrix products, arithmetic and copies ran while one was open for 23% -> 20% of each run, Pallas kernels for 34% -> 35%
where the time goes in v5:
time: 632 us; the launch traced here: 622 us
  Pallas kernels  216 us (34%)
  waiting for transfers between devices  169 us (27%)
  matrix products  73.6 us (12%)
  other arithmetic  72.7 us (12%)
  starting transfers between devices  51.9 us (8%)
  local copies, waits for them, and re-layouts  23.4 us (4%)
  between operations  15.3 us (2%)
    ppermute x23, waiting for transfers between devices, swap_y(): return lax.ppermute(v, 'batch', YSW)  82.1 us
    ppermute x18, waiting for transfers between devices, next_z(): return lax.ppermute(v, 'batch', ZUP)  61.6 us
    pallas_call x1, Pallas kernels, mlp_back(): pl.pallas_call(kernel, out_shape=(split, split, whole, whole, jax.ShapeDt...  51.5 us
    pallas_call x1, Pallas kernels, attn_bwd(): pl.pallas_call(lambda *r: bwd_kernel(*r, kstep=kstep), out_shape=(jax.Sha...  46.8 us
    convert_element_type x25, other arithmetic, b16(): return v.astype(jnp.bfloat16)  45.2 us
    pallas_call x1, Pallas kernels, mlp_up(): pl.pallas_call(kernel, out_shape=(out, out, split, split), grid_spec=pltp...  42.7 us
    dot_general x5, matrix products, back_dot(): lax.dot_general(grad_rows, weight, (((1,), (1,)), ((), ())), preferred_el...  35.4 us
    dot_general x5, matrix products, fwd_dot(): return jnp.dot(left, right, preferred_element_type=jnp.float32)  28 us
  transfers between devices with their start and end apart: 89, of which 44 were waited for; matrix products, arithmetic and copies ran while one was open for 20% of the time, Pallas kernels for 35%

profile of v5, /device:TPU:0, one launch (start us, length us, event | category | flops | bytes accessed | tf_op | source)
XLA Modules:
  0.0 621.7 jit_solution(12091464642897459825)
XLA Ops:
  22.3 7.8 %collective-permute-done.3.refs_5_ = bf16[144,1152]{1,0:T(8,128)(2,1)S(1)} collective-permute-done((bf16[144,1152]{1,0:T(8,128)(2,1)S(1)}, bf16[144,1152]{1,0:T(8,128)(2,1)S(1)}, u32[]{:S(2)}, u32[]{:S(2)}) %collective-permute-start.3) | collective-permute-done | bytes 331808 | tf_op jit(solution)/shard_map/ppermute | solution.py:696
  47.8 6.5 %collective-permute-done.14.refs_7_ = bf16[144,1152]{1,0:T(8,128)(2,1)S(1)} collective-permute-done((bf16[144,1152]{1,0:T(8,128)(2,1)}, bf16[144,1152]{1,0:T(8,128)(2,1)S(1)}, u32[]{:S(2)}, u32[]{:S(2)}) %collective-permute-start.14) | collective-permute-done | bytes 331808 | tf_op jit(solution)/shard_map/ppermute | solution.py:696
  54.2 8.2 %collective-permute-done.16.refs_1_ = bf16[144,2304]{1,0:T(8,128)(2,1)S(1)} collective-permute-done((bf16[144,2304]{1,0:T(8,128)(2,1)S(1)}, bf16[144,2304]{1,0:T(8,128)(2,1)S(1)}, u32[]{:S(2)}, u32[]{:S(2)}) %collective-permute-start.16) | collective-permute-done | bytes 663584 | tf_op jit(solution)/shard_map/ppermute | solution.py:704
  85.3 14.3 %collective-permute-done.23.refs_6_ = bf16[144,2304]{1,0:T(8,128)(2,1)S(1)} collective-permute-done((bf16[144,2304]{1,0:T(8,128)(2,1)S(1)}, bf16[144,2304]{1,0:T(8,128)(2,1)S(1)}, u32[]{:S(2)}, u32[]{:S(2)}) %collective-permute-start.23) | collective-permute-done | bytes 663584 | tf_op jit(solution)/shard_map/ppermute | solution.py:696
  106.9 12.9 %collective-permute-done.27.refs_7_ = bf16[144,2304]{1,0:T(8,128)(2,1)S(1)} collective-permute-done((bf16[144,2304]{1,0:T(8,128)(2,1)S(1)}, bf16[144,2304]{1,0:T(8,128)(2,1)S(1)}, u32[]{:S(2)}, u32[]{:S(2)}) %collective-permute-start.27) | collective-permute-done | bytes 663584 | tf_op jit(solution)/shard_map/ppermute | solution.py:696
  133.5 6.7 %collective-permute-done.34.refs_4_ = bf16[144,2304]{1,0:T(8,128)(2,1)S(1)} collective-permute-done((bf16[144,2304]{1,0:T(8,128)(2,1)S(1)}, bf16[144,2304]{1,0:T(8,128)(2,1)S(1)}, u32[]{:S(2)}, u32[]{:S(2)}) %collective-permute-start.34) | collective-permute-done | bytes 663584 | tf_op jit(solution)/shard_map/ppermute | solution.py:696
  144.3 9.8 %convolution_convert_fusion.1.r_1_ = bf16[832,3456]{1,0:T(8,128)(2,1)} fusion(bf16[832,1152]{1,0:T(8,128)(2,1)S(1)} %add_convert_fusion.7.a_ref, bf16[1152,3456]{1,0:T(8,128)(2,1)S(1)} %get-tuple-element.245), kind=kOutput, calls=%fused_computation.1 | convolution fusion | flops 6627778560 | bytes 15630336 | tf_op jit(solution)/shard_map/dot_general | solution.py:493
  168.9 28.0 %attn_fwd.1 = (bf16[832,1152]{1,0:T(8,128)(2,1)}, f32[832,128]{1,0:T(8,128)}) custom-call(s32[1]{0:T(128)} %bitcast.3.r_0_, bf16[832,3456]{1,0:T(8,128)(2,1)} %convolution_convert_fusion.1.r_1_, bf16[576,2304]{1,0:T(8,128)(2,1)} %fusion.4.r_2_), custom_call_target="tpu_custom_call" | custom-call | tf_op jit(solution)/shard_map/attn_fwd/pallas_call | solution.py:117
  196.9 6.4 %collective-permute-done.43.refs_7_ = bf16[144,2304]{1,0:T(8,128)(2,1)} collective-permute-done((bf16[144,2304]{1,0:T(8,128)(2,1)}, bf16[144,2304]{1,0:T(8,128)(2,1)}, u32[]{:S(2)}, u32[]{:S(2)}) %collective-permute-start.43) | collective-permute-done | bytes 663584 | tf_op jit(solution)/shard_map/ppermute | solution.py:696
  203.8 7.3 %fusion.77 = (f32[832]{0:T(1024)S(1)}, f32[832,1152]{1,0:T(8,128)S(1)}) fusion(f32[1152]{0:T(1024)S(1)} %copy-done.74, f32[832,1152]{1,0:T(8,128)} %copy-done.32, bf16[832,1152]{1,0:T(8,128)(2,1)} %get-tuple-element.253, bf16[1152,1152]{1,0:T(8,128)(2,1)} %copy-done.30), kind=kOutput, calls=%fused_computation.174 | convolution fusion | flops 2211175680 | bytes 12246784 | tf_op jit(solution)/shard_map/dot_general | solution.py:493
  225.0 42.7 %mlp_up.1 = (bf16[832,4608]{1,0:T(8,128)(2,1)}, bf16[832,4608]{1,0:T(8,128)(2,1)}, bf16[2,2,4,144,1152]{4,3,2,1,0:T(8,128)(2,1)}, bf16[2,2,4,144,1152]{4,3,2,1,0:T(8,128)(2,1)}) custom-call(s32[4]{0:T(128)} %copy-done.27, bf16[832,1152]{1,0:T(8,128)(2,1)} %get-tuple-element.421.a_ref, bf16[1152,4608]{1,0:T(8,128)(2,1)} %copy-done, ...), custom_call_target="tpu_custom_call" | custom-call | tf_op jit(solution)/shard_map/mlp_up/pallas_call | solution.py:287
  268.3 51.5 %mlp_back.1 = (bf16[2,4,72,4608]{3,2,1,0:T(8,128)(2,1)}, bf16[2,4,72,4608]{3,2,1,0:T(8,128)(2,1)}, f32[832,1152]{1,0:T(8,128)}, f32[832,1152]{1,0:T(8,128)}, f32[1,4608]{1,0:T(1,128)}) custom-call(s32[4]{0:T(128)} %copy-done.27, bf16[832,1152]{1,0:T(8,128)(2,1)} %get-tuple-element.421.a_ref, bf16[832,1152]{1,0:T(8,128)(2,1)} %get-tuple-element.420.e_ref, ...), custom_call_target="tpu_custom_call" | custom-call | tf_op jit(solution)/shard_map/mlp_back/pallas_call | solution.py:356
  332.2 5.9 fusion.23
  347.2 6.3 %fusion.24 = (bf16[4,72,4608]{2,1,0:T(8,128)(2,1)}, bf16[4,72,4608]{2,1,0:T(8,128)(2,1)}) fusion(bf16[2,4,72,4608]{3,2,1,0:T(8,128)(2,1)} %collective-permute-done.50, bf16[2,4,72,4608]{3,2,1,0:T(8,128)(2,1)} %get-tuple-element.280), kind=kLoop, calls=%fused_computation.47 | loop fusion | flops 10616832 | bytes 15925248 | tf_op jit(solution)/shard_map/convert_element_type | solution.py:721
  364.5 46.8 %attn_bwd.1 = (bf16[832,3456]{1,0:T(8,128)(2,1)}, bf16[576,2304]{1,0:T(8,128)(2,1)}) custom-call(s32[1]{0:T(128)} %bitcast.3.r_0_, bf16[832,3456]{1,0:T(8,128)(2,1)} %convolution_convert_fusion.1.r_1_, bf16[576,2304]{1,0:T(8,128)(2,1)} %fusion.4.r_2_, bf16[832,1152]{1,0:T(8,128)(2,1)} %convolution_convert_fusion.2.r_3_, f32[16,832]{1,0:T(8,128)} %slice_bitcast_fusion.r_4_, ...), custom_call_target="tpu_custom_call" | custom-call | tf_op jit(solution)/shard_map/attn_bwd/pallas_call | solution.py:192
  411.3 8.0 %fusion.18 = bf16[576,1152]{1,0:T(8,128)(2,1)} fusion(bf16[576,2304]{1,0:T(8,128)(2,1)} %get-tuple-element.298.h_ref, bf16[1152,3456]{1,0:T(8,128)(2,1)} %copy-done.29), kind=kOutput, calls=%fused_computation.43 | convolution fusion | flops 3058311168 | bytes 9289728 | tf_op jit(solution)/shard_map/dot_general | solution.py:503
  436.6 22.4 %qkv_grad.1 = (bf16[2,4,72,3456]{3,2,1,0:T(8,128)(2,1)}, bf16[2,4,72,3456]{3,2,1,0:T(8,128)(2,1)}) custom-call(s32[4]{0:T(128)} %copy-done.27, bf16[832,1152]{1,0:T(8,128)(2,1)} %copy-done.42, bf16[576,1152]{1,0:T(8,128)(2,1)} %copy-done.49, bf16[832,3456]{1,0:T(8,128)(2,1)} %get-tuple-element.305.g_ref, bf16[576,2304]{1,0:T(8,128)(2,1)} %get-tuple-element.298.h_ref), custom_call_target="tpu_custom_call" | custom-call | tf_op jit(solution)/shard_map/qkv_grad/pallas_call | solution.py:415
  461.5 11.7 %fusion.78 = f32[832,1152]{1,0:T(8,128)S(1)} fusion(bf16[832,3456]{1,0:T(8,128)(2,1)} %get-tuple-element.305.g_ref, bf16[1152,3456]{1,0:T(8,128)(2,1)} %copy-done.29), kind=kOutput, calls=%fused_computation.175 | convolution fusion | flops 6624903168 | bytes 17547264 | tf_op jit(solution)/shard_map/dot_general | solution.py:503
  493.1 9.6 %skip_back.1 = (bf16[2,4,144,1152]{3,2,1,0:T(8,128)(2,1)S(1)}, bf16[2,4,144,1152]{3,2,1,0:T(8,128)(2,1)}) custom-call(s32[4]{0:T(128)S(1)} %copy-done.28, bf16[832,1152]{1,0:T(8,128)(2,1)S(1)} %bitcast.144, bf16[832,1152]{1,0:T(8,128)(2,1)S(1)} %copy-done.2, bf16[832,1152]{1,0:T(8,128)(2,1)S(1)} %get-tuple-element.339.g_ref), custom_call_target="tpu_custom_call" | custom-call | tf_op jit(solution)/shard_map/skip_back/pallas_call | solution.py:462
  502.9 7.5 %collective-permute-done.58 = bf16[72,3456]{1,0:T(8,128)(2,1)S(1)} collective-permute-done((bf16[72,3456]{1,0:T(8,128)(2,1)}, bf16[72,3456]{1,0:T(8,128)(2,1)S(1)}, u32[]{:S(2)}, u32[]{:S(2)}) %collective-permute-start.58) | collective-permute-done | bytes 497696 | tf_op jit(solution)/shard_map/ppermute | solution.py:696
  525.9 10.3 %collective-permute-done.61 = bf16[72,3456]{1,0:T(8,128)(2,1)} collective-permute-done((bf16[72,3456]{1,0:T(8,128)(2,1)}, bf16[72,3456]{1,0:T(8,128)(2,1)}, u32[]{:S(2)}, u32[]{:S(2)}) %collective-permute-start.61) | collective-permute-done | bytes 497696 | tf_op jit(solution)/shard_map/ppermute | solution.py:704
  546.0 6.5 %convolution_bitcast_fusion.1 = f32[1,832,1152]{2,1,0:T(8,128)} fusion(bf16[832,1152]{1,0:T(8,128)(2,1)S(1)} %get-tuple-element.339.g_ref, bf16[2304,1152]{1,0:T(8,128)(2,1)} %copy-done.3), kind=kOutput, calls=%fused_computation.20 | convolution fusion | flops 2208301056 | bytes 8404992 | tf_op jit(solution)/shard_map/dot_general | solution.py:503
  554.1 9.0 %collective-permute-done.67 = bf16[72,3456]{1,0:T(8,128)(2,1)S(1)} collective-permute-done((bf16[72,3456]{1,0:T(8,128)(2,1)S(1)}, bf16[72,3456]{1,0:T(8,128)(2,1)S(1)}, u32[]{:S(2)}, u32[]{:S(2)}) %collective-permute-start.67) | collective-permute-done | bytes 497696 | tf_op jit(solution)/shard_map/ppermute | solution.py:704
  569.7 7.7 %collective-permute-done.74 = bf16[144,1152]{1,0:T(8,128)(2,1)S(1)} collective-permute-done((bf16[144,1152]{1,0:T(8,128)(2,1)S(1)}, bf16[144,1152]{1,0:T(8,128)(2,1)S(1)}, u32[]{:S(2)}, u32[]{:S(2)}) %collective-permute-start.74) | collective-permute-done | bytes 331808 | tf_op jit(solution)/shard_map/ppermute | solution.py:704
  (417 shorter events, 252.7 us)
Async XLA Ops:
  7.2 260.6 %all-gather.2.cloned.1.call-start = ((), (), s32[]{:S(2)}) async-start(), calls=%async_computation.2 | async-start | bytes 11280384 | tf_op jit(solution)/shard_map/all_gather | solution.py:920
  16.1 46.3 %collective-permute-start.15 = (bf16[832,1152]{1,0:T(8,128)(2,1)}, bf16[832,1152]{1,0:T(8,128)(2,1)}, u32[]{:S(2)}, u32[]{:S(2)}) collective-permute-start(bf16[832,1152]{1,0:T(8,128)(2,1)} %dynamic-slice_bitcast_fusion), channel_id=1, source_target_pairs={{0,1},{1,0},{2,3},{3,2},{4,5},{5,4},{6,7},{7,6},{8,9},{9,8},{10,11... | collective-permute-start | bytes 5750792 | tf_op jit(solution)/shard_map/ppermute | solution.py:708
  46.9 31.9 %collective-permute-start.20 = (bf16[144,2304]{1,0:T(8,128)(2,1)S(1)}, bf16[144,2304]{1,0:T(8,128)(2,1)S(1)}, u32[]{:S(2)}, u32[]{:S(2)}) collective-permute-start(bf16[144,2304]{1,0:T(8,128)(2,1)S(1)} %maximum_select_fusion.1.refs_0_), channel_id=1, source_target_pairs={{0,4},{2,6},{4,0},{6,2},{8,12},{10,14},{12,8},{14,10},{16,20},{18,... | collective-permute-start | bytes 1990664 | tf_op jit(solution)/shard_map/ppermute | solution.py:696
  105.0 35.1 %collective-permute-start.36 = (bf16[576,1152]{1,0:T(8,128)(2,1)S(1)}, bf16[576,1152]{1,0:T(8,128)(2,1)S(1)}, u32[]{:S(2)}, u32[]{:S(2)}) collective-permute-start(bf16[576,1152]{1,0:T(8,128)(2,1)S(1)} %constant_dynamic-slice_fusion), channel_id=1, source_target_pairs={{0,1},{1,0},{2,3},{3,2},{4,5},{5,4},{6,7},{7,6},{8,9},{9,8},{10,11... | collective-permute-start | bytes 3981320 | tf_op jit(solution)/shard_map/ppermute | solution.py:708
  142.9 21.4 %collective-permute-start.40 = (bf16[144,2304]{1,0:T(8,128)(2,1)S(1)}, bf16[144,2304]{1,0:T(8,128)(2,1)S(1)}, u32[]{:S(2)}, u32[]{:S(2)}) collective-permute-start(bf16[144,2304]{1,0:T(8,128)(2,1)S(1)} %collective-permute-done.28.refs_1_), channel_id=1, source_target_pairs={{0,2},{2,0},{4,6},{6,4},{8,10},{10,8},{12,14},{14,12},{16,18},{18,... | collective-permute-start | bytes 1990664 | tf_op jit(solution)/shard_map/ppermute | solution.py:700
  142.9 21.4 %collective-permute-start.38 = (bf16[144,2304]{1,0:T(8,128)(2,1)S(1)}, bf16[144,2304]{1,0:T(8,128)(2,1)}, u32[]{:S(2)}, u32[]{:S(2)}) collective-permute-start(bf16[144,2304]{1,0:T(8,128)(2,1)S(1)} %collective-permute-done.28.refs_1_), channel_id=1, source_target_pairs={{0,4},{2,6},{4,0},{6,2},{8,12},{10,14},{12,8},{14,10},{16,20},{18,... | collective-permute-start | bytes 1990664 | tf_op jit(solution)/shard_map/ppermute | solution.py:696
  164.3 260.6 %reduce-scatter.7.cloned.1.call-start = ((), (), s32[]{:S(2)}) async-start(), calls=%async_computation.4 | async-start | bytes 2820096
  164.4 32.5 %collective-permute-start.46 = (bf16[144,2304]{1,0:T(8,128)(2,1)}, bf16[144,2304]{1,0:T(8,128)(2,1)}, u32[]{:S(2)}, u32[]{:S(2)}) collective-permute-start(bf16[144,2304]{1,0:T(8,128)(2,1)} %collective-permute-done.38.refs_5_), channel_id=1, source_target_pairs={{0,2},{2,0},{4,6},{6,4},{8,10},{10,8},{12,14},{14,12},{16,18},{18,... | collective-permute-start | bytes 1990664 | tf_op jit(solution)/shard_map/ppermute | solution.py:700
  164.5 32.4 %collective-permute-start.44 = (bf16[144,2304]{1,0:T(8,128)(2,1)S(1)}, bf16[144,2304]{1,0:T(8,128)(2,1)}, u32[]{:S(2)}, u32[]{:S(2)}) collective-permute-start(bf16[144,2304]{1,0:T(8,128)(2,1)S(1)} %collective-permute-done.33.refs_2_), channel_id=1, source_target_pairs={{0,2},{2,0},{4,6},{6,4},{8,10},{10,8},{12,14},{14,12},{16,18},{18,... | collective-permute-start | bytes 1990664 | tf_op jit(solution)/shard_map/ppermute | solution.py:700
  165.0 31.9 %collective-permute-start.42 = (bf16[144,2304]{1,0:T(8,128)(2,1)S(1)}, bf16[144,2304]{1,0:T(8,128)(2,1)}, u32[]{:S(2)}, u32[]{:S(2)}) collective-permute-start(bf16[144,2304]{1,0:T(8,128)(2,1)S(1)} %collective-permute-done.33.refs_2_), channel_id=1, source_target_pairs={{0,4},{2,6},{4,0},{6,2},{8,12},{10,14},{12,8},{14,10},{16,20},{18,... | collective-permute-start | bytes 1990664 | tf_op jit(solution)/shard_map/ppermute | solution.py:696
  166.2 30.7 %collective-permute-start.45 = (bf16[144,2304]{1,0:T(8,128)(2,1)}, bf16[144,2304]{1,0:T(8,128)(2,1)}, u32[]{:S(2)}, u32[]{:S(2)}) collective-permute-start(bf16[144,2304]{1,0:T(8,128)(2,1)} %copy-done.8), channel_id=1, source_target_pairs={{0,2},{2,0},{4,6},{6,4},{8,10},{10,8},{12,14},{14,12},{16,18},{18,... | collective-permute-start | bytes 1990664 | tf_op jit(solution)/shard_map/ppermute | solution.py:700
  166.2 37.1 %collective-permute-start.43 = (bf16[144,2304]{1,0:T(8,128)(2,1)}, bf16[144,2304]{1,0:T(8,128)(2,1)}, u32[]{:S(2)}, u32[]{:S(2)}) collective-permute-start(bf16[144,2304]{1,0:T(8,128)(2,1)} %copy-done.8), channel_id=1, source_target_pairs={{0,4},{2,6},{4,0},{6,2},{8,12},{10,14},{12,8},{14,10},{16,20},{18,... | collective-permute-start | bytes 1990664 | tf_op jit(solution)/shard_map/ppermute | solution.py:696
  267.8 52.0 %collective-permute-start.49 = (bf16[2,2,4,144,1152]{4,3,2,1,0:T(8,128)(2,1)}, bf16[2,2,4,144,1152]{4,3,2,1,0:T(8,128)(2,1)}, u32[]{:S(2)}, u32[]{:S(2)}) collective-permute-start(bf16[2,2,4,144,1152]{4,3,2,1,0:T(8,128)(2,1)} %get-tuple-element.268), channel_id=1, source_target_pairs={{0,2},{2,0},{4,6},{6,4},{8,10},{10,8},{12,14},{14,12},{16,18},{18,... | collective-permute-start | bytes 15925256 | tf_op jit(solution)/shard_map/ppermute | solution.py:700
  353.6 169.9 %reduce-scatter.5.cloned.1.call-start = ((), (), s32[]{:S(2)}) async-start(), calls=%async_computation.3 | async-start | bytes 3317760 | tf_op jit(solution)/shard_map/reduce_scatter | solution.py:837
  353.6 65.7 %collective-permute-start.51 = (bf16[2,4,144,1152]{3,2,1,0:T(8,128)(2,1)}, bf16[2,4,144,1152]{3,2,1,0:T(8,128)(2,1)}, u32[]{:S(2)}, u32[]{:S(2)}) collective-permute-start(bf16[2,4,144,1152]{3,2,1,0:T(8,128)(2,1)} %get-tuple-element.387), channel_id=1, source_target_pairs={{0,1},{1,0},{2,3},{3,2},{4,5},{5,4},{6,7},{7,6},{8,9},{9,8},{10,11... | collective-permute-start | bytes 7962632 | tf_op jit(solution)/shard_map/ppermute | solution.py:708
  355.5 68.5 %collective-permute-start.52 = (bf16[4,72,4608]{2,1,0:T(8,128)(2,1)}, bf16[4,72,4608]{2,1,0:T(8,128)(2,1)}, u32[]{:S(2)}, u32[]{:S(2)}) collective-permute-start(bf16[4,72,4608]{2,1,0:T(8,128)(2,1)} %get-tuple-element.385), channel_id=1, source_target_pairs={{0,4},{2,6},{4,0},{6,2},{8,12},{10,14},{12,8},{14,10},{16,20},{18,... | collective-permute-start | bytes 7962632 | tf_op jit(solution)/shard_map/ppermute | solution.py:696
  434.5 24.5 %collective-permute-start.53 = (bf16[288,1152]{1,0:T(8,128)(2,1)S(1)}, bf16[288,1152]{1,0:T(8,128)(2,1)S(1)}, u32[]{:S(2)}, u32[]{:S(2)}) collective-permute-start(bf16[288,1152]{1,0:T(8,128)(2,1)S(1)} %slice.229), channel_id=1, source_target_pairs={{0,1},{1,0},{2,3},{3,2},{4,5},{5,4},{6,7},{7,6},{8,9},{9,8},{10,11... | collective-permute-start | bytes 1990664 | tf_op jit(solution)/shard_map/ppermute | solution.py:708
  436.0 23.0 %collective-permute-start.54 = (bf16[2,144,1152]{2,1,0:T(8,128)(2,1)}, bf16[2,144,1152]{2,1,0:T(8,128)(2,1)S(1)}, u32[]{:S(2)}, u32[]{:S(2)}) collective-permute-start(bf16[2,144,1152]{2,1,0:T(8,128)(2,1)} %get-tuple-element.302), channel_id=1, source_target_pairs={{0,4},{2,6},{4,0},{6,2},{8,12},{10,14},{12,8},{14,10},{16,20},{18,... | collective-permute-start | bytes 1990664 | tf_op jit(solution)/shard_map/ppermute | solution.py:696
  481.7 21.1 %collective-permute-start.60 = (bf16[144,1152]{1,0:T(8,128)(2,1)S(1)}, bf16[144,1152]{1,0:T(8,128)(2,1)}, u32[]{:S(2)}, u32[]{:S(2)}) collective-permute-start(bf16[144,1152]{1,0:T(8,128)(2,1)S(1)} %get-tuple-element.404), channel_id=1, source_target_pairs={{0,8},{2,10},{4,12},{6,14},{8,16},{10,18},{12,20},{14,22},{16,24},... | collective-permute-start | bytes 995336 | tf_op jit(solution)/shard_map/ppermute | solution.py:704
  487.3 23.0 %collective-permute-start.58 = (bf16[72,3456]{1,0:T(8,128)(2,1)}, bf16[72,3456]{1,0:T(8,128)(2,1)S(1)}, u32[]{:S(2)}, u32[]{:S(2)}) collective-permute-start(bf16[72,3456]{1,0:T(8,128)(2,1)} %get-tuple-element.393), channel_id=1, source_target_pairs={{0,4},{2,6},{4,0},{6,2},{8,12},{10,14},{12,8},{14,10},{16,20},{18,... | collective-permute-start | bytes 1493000 | tf_op jit(solution)/shard_map/ppermute | solution.py:696
  510.3 25.9 %collective-permute-start.63 = (bf16[2,4,144,1152]{3,2,1,0:T(8,128)(2,1)}, bf16[2,4,144,1152]{3,2,1,0:T(8,128)(2,1)}, u32[]{:S(2)}, u32[]{:S(2)}) collective-permute-start(bf16[2,4,144,1152]{3,2,1,0:T(8,128)(2,1)} %get-tuple-element.324), channel_id=1, source_target_pairs={{0,2},{2,0},{4,6},{6,4},{8,10},{10,8},{12,14},{14,12},{16,18},{18,... | collective-permute-start | bytes 7962632 | tf_op jit(solution)/shard_map/ppermute | solution.py:700
  514.5 21.7 %collective-permute-start.61 = (bf16[72,3456]{1,0:T(8,128)(2,1)}, bf16[72,3456]{1,0:T(8,128)(2,1)}, u32[]{:S(2)}, u32[]{:S(2)}) collective-permute-start(bf16[72,3456]{1,0:T(8,128)(2,1)} %fusion.40), channel_id=1, source_target_pairs={{0,8},{2,10},{4,12},{6,14},{8,16},{10,18},{12,20},{14,22},{16,24},... | collective-permute-start | bytes 1493000 | tf_op jit(solution)/shard_map/ppermute | solution.py:704
  522.2 30.3 %collective-permute-start.68 = (bf16[72,3456]{1,0:T(8,128)(2,1)S(1)}, bf16[72,3456]{1,0:T(8,128)(2,1)}, u32[]{:S(2)}, u32[]{:S(2)}) collective-permute-start(bf16[72,3456]{1,0:T(8,128)(2,1)S(1)} %get-tuple-element.334), channel_id=1, source_target_pairs={{0,4},{2,6},{4,0},{6,2},{8,12},{10,14},{12,8},{14,10},{16,20},{18,... | collective-permute-start | bytes 1493000 | tf_op jit(solution)/shard_map/ppermute | solution.py:696
  541.6 21.5 %collective-permute-start.71 = (bf16[72,4608]{1,0:T(8,128)(2,1)S(1)}, bf16[72,4608]{1,0:T(8,128)(2,1)S(1)}, u32[]{:S(2)}, u32[]{:S(2)}) collective-permute-start(bf16[72,4608]{1,0:T(8,128)(2,1)S(1)} %copy-done.52), channel_id=1, source_target_pairs={{0,1},{1,0},{2,3},{3,2},{4,5},{5,4},{6,7},{7,6},{8,9},{9,8},{10,11... | collective-permute-start | bytes 1990664 | tf_op jit(solution)/shard_map/ppermute | solution.py:708
  (143 other events, 1653.5 us)
Sparse Core Ops, SparseCore 0:
  164.5 90.0 all-gather.1
  353.7 71.2 reduce-scatter.6
  459.4 58.5 reduce-scatter.4

commit v6 on v5

--- a/solution.py
+++ b/solution.py
@@ -963,12 +963,11 @@
     lse = lse[:, :HEADS].T
     d_qkv, d_far = attn_bwd(index, qkv, kv_far, d_att, lse, row_dot)
     far = b16(back_dot(d_far, w_qkv[:, D:]))
-    far, d_qkv, d_far, dn, dn_far, up, up_far, proj_part = tied(
-        far, d_qkv, d_far, dn, dn_far, up, up_far, proj_part
-    )
-    up = added(up, up_far)
+    far, d_qkv, d_far, dn, dn_far = tied(far, d_qkv, d_far, dn, dn_far)
     dn_send = [added(dn[1, 0:2], dn_far[1, 0:2]), added(dn[1, 2:4], dn_far[1, 2:4])]
     dn = added(dn[0], dn_far[0])
+    dn, dn_send, up_far = tied(dn, dn_send, up_far)
+    up = added(up, up_far)
     far, d_qkv, d_far, dn, dn_send, up = tied(far, d_qkv, d_far, dn, dn_send, up)
     up_part = z_scatter(up.reshape(4 * 72, 4 * D))
     low_far = swap_seq(far[: REM // 2])

time: 632 us -> 619 us (0.979)
  waiting for transfers between devices: 169 us -> 156 us
    ppermute x23, waiting for transfers between devices: 82.1 us -> 72.8 us  [swap_y(): return lax.ppermute(v, 'batch', YSW)]
    unnamed x163 -> x139, local copies, waits for them, and re-layouts: 17.4 us -> 19.2 us
  transfers between devices with their start and end apart: 89 -> 89, of which waited for: 44 -> 42; matrix products, arithmetic and copies ran while one was open for 20% -> 25% of each run, Pallas kernels for 35% -> 35%
where the time goes in v6:
time: 619 us; the launch traced here: 608 us
  Pallas kernels  215 us (35%)
  waiting for transfers between devices  156 us (25%)
  matrix products  74.1 us (12%)
  other arithmetic  72.3 us (12%)
  starting transfers between devices  49.5 us (8%)
  local copies, waits for them, and re-layouts  25.9 us (4%)
  between operations  15.2 us (2%)
    ppermute x23, waiting for transfers between devices, swap_y(): return lax.ppermute(v, 'batch', YSW)  72.8 us
    ppermute x18, waiting for transfers between devices, next_z(): return lax.ppermute(v, 'batch', ZUP)  62 us
    pallas_call x1, Pallas kernels, mlp_back(): pl.pallas_call(kernel, out_shape=(split, split, whole, whole, jax.ShapeDt...  51.5 us
    convert_element_type x25, other arithmetic, b16(): return v.astype(jnp.bfloat16)  47.8 us
    pallas_call x1, Pallas kernels, attn_bwd(): pl.pallas_call(lambda *r: bwd_kernel(*r, kstep=kstep), out_shape=(jax.Sha...  46.7 us
    pallas_call x1, Pallas kernels, mlp_up(): pl.pallas_call(kernel, out_shape=(out, out, split, split), grid_spec=pltp...  42.7 us
    dot_general x5, matrix products, back_dot(): lax.dot_general(grad_rows, weight, (((1,), (1,)), ((), ())), preferred_el...  36 us
    pallas_call x1, Pallas kernels, attn_fwd(): pl.pallas_call(lambda *r: fwd_kernel(*r, qstep=qstep), out_shape=(jax.Sha...  28 us
  transfers between devices with their start and end apart: 89, of which 42 were waited for; matrix products, arithmetic and copies ran while one was open for 25% of the time, Pallas kernels for 35%

profile of v6, /device:TPU:0, one launch (start us, length us, event | category | flops | bytes accessed | tf_op | source)
XLA Modules:
  0.0 608.3 jit_solution(12706617380139732800)
XLA Ops:
  22.3 7.8 %collective-permute-done.3.refs_5_ = bf16[144,1152]{1,0:T(8,128)(2,1)S(1)} collective-permute-done((bf16[144,1152]{1,0:T(8,128)(2,1)S(1)}, bf16[144,1152]{1,0:T(8,128)(2,1)S(1)}, u32[]{:S(2)}, u32[]{:S(2)}) %collective-permute-start.3) | collective-permute-done | bytes 331808 | tf_op jit(solution)/shard_map/ppermute | solution.py:696
  47.8 6.5 %collective-permute-done.14.refs_7_ = bf16[144,1152]{1,0:T(8,128)(2,1)S(1)} collective-permute-done((bf16[144,1152]{1,0:T(8,128)(2,1)}, bf16[144,1152]{1,0:T(8,128)(2,1)S(1)}, u32[]{:S(2)}, u32[]{:S(2)}) %collective-permute-start.14) | collective-permute-done | bytes 331808 | tf_op jit(solution)/shard_map/ppermute | solution.py:696
  54.2 8.2 %collective-permute-done.16.refs_1_ = bf16[144,2304]{1,0:T(8,128)(2,1)S(1)} collective-permute-done((bf16[144,2304]{1,0:T(8,128)(2,1)S(1)}, bf16[144,2304]{1,0:T(8,128)(2,1)S(1)}, u32[]{:S(2)}, u32[]{:S(2)}) %collective-permute-start.16) | collective-permute-done | bytes 663584 | tf_op jit(solution)/shard_map/ppermute | solution.py:704
  85.3 14.3 %collective-permute-done.23.refs_6_ = bf16[144,2304]{1,0:T(8,128)(2,1)S(1)} collective-permute-done((bf16[144,2304]{1,0:T(8,128)(2,1)S(1)}, bf16[144,2304]{1,0:T(8,128)(2,1)S(1)}, u32[]{:S(2)}, u32[]{:S(2)}) %collective-permute-start.23) | collective-permute-done | bytes 663584 | tf_op jit(solution)/shard_map/ppermute | solution.py:696
  106.9 12.9 %collective-permute-done.27.refs_7_ = bf16[144,2304]{1,0:T(8,128)(2,1)S(1)} collective-permute-done((bf16[144,2304]{1,0:T(8,128)(2,1)S(1)}, bf16[144,2304]{1,0:T(8,128)(2,1)S(1)}, u32[]{:S(2)}, u32[]{:S(2)}) %collective-permute-start.27) | collective-permute-done | bytes 663584 | tf_op jit(solution)/shard_map/ppermute | solution.py:696
  133.5 6.7 %collective-permute-done.34.refs_4_ = bf16[144,2304]{1,0:T(8,128)(2,1)S(1)} collective-permute-done((bf16[144,2304]{1,0:T(8,128)(2,1)S(1)}, bf16[144,2304]{1,0:T(8,128)(2,1)S(1)}, u32[]{:S(2)}, u32[]{:S(2)}) %collective-permute-start.34) | collective-permute-done | bytes 663584 | tf_op jit(solution)/shard_map/ppermute | solution.py:696
  144.3 9.7 %convolution_convert_fusion.1.r_1_ = bf16[832,3456]{1,0:T(8,128)(2,1)} fusion(bf16[832,1152]{1,0:T(8,128)(2,1)S(1)} %add_convert_fusion.7.a_ref, bf16[1152,3456]{1,0:T(8,128)(2,1)S(1)} %get-tuple-element.246), kind=kOutput, calls=%fused_computation.1 | convolution fusion | flops 6627778560 | bytes 15630336 | tf_op jit(solution)/shard_map/dot_general | solution.py:493
  168.9 28.0 %attn_fwd.1 = (bf16[832,1152]{1,0:T(8,128)(2,1)}, f32[832,128]{1,0:T(8,128)}) custom-call(s32[1]{0:T(128)} %bitcast.3.r_0_, bf16[832,3456]{1,0:T(8,128)(2,1)} %convolution_convert_fusion.1.r_1_, bf16[576,2304]{1,0:T(8,128)(2,1)} %fusion.4.r_2_), custom_call_target="tpu_custom_call" | custom-call | tf_op jit(solution)/shard_map/attn_fwd/pallas_call | solution.py:117
  197.0 6.3 %collective-permute-done.43.refs_7_ = bf16[144,2304]{1,0:T(8,128)(2,1)} collective-permute-done((bf16[144,2304]{1,0:T(8,128)(2,1)}, bf16[144,2304]{1,0:T(8,128)(2,1)}, u32[]{:S(2)}, u32[]{:S(2)}) %collective-permute-start.43) | collective-permute-done | bytes 663584 | tf_op jit(solution)/shard_map/ppermute | solution.py:696
  203.8 7.3 %fusion.77 = (f32[832]{0:T(1024)S(1)}, f32[832,1152]{1,0:T(8,128)S(1)}) fusion(f32[1152]{0:T(1024)S(1)} %copy-done.64, f32[832,1152]{1,0:T(8,128)} %copy-done.33, bf16[832,1152]{1,0:T(8,128)(2,1)} %get-tuple-element.254, bf16[1152,1152]{1,0:T(8,128)(2,1)} %copy-done.30), kind=kOutput, calls=%fused_computation.174 | convolution fusion | flops 2211175680 | bytes 12246784 | tf_op jit(solution)/shard_map/dot_general | solution.py:493
  225.1 42.7 %mlp_up.1 = (bf16[832,4608]{1,0:T(8,128)(2,1)}, bf16[832,4608]{1,0:T(8,128)(2,1)}, bf16[2,2,4,144,1152]{4,3,2,1,0:T(8,128)(2,1)}, bf16[2,2,4,144,1152]{4,3,2,1,0:T(8,128)(2,1)}) custom-call(s32[4]{0:T(128)} %copy-done.27, bf16[832,1152]{1,0:T(8,128)(2,1)} %get-tuple-element.423.a_ref, bf16[1152,4608]{1,0:T(8,128)(2,1)} %copy-done, ...), custom_call_target="tpu_custom_call" | custom-call | tf_op jit(solution)/shard_map/mlp_up/pallas_call | solution.py:287
  268.3 51.5 %mlp_back.1 = (bf16[2,4,72,4608]{3,2,1,0:T(8,128)(2,1)}, bf16[2,4,72,4608]{3,2,1,0:T(8,128)(2,1)}, f32[832,1152]{1,0:T(8,128)}, f32[832,1152]{1,0:T(8,128)}, f32[1,4608]{1,0:T(1,128)}) custom-call(s32[4]{0:T(128)} %copy-done.27, bf16[832,1152]{1,0:T(8,128)(2,1)} %get-tuple-element.423.a_ref, bf16[832,1152]{1,0:T(8,128)(2,1)} %get-tuple-element.422.e_ref, ...), custom_call_target="tpu_custom_call" | custom-call | tf_op jit(solution)/shard_map/mlp_back/pallas_call | solution.py:356
  320.8 5.9 fusion.23
  337.0 6.6 %fusion.24 = (bf16[4,72,4608]{2,1,0:T(8,128)(2,1)}, bf16[4,72,4608]{2,1,0:T(8,128)(2,1)}) fusion(bf16[2,4,72,4608]{3,2,1,0:T(8,128)(2,1)} %collective-permute-done.50, bf16[2,4,72,4608]{3,2,1,0:T(8,128)(2,1)} %get-tuple-element.281), kind=kLoop, calls=%fused_computation.47 | loop fusion | flops 10616832 | bytes 15925248 | tf_op jit(solution)/shard_map/convert_element_type | solution.py:721
  359.2 46.7 %attn_bwd.1 = (bf16[832,3456]{1,0:T(8,128)(2,1)}, bf16[576,2304]{1,0:T(8,128)(2,1)}) custom-call(s32[1]{0:T(128)} %bitcast.3.r_0_, bf16[832,3456]{1,0:T(8,128)(2,1)} %convolution_convert_fusion.1.r_1_, bf16[576,2304]{1,0:T(8,128)(2,1)} %fusion.4.r_2_, bf16[832,1152]{1,0:T(8,128)(2,1)} %convolution_convert_fusion.2.r_3_, f32[16,832]{1,0:T(8,128)} %slice_bitcast_fusion.r_4_, ...), custom_call_target="tpu_custom_call" | custom-call | tf_op jit(solution)/shard_map/attn_bwd/pallas_call | solution.py:192
  405.9 6.9 %fusion.18 = bf16[576,1152]{1,0:T(8,128)(2,1)S(1)} fusion(bf16[576,2304]{1,0:T(8,128)(2,1)} %get-tuple-element.300.h_ref, bf16[1152,3456]{1,0:T(8,128)(2,1)} %copy-done.29), kind=kOutput, calls=%fused_computation.43 | convolution fusion | flops 3058311168 | bytes 9289728 | tf_op jit(solution)/shard_map/dot_general | solution.py:503
  423.4 22.4 %qkv_grad.1 = (bf16[2,4,72,3456]{3,2,1,0:T(8,128)(2,1)}, bf16[2,4,72,3456]{3,2,1,0:T(8,128)(2,1)}) custom-call(s32[4]{0:T(128)} %copy-done.27, bf16[832,1152]{1,0:T(8,128)(2,1)} %copy-done.43, bf16[576,1152]{1,0:T(8,128)(2,1)} %copy-done.49, bf16[832,3456]{1,0:T(8,128)(2,1)} %get-tuple-element.307.g_ref, bf16[576,2304]{1,0:T(8,128)(2,1)} %get-tuple-element.300.h_ref), custom_call_target="tpu_custom_call" | custom-call | tf_op jit(solution)/shard_map/qkv_grad/pallas_call | solution.py:415
  449.6 11.9 %fusion.78 = f32[832,1152]{1,0:T(8,128)S(1)} fusion(bf16[832,3456]{1,0:T(8,128)(2,1)} %get-tuple-element.307.g_ref, bf16[1152,3456]{1,0:T(8,128)(2,1)} %copy-done.29), kind=kOutput, calls=%fused_computation.175 | convolution fusion | flops 6624903168 | bytes 17547264 | tf_op jit(solution)/shard_map/dot_general | solution.py:503
  482.0 9.0 %skip_back.1 = (bf16[2,4,144,1152]{3,2,1,0:T(8,128)(2,1)S(1)}, bf16[2,4,144,1152]{3,2,1,0:T(8,128)(2,1)S(1)}) custom-call(s32[4]{0:T(128)S(1)} %copy-done.28, bf16[832,1152]{1,0:T(8,128)(2,1)S(1)} %bitcast.142, bf16[832,1152]{1,0:T(8,128)(2,1)S(1)} %copy-done.2, bf16[832,1152]{1,0:T(8,128)(2,1)S(1)} %get-tuple-element.341.g_ref), custom_call_target="tpu_custom_call" | custom-call | tf_op jit(solution)/shard_map/skip_back/pallas_call | solution.py:462
  505.4 6.5 %convolution_bitcast_fusion.2 = f32[1,832,1152]{2,1,0:T(8,128)} fusion(bf16[832,1152]{1,0:T(8,128)(2,1)S(1)} %get-tuple-element.341.g_ref, bf16[2304,1152]{1,0:T(8,128)(2,1)} %copy-done.3), kind=kOutput, calls=%fused_computation.21 | convolution fusion | flops 2208301056 | bytes 8404992 | tf_op jit(solution)/shard_map/dot_general | solution.py:503
  515.1 9.5 %collective-permute-done.61 = bf16[72,3456]{1,0:T(8,128)(2,1)} collective-permute-done((bf16[72,3456]{1,0:T(8,128)(2,1)}, bf16[72,3456]{1,0:T(8,128)(2,1)}, u32[]{:S(2)}, u32[]{:S(2)}) %collective-permute-start.61) | collective-permute-done | bytes 497696 | tf_op jit(solution)/shard_map/ppermute | solution.py:704
  533.7 6.5 %convolution_bitcast_fusion.1 = f32[1,832,1152]{2,1,0:T(8,128)} fusion(bf16[832,1152]{1,0:T(8,128)(2,1)S(1)} %get-tuple-element.341.g_ref, bf16[2304,1152]{1,0:T(8,128)(2,1)} %copy-done.3), kind=kOutput, calls=%fused_computation.20 | convolution fusion | flops 2208301056 | bytes 8404992 | tf_op jit(solution)/shard_map/dot_general | solution.py:503
  541.6 8.2 %collective-permute-done.67 = bf16[72,3456]{1,0:T(8,128)(2,1)S(1)} collective-permute-done((bf16[72,3456]{1,0:T(8,128)(2,1)S(1)}, bf16[72,3456]{1,0:T(8,128)(2,1)S(1)}, u32[]{:S(2)}, u32[]{:S(2)}) %collective-permute-start.67) | collective-permute-done | bytes 497696 | tf_op jit(solution)/shard_map/ppermute | solution.py:704
  557.7 6.4 %collective-permute-done.74 = bf16[144,1152]{1,0:T(8,128)(2,1)S(1)} collective-permute-done((bf16[144,1152]{1,0:T(8,128)(2,1)S(1)}, bf16[144,1152]{1,0:T(8,128)(2,1)S(1)}, u32[]{:S(2)}, u32[]{:S(2)}) %collective-permute-start.74) | collective-permute-done | bytes 331808 | tf_op jit(solution)/shard_map/ppermute | solution.py:704
  (392 shorter events, 244.6 us)
Async XLA Ops:
  7.2 260.6 %all-gather.2.cloned.1.call-start = ((), (), s32[]{:S(2)}) async-start(), calls=%async_computation.2 | async-start | bytes 11280384 | tf_op jit(solution)/shard_map/all_gather | solution.py:920
  16.1 46.3 %collective-permute-start.15 = (bf16[832,1152]{1,0:T(8,128)(2,1)}, bf16[832,1152]{1,0:T(8,128)(2,1)}, u32[]{:S(2)}, u32[]{:S(2)}) collective-permute-start(bf16[832,1152]{1,0:T(8,128)(2,1)} %dynamic-slice_bitcast_fusion), channel_id=1, source_target_pairs={{0,1},{1,0},{2,3},{3,2},{4,5},{5,4},{6,7},{7,6},{8,9},{9,8},{10,11... | collective-permute-start | bytes 5750792 | tf_op jit(solution)/shard_map/ppermute | solution.py:708
  46.9 31.9 %collective-permute-start.20 = (bf16[144,2304]{1,0:T(8,128)(2,1)S(1)}, bf16[144,2304]{1,0:T(8,128)(2,1)S(1)}, u32[]{:S(2)}, u32[]{:S(2)}) collective-permute-start(bf16[144,2304]{1,0:T(8,128)(2,1)S(1)} %maximum_select_fusion.1.refs_0_), channel_id=1, source_target_pairs={{0,4},{2,6},{4,0},{6,2},{8,12},{10,14},{12,8},{14,10},{16,20},{18,... | collective-permute-start | bytes 1990664 | tf_op jit(solution)/shard_map/ppermute | solution.py:696
  63.2 20.4 %collective-permute-start.24 = (bf16[144,2304]{1,0:T(8,128)(2,1)S(1)}, bf16[144,2304]{1,0:T(8,128)(2,1)S(1)}, u32[]{:S(2)}, u32[]{:S(2)}) collective-permute-start(bf16[144,2304]{1,0:T(8,128)(2,1)S(1)} %maximum_select_fusion.1.refs_0_), channel_id=1, source_target_pairs={{0,2},{2,0},{4,6},{6,4},{8,10},{10,8},{12,14},{14,12},{16,18},{18,... | collective-permute-start | bytes 1990664 | tf_op jit(solution)/shard_map/ppermute | solution.py:700
  105.0 35.1 %collective-permute-start.36 = (bf16[576,1152]{1,0:T(8,128)(2,1)S(1)}, bf16[576,1152]{1,0:T(8,128)(2,1)S(1)}, u32[]{:S(2)}, u32[]{:S(2)}) collective-permute-start(bf16[576,1152]{1,0:T(8,128)(2,1)S(1)} %constant_dynamic-slice_fusion), channel_id=1, source_target_pairs={{0,1},{1,0},{2,3},{3,2},{4,5},{5,4},{6,7},{7,6},{8,9},{9,8},{10,11... | collective-permute-start | bytes 3981320 | tf_op jit(solution)/shard_map/ppermute | solution.py:708
  142.9 21.4 %collective-permute-start.40 = (bf16[144,2304]{1,0:T(8,128)(2,1)S(1)}, bf16[144,2304]{1,0:T(8,128)(2,1)S(1)}, u32[]{:S(2)}, u32[]{:S(2)}) collective-permute-start(bf16[144,2304]{1,0:T(8,128)(2,1)S(1)} %collective-permute-done.28.refs_1_), channel_id=1, source_target_pairs={{0,2},{2,0},{4,6},{6,4},{8,10},{10,8},{12,14},{14,12},{16,18},{18,... | collective-permute-start | bytes 1990664 | tf_op jit(solution)/shard_map/ppermute | solution.py:700
  142.9 21.4 %collective-permute-start.38 = (bf16[144,2304]{1,0:T(8,128)(2,1)S(1)}, bf16[144,2304]{1,0:T(8,128)(2,1)}, u32[]{:S(2)}, u32[]{:S(2)}) collective-permute-start(bf16[144,2304]{1,0:T(8,128)(2,1)S(1)} %collective-permute-done.28.refs_1_), channel_id=1, source_target_pairs={{0,4},{2,6},{4,0},{6,2},{8,12},{10,14},{12,8},{14,10},{16,20},{18,... | collective-permute-start | bytes 1990664 | tf_op jit(solution)/shard_map/ppermute | solution.py:696
  164.3 329.7 %reduce-scatter.7.cloned.1.call-start = ((), (), s32[]{:S(2)}) async-start(), calls=%async_computation.4 | async-start | bytes 2820096
  164.4 32.6 %collective-permute-start.46 = (bf16[144,2304]{1,0:T(8,128)(2,1)}, bf16[144,2304]{1,0:T(8,128)(2,1)}, u32[]{:S(2)}, u32[]{:S(2)}) collective-permute-start(bf16[144,2304]{1,0:T(8,128)(2,1)} %collective-permute-done.38.refs_5_), channel_id=1, source_target_pairs={{0,2},{2,0},{4,6},{6,4},{8,10},{10,8},{12,14},{14,12},{16,18},{18,... | collective-permute-start | bytes 1990664 | tf_op jit(solution)/shard_map/ppermute | solution.py:700
  164.5 32.5 %collective-permute-start.44 = (bf16[144,2304]{1,0:T(8,128)(2,1)S(1)}, bf16[144,2304]{1,0:T(8,128)(2,1)}, u32[]{:S(2)}, u32[]{:S(2)}) collective-permute-start(bf16[144,2304]{1,0:T(8,128)(2,1)S(1)} %collective-permute-done.33.refs_2_), channel_id=1, source_target_pairs={{0,2},{2,0},{4,6},{6,4},{8,10},{10,8},{12,14},{14,12},{16,18},{18,... | collective-permute-start | bytes 1990664 | tf_op jit(solution)/shard_map/ppermute | solution.py:700
  165.0 32.0 %collective-permute-start.42 = (bf16[144,2304]{1,0:T(8,128)(2,1)S(1)}, bf16[144,2304]{1,0:T(8,128)(2,1)}, u32[]{:S(2)}, u32[]{:S(2)}) collective-permute-start(bf16[144,2304]{1,0:T(8,128)(2,1)S(1)} %collective-permute-done.33.refs_2_), channel_id=1, source_target_pairs={{0,4},{2,6},{4,0},{6,2},{8,12},{10,14},{12,8},{14,10},{16,20},{18,... | collective-permute-start | bytes 1990664 | tf_op jit(solution)/shard_map/ppermute | solution.py:696
  166.2 30.8 %collective-permute-start.45 = (bf16[144,2304]{1,0:T(8,128)(2,1)}, bf16[144,2304]{1,0:T(8,128)(2,1)}, u32[]{:S(2)}, u32[]{:S(2)}) collective-permute-start(bf16[144,2304]{1,0:T(8,128)(2,1)} %copy-done.8), channel_id=1, source_target_pairs={{0,2},{2,0},{4,6},{6,4},{8,10},{10,8},{12,14},{14,12},{16,18},{18,... | collective-permute-start | bytes 1990664 | tf_op jit(solution)/shard_map/ppermute | solution.py:700
  166.2 37.1 %collective-permute-start.43 = (bf16[144,2304]{1,0:T(8,128)(2,1)}, bf16[144,2304]{1,0:T(8,128)(2,1)}, u32[]{:S(2)}, u32[]{:S(2)}) collective-permute-start(bf16[144,2304]{1,0:T(8,128)(2,1)} %copy-done.8), channel_id=1, source_target_pairs={{0,4},{2,6},{4,0},{6,2},{8,12},{10,14},{12,8},{14,10},{16,20},{18,... | collective-permute-start | bytes 1990664 | tf_op jit(solution)/shard_map/ppermute | solution.py:696
  267.8 52.0 %collective-permute-start.49 = (bf16[2,2,4,144,1152]{4,3,2,1,0:T(8,128)(2,1)}, bf16[2,2,4,144,1152]{4,3,2,1,0:T(8,128)(2,1)}, u32[]{:S(2)}, u32[]{:S(2)}) collective-permute-start(bf16[2,2,4,144,1152]{4,3,2,1,0:T(8,128)(2,1)} %get-tuple-element.269), channel_id=1, source_target_pairs={{0,2},{2,0},{4,6},{6,4},{8,10},{10,8},{12,14},{14,12},{16,18},{18,... | collective-permute-start | bytes 15925256 | tf_op jit(solution)/shard_map/ppermute | solution.py:700
  326.8 86.1 %collective-permute-start.51 = (bf16[2,4,144,1152]{3,2,1,0:T(8,128)(2,1)}, bf16[2,4,144,1152]{3,2,1,0:T(8,128)(2,1)}, u32[]{:S(2)}, u32[]{:S(2)}) collective-permute-start(bf16[2,4,144,1152]{3,2,1,0:T(8,128)(2,1)} %get-tuple-element.389), channel_id=1, source_target_pairs={{0,1},{1,0},{2,3},{3,2},{4,5},{5,4},{6,7},{7,6},{8,9},{9,8},{10,11... | collective-permute-start | bytes 7962632 | tf_op jit(solution)/shard_map/ppermute | solution.py:708
  343.6 74.9 %collective-permute-start.52 = (bf16[4,72,4608]{2,1,0:T(8,128)(2,1)}, bf16[4,72,4608]{2,1,0:T(8,128)(2,1)}, u32[]{:S(2)}, u32[]{:S(2)}) collective-permute-start(bf16[4,72,4608]{2,1,0:T(8,128)(2,1)} %get-tuple-element.387), channel_id=1, source_target_pairs={{0,4},{2,6},{4,0},{6,2},{8,12},{10,14},{12,8},{14,10},{16,20},{18,... | collective-permute-start | bytes 7962632 | tf_op jit(solution)/shard_map/ppermute | solution.py:696
  353.8 159.6 %reduce-scatter.5.cloned.1.call-start = ((), (), s32[]{:S(2)}) async-start(), calls=%async_computation.3 | async-start | bytes 3317760 | tf_op jit(solution)/shard_map/reduce_scatter | solution.py:837
  422.6 23.2 %collective-permute-start.53 = (bf16[288,1152]{1,0:T(8,128)(2,1)S(1)}, bf16[288,1152]{1,0:T(8,128)(2,1)}, u32[]{:S(2)}, u32[]{:S(2)}) collective-permute-start(bf16[288,1152]{1,0:T(8,128)(2,1)S(1)} %slice.229), channel_id=1, source_target_pairs={{0,1},{1,0},{2,3},{3,2},{4,5},{5,4},{6,7},{7,6},{8,9},{9,8},{10,11... | collective-permute-start | bytes 1990664 | tf_op jit(solution)/shard_map/ppermute | solution.py:708
  422.6 23.1 %collective-permute-start.54 = (bf16[2,144,1152]{2,1,0:T(8,128)(2,1)}, bf16[2,144,1152]{2,1,0:T(8,128)(2,1)S(1)}, u32[]{:S(2)}, u32[]{:S(2)}) collective-permute-start(bf16[2,144,1152]{2,1,0:T(8,128)(2,1)} %get-tuple-element.304), channel_id=1, source_target_pairs={{0,4},{2,6},{4,0},{6,2},{8,12},{10,14},{12,8},{14,10},{16,20},{18,... | collective-permute-start | bytes 1990664 | tf_op jit(solution)/shard_map/ppermute | solution.py:696
  470.3 23.7 %collective-permute-start.60 = (bf16[144,1152]{1,0:T(8,128)(2,1)}, bf16[144,1152]{1,0:T(8,128)(2,1)}, u32[]{:S(2)}, u32[]{:S(2)}) collective-permute-start(bf16[144,1152]{1,0:T(8,128)(2,1)} %get-tuple-element.406), channel_id=1, source_target_pairs={{0,8},{2,10},{4,12},{6,14},{8,16},{10,18},{12,20},{14,22},{16,24},... | collective-permute-start | bytes 995336 | tf_op jit(solution)/shard_map/ppermute | solution.py:704
  475.5 23.1 %collective-permute-start.58 = (bf16[72,3456]{1,0:T(8,128)(2,1)}, bf16[72,3456]{1,0:T(8,128)(2,1)}, u32[]{:S(2)}, u32[]{:S(2)}) collective-permute-start(bf16[72,3456]{1,0:T(8,128)(2,1)} %get-tuple-element.395), channel_id=1, source_target_pairs={{0,4},{2,6},{4,0},{6,2},{8,12},{10,14},{12,8},{14,10},{16,20},{18,... | collective-permute-start | bytes 1493000 | tf_op jit(solution)/shard_map/ppermute | solution.py:696
  498.6 26.0 %collective-permute-start.63 = (bf16[2,4,144,1152]{3,2,1,0:T(8,128)(2,1)}, bf16[2,4,144,1152]{3,2,1,0:T(8,128)(2,1)}, u32[]{:S(2)}, u32[]{:S(2)}) collective-permute-start(bf16[2,4,144,1152]{3,2,1,0:T(8,128)(2,1)} %copy-done.32), channel_id=1, source_target_pairs={{0,2},{2,0},{4,6},{6,4},{8,10},{10,8},{12,14},{14,12},{16,18},{18,... | collective-permute-start | bytes 7962632 | tf_op jit(solution)/shard_map/ppermute | solution.py:700
  512.0 28.3 %collective-permute-start.68 = (bf16[72,3456]{1,0:T(8,128)(2,1)S(1)}, bf16[72,3456]{1,0:T(8,128)(2,1)}, u32[]{:S(2)}, u32[]{:S(2)}) collective-permute-start(bf16[72,3456]{1,0:T(8,128)(2,1)S(1)} %get-tuple-element.336), channel_id=1, source_target_pairs={{0,4},{2,6},{4,0},{6,2},{8,12},{10,14},{12,8},{14,10},{16,20},{18,... | collective-permute-start | bytes 1493000 | tf_op jit(solution)/shard_map/ppermute | solution.py:696
  529.1 20.7 %collective-permute-start.71 = (bf16[72,4608]{1,0:T(8,128)(2,1)S(1)}, bf16[72,4608]{1,0:T(8,128)(2,1)S(1)}, u32[]{:S(2)}, u32[]{:S(2)}) collective-permute-start(bf16[72,4608]{1,0:T(8,128)(2,1)S(1)} %copy-done.53), channel_id=1, source_target_pairs={{0,1},{1,0},{2,3},{3,2},{4,5},{5,4},{6,7},{7,6},{8,9},{9,8},{10,11... | collective-permute-start | bytes 1990664 | tf_op jit(solution)/shard_map/ppermute | solution.py:708
  (131 other events, 1561.6 us)
Sparse Core Ops, SparseCore 0:
  164.5 90.0 all-gather.1
  353.9 68.6 reduce-scatter.6
  447.6 57.4 reduce-scatter.4

commit v7 on v6

--- a/solution.py
+++ b/solution.py
@@ -978,7 +978,7 @@
     high_far = swap_seq(far[REM // 2 :])
     dn_high = swap_y(dn_send[1])
     d_act_one = back_dot(d_qkv, w_qkv)
-    q_got, d_act_one, high_far, dn_high = tied(q_got, d_act_one, high_far, dn_high)
+    q_got, d_act_one, high_far = tied(q_got, d_act_one, high_far)
     far = f32(jnp.concatenate([low_far, high_far], 0))
     here = lax.dynamic_slice(d_act_one, (shared, 0), (REM, D))
     d_act_one = lax.dynamic_update_slice(d_act_one, here + far, (shared, 0))

time: 619 us -> 626 us (1.011)
  waiting for transfers between devices: 156 us -> 163 us
    ppermute x11, waiting for transfers between devices: 10.2 us -> 19.4 us  [swap_seq(): return lax.ppermute(v, 'seq', [(0, 1), (1, 0)])]
  transfers between devices with their start and end apart: 89 -> 89, of which waited for: 42 -> 43; matrix products, arithmetic and copies ran while one was open for 25% -> 24% of each run, Pallas kernels for 35% -> 35%
where the time goes in v7:
time: 626 us; the launch traced here: 616 us
  Pallas kernels  215 us (34%)
  waiting for transfers between devices  163 us (26%)
  matrix products  73.7 us (12%)
  other arithmetic  70.9 us (11%)
  starting transfers between devices  53.1 us (8%)
  local copies, waits for them, and re-layouts  25.1 us (4%)
  between operations  15.2 us (2%)
    ppermute x23, waiting for transfers between devices, swap_y(): return lax.ppermute(v, 'batch', YSW)  72.4 us
    ppermute x18, waiting for transfers between devices, next_z(): return lax.ppermute(v, 'batch', ZUP)  60.7 us
    pallas_call x1, Pallas kernels, mlp_back(): pl.pallas_call(kernel, out_shape=(split, split, whole, whole, jax.ShapeDt...  51.5 us
    convert_element_type x25, other arithmetic, b16(): return v.astype(jnp.bfloat16)  47.5 us
    pallas_call x1, Pallas kernels, attn_bwd(): pl.pallas_call(lambda *r: bwd_kernel(*r, kstep=kstep), out_shape=(jax.Sha...  46.7 us
    pallas_call x1, Pallas kernels, mlp_up(): pl.pallas_call(kernel, out_shape=(out, out, split, split), grid_spec=pltp...  42.7 us
    dot_general x5, matrix products, back_dot(): lax.dot_general(grad_rows, weight, (((1,), (1,)), ((), ())), preferred_el...  35.6 us
    pallas_call x1, Pallas kernels, attn_fwd(): pl.pallas_call(lambda *r: fwd_kernel(*r, qstep=qstep), out_shape=(jax.Sha...  28 us
  transfers between devices with their start and end apart: 89, of which 43 were waited for; matrix products, arithmetic and copies ran while one was open for 24% of the time, Pallas kernels for 35%

profile of v7, /device:TPU:0, one launch (start us, length us, event | category | flops | bytes accessed | tf_op | source)
XLA Modules:
  0.0 615.5 jit_solution(4784383317793281870)
XLA Ops:
  22.3 7.8 %collective-permute-done.3.refs_5_ = bf16[144,1152]{1,0:T(8,128)(2,1)S(1)} collective-permute-done((bf16[144,1152]{1,0:T(8,128)(2,1)S(1)}, bf16[144,1152]{1,0:T(8,128)(2,1)S(1)}, u32[]{:S(2)}, u32[]{:S(2)}) %collective-permute-start.3) | collective-permute-done | bytes 331808 | tf_op jit(solution)/shard_map/ppermute | solution.py:696
  47.8 6.5 %collective-permute-done.14.refs_7_ = bf16[144,1152]{1,0:T(8,128)(2,1)S(1)} collective-permute-done((bf16[144,1152]{1,0:T(8,128)(2,1)}, bf16[144,1152]{1,0:T(8,128)(2,1)S(1)}, u32[]{:S(2)}, u32[]{:S(2)}) %collective-permute-start.14) | collective-permute-done | bytes 331808 | tf_op jit(solution)/shard_map/ppermute | solution.py:696
  54.2 8.2 %collective-permute-done.16.refs_1_ = bf16[144,2304]{1,0:T(8,128)(2,1)S(1)} collective-permute-done((bf16[144,2304]{1,0:T(8,128)(2,1)S(1)}, bf16[144,2304]{1,0:T(8,128)(2,1)S(1)}, u32[]{:S(2)}, u32[]{:S(2)}) %collective-permute-start.16) | collective-permute-done | bytes 663584 | tf_op jit(solution)/shard_map/ppermute | solution.py:704
  85.3 14.3 %collective-permute-done.23.refs_6_ = bf16[144,2304]{1,0:T(8,128)(2,1)S(1)} collective-permute-done((bf16[144,2304]{1,0:T(8,128)(2,1)S(1)}, bf16[144,2304]{1,0:T(8,128)(2,1)S(1)}, u32[]{:S(2)}, u32[]{:S(2)}) %collective-permute-start.23) | collective-permute-done | bytes 663584 | tf_op jit(solution)/shard_map/ppermute | solution.py:696
  106.9 12.9 %collective-permute-done.27.refs_7_ = bf16[144,2304]{1,0:T(8,128)(2,1)S(1)} collective-permute-done((bf16[144,2304]{1,0:T(8,128)(2,1)S(1)}, bf16[144,2304]{1,0:T(8,128)(2,1)S(1)}, u32[]{:S(2)}, u32[]{:S(2)}) %collective-permute-start.27) | collective-permute-done | bytes 663584 | tf_op jit(solution)/shard_map/ppermute | solution.py:696
  133.5 6.7 %collective-permute-done.34.refs_4_ = bf16[144,2304]{1,0:T(8,128)(2,1)S(1)} collective-permute-done((bf16[144,2304]{1,0:T(8,128)(2,1)S(1)}, bf16[144,2304]{1,0:T(8,128)(2,1)S(1)}, u32[]{:S(2)}, u32[]{:S(2)}) %collective-permute-start.34) | collective-permute-done | bytes 663584 | tf_op jit(solution)/shard_map/ppermute | solution.py:696
  144.3 9.7 %convolution_convert_fusion.1.r_1_ = bf16[832,3456]{1,0:T(8,128)(2,1)} fusion(bf16[832,1152]{1,0:T(8,128)(2,1)S(1)} %add_convert_fusion.7.a_ref, bf16[1152,3456]{1,0:T(8,128)(2,1)S(1)} %get-tuple-element.245), kind=kOutput, calls=%fused_computation.1 | convolution fusion | flops 6627778560 | bytes 15630336 | tf_op jit(solution)/shard_map/dot_general | solution.py:493
  168.9 28.0 %attn_fwd.1 = (bf16[832,1152]{1,0:T(8,128)(2,1)}, f32[832,128]{1,0:T(8,128)}) custom-call(s32[1]{0:T(128)} %bitcast.3.r_0_, bf16[832,3456]{1,0:T(8,128)(2,1)} %convolution_convert_fusion.1.r_1_, bf16[576,2304]{1,0:T(8,128)(2,1)} %fusion.4.r_2_), custom_call_target="tpu_custom_call" | custom-call | tf_op jit(solution)/shard_map/attn_fwd/pallas_call | solution.py:117
  197.0 6.3 %collective-permute-done.43.refs_7_ = bf16[144,2304]{1,0:T(8,128)(2,1)} collective-permute-done((bf16[144,2304]{1,0:T(8,128)(2,1)}, bf16[144,2304]{1,0:T(8,128)(2,1)}, u32[]{:S(2)}, u32[]{:S(2)}) %collective-permute-start.43) | collective-permute-done | bytes 663584 | tf_op jit(solution)/shard_map/ppermute | solution.py:696
  203.8 7.3 %fusion.77 = (f32[832]{0:T(1024)S(1)}, f32[832,1152]{1,0:T(8,128)S(1)}) fusion(f32[1152]{0:T(1024)S(1)} %copy-done.64, f32[832,1152]{1,0:T(8,128)} %copy-done.33, bf16[832,1152]{1,0:T(8,128)(2,1)} %get-tuple-element.253, bf16[1152,1152]{1,0:T(8,128)(2,1)} %copy-done.30), kind=kOutput, calls=%fused_computation.174 | convolution fusion | flops 2211175680 | bytes 12246784 | tf_op jit(solution)/shard_map/dot_general | solution.py:493
  225.1 42.7 %mlp_up.1 = (bf16[832,4608]{1,0:T(8,128)(2,1)}, bf16[832,4608]{1,0:T(8,128)(2,1)}, bf16[2,2,4,144,1152]{4,3,2,1,0:T(8,128)(2,1)}, bf16[2,2,4,144,1152]{4,3,2,1,0:T(8,128)(2,1)}) custom-call(s32[4]{0:T(128)} %copy-done.27, bf16[832,1152]{1,0:T(8,128)(2,1)} %get-tuple-element.421.a_ref, bf16[1152,4608]{1,0:T(8,128)(2,1)} %copy-done, ...), custom_call_target="tpu_custom_call" | custom-call | tf_op jit(solution)/shard_map/mlp_up/pallas_call | solution.py:287
  268.3 51.5 %mlp_back.1 = (bf16[2,4,72,4608]{3,2,1,0:T(8,128)(2,1)}, bf16[2,4,72,4608]{3,2,1,0:T(8,128)(2,1)}, f32[832,1152]{1,0:T(8,128)}, f32[832,1152]{1,0:T(8,128)}, f32[1,4608]{1,0:T(1,128)}) custom-call(s32[4]{0:T(128)} %copy-done.27, bf16[832,1152]{1,0:T(8,128)(2,1)} %get-tuple-element.421.a_ref, bf16[832,1152]{1,0:T(8,128)(2,1)} %get-tuple-element.420.e_ref, ...), custom_call_target="tpu_custom_call" | custom-call | tf_op jit(solution)/shard_map/mlp_back/pallas_call | solution.py:356
  320.8 5.9 fusion.23
  337.0 6.6 %fusion.24 = (bf16[4,72,4608]{2,1,0:T(8,128)(2,1)}, bf16[4,72,4608]{2,1,0:T(8,128)(2,1)}) fusion(bf16[2,4,72,4608]{3,2,1,0:T(8,128)(2,1)} %collective-permute-done.50, bf16[2,4,72,4608]{3,2,1,0:T(8,128)(2,1)} %get-tuple-element.280), kind=kLoop, calls=%fused_computation.47 | loop fusion | flops 10616832 | bytes 15925248 | tf_op jit(solution)/shard_map/convert_element_type | solution.py:721
  359.2 46.7 %attn_bwd.1 = (bf16[832,3456]{1,0:T(8,128)(2,1)}, bf16[576,2304]{1,0:T(8,128)(2,1)}) custom-call(s32[1]{0:T(128)} %bitcast.3.r_0_, bf16[832,3456]{1,0:T(8,128)(2,1)} %convolution_convert_fusion.1.r_1_, bf16[576,2304]{1,0:T(8,128)(2,1)} %fusion.4.r_2_, bf16[832,1152]{1,0:T(8,128)(2,1)} %convolution_convert_fusion.2.r_3_, f32[16,832]{1,0:T(8,128)} %slice_bitcast_fusion.r_4_, ...), custom_call_target="tpu_custom_call" | custom-call | tf_op jit(solution)/shard_map/attn_bwd/pallas_call | solution.py:192
  405.9 6.9 %fusion.18 = bf16[576,1152]{1,0:T(8,128)(2,1)S(1)} fusion(bf16[576,2304]{1,0:T(8,128)(2,1)} %get-tuple-element.299.h_ref, bf16[1152,3456]{1,0:T(8,128)(2,1)} %copy-done.29), kind=kOutput, calls=%fused_computation.43 | convolution fusion | flops 3058311168 | bytes 9289728 | tf_op jit(solution)/shard_map/dot_general | solution.py:503
  423.4 22.4 %qkv_grad.1 = (bf16[2,4,72,3456]{3,2,1,0:T(8,128)(2,1)}, bf16[2,4,72,3456]{3,2,1,0:T(8,128)(2,1)}) custom-call(s32[4]{0:T(128)} %copy-done.27, bf16[832,1152]{1,0:T(8,128)(2,1)} %copy-done.43, bf16[576,1152]{1,0:T(8,128)(2,1)} %copy-done.49, bf16[832,3456]{1,0:T(8,128)(2,1)} %get-tuple-element.306.g_ref, bf16[576,2304]{1,0:T(8,128)(2,1)} %get-tuple-element.299.h_ref), custom_call_target="tpu_custom_call" | custom-call | tf_op jit(solution)/shard_map/qkv_grad/pallas_call | solution.py:415
  447.5 11.6 %fusion.78 = f32[832,1152]{1,0:T(8,128)S(1)} fusion(bf16[832,3456]{1,0:T(8,128)(2,1)} %get-tuple-element.306.g_ref, bf16[1152,3456]{1,0:T(8,128)(2,1)} %copy-done.29), kind=kOutput, calls=%fused_computation.175 | convolution fusion | flops 6624903168 | bytes 17547264 | tf_op jit(solution)/shard_map/dot_general | solution.py:503
  463.8 12.5 %collective-permute-done.56 = bf16[288,1152]{1,0:T(8,128)(2,1)S(1)} collective-permute-done((bf16[288,1152]{1,0:T(8,128)(2,1)S(1)}, bf16[288,1152]{1,0:T(8,128)(2,1)S(1)}, u32[]{:S(2)}, u32[]{:S(2)}) %collective-permute-start.56) | collective-permute-done | bytes 663584 | tf_op jit(solution)/shard_map/ppermute | solution.py:708
  490.8 9.0 %skip_back.1 = (bf16[2,4,144,1152]{3,2,1,0:T(8,128)(2,1)S(1)}, bf16[2,4,144,1152]{3,2,1,0:T(8,128)(2,1)S(1)}) custom-call(s32[4]{0:T(128)S(1)} %copy-done.28, bf16[832,1152]{1,0:T(8,128)(2,1)S(1)} %bitcast.142, bf16[832,1152]{1,0:T(8,128)(2,1)S(1)} %copy-done.2, bf16[832,1152]{1,0:T(8,128)(2,1)S(1)} %get-tuple-element.339.g_ref), custom_call_target="tpu_custom_call" | custom-call | tf_op jit(solution)/shard_map/skip_back/pallas_call | solution.py:462
  514.1 6.5 %convolution_bitcast_fusion.2 = f32[1,832,1152]{2,1,0:T(8,128)} fusion(bf16[832,1152]{1,0:T(8,128)(2,1)S(1)} %get-tuple-element.339.g_ref, bf16[2304,1152]{1,0:T(8,128)(2,1)} %copy-done.3), kind=kOutput, calls=%fused_computation.21 | convolution fusion | flops 2208301056 | bytes 8404992 | tf_op jit(solution)/shard_map/dot_general | solution.py:503
  523.8 9.5 %collective-permute-done.61 = bf16[72,3456]{1,0:T(8,128)(2,1)} collective-permute-done((bf16[72,3456]{1,0:T(8,128)(2,1)}, bf16[72,3456]{1,0:T(8,128)(2,1)}, u32[]{:S(2)}, u32[]{:S(2)}) %collective-permute-start.61) | collective-permute-done | bytes 497696 | tf_op jit(solution)/shard_map/ppermute | solution.py:704
  542.5 6.5 %convolution_bitcast_fusion.1 = f32[1,832,1152]{2,1,0:T(8,128)} fusion(bf16[832,1152]{1,0:T(8,128)(2,1)S(1)} %get-tuple-element.339.g_ref, bf16[2304,1152]{1,0:T(8,128)(2,1)} %copy-done.3), kind=kOutput, calls=%fused_computation.20 | convolution fusion | flops 2208301056 | bytes 8404992 | tf_op jit(solution)/shard_map/dot_general | solution.py:503
  550.3 8.2 %collective-permute-done.67 = bf16[72,3456]{1,0:T(8,128)(2,1)S(1)} collective-permute-done((bf16[72,3456]{1,0:T(8,128)(2,1)S(1)}, bf16[72,3456]{1,0:T(8,128)(2,1)S(1)}, u32[]{:S(2)}, u32[]{:S(2)}) %collective-permute-start.67) | collective-permute-done | bytes 497696 | tf_op jit(solution)/shard_map/ppermute | solution.py:704
  (392 shorter events, 246.1 us)
Async XLA Ops:
  7.2 260.6 %all-gather.2.cloned.1.call-start = ((), (), s32[]{:S(2)}) async-start(), calls=%async_computation.2 | async-start | bytes 11280384 | tf_op jit(solution)/shard_map/all_gather | solution.py:920
  16.1 46.3 %collective-permute-start.15 = (bf16[832,1152]{1,0:T(8,128)(2,1)}, bf16[832,1152]{1,0:T(8,128)(2,1)}, u32[]{:S(2)}, u32[]{:S(2)}) collective-permute-start(bf16[832,1152]{1,0:T(8,128)(2,1)} %dynamic-slice_bitcast_fusion), channel_id=1, source_target_pairs={{0,1},{1,0},{2,3},{3,2},{4,5},{5,4},{6,7},{7,6},{8,9},{9,8},{10,11... | collective-permute-start | bytes 5750792 | tf_op jit(solution)/shard_map/ppermute | solution.py:708
  46.9 31.9 %collective-permute-start.20 = (bf16[144,2304]{1,0:T(8,128)(2,1)S(1)}, bf16[144,2304]{1,0:T(8,128)(2,1)S(1)}, u32[]{:S(2)}, u32[]{:S(2)}) collective-permute-start(bf16[144,2304]{1,0:T(8,128)(2,1)S(1)} %maximum_select_fusion.1.refs_0_), channel_id=1, source_target_pairs={{0,4},{2,6},{4,0},{6,2},{8,12},{10,14},{12,8},{14,10},{16,20},{18,... | collective-permute-start | bytes 1990664 | tf_op jit(solution)/shard_map/ppermute | solution.py:696
  105.0 35.1 %collective-permute-start.36 = (bf16[576,1152]{1,0:T(8,128)(2,1)S(1)}, bf16[576,1152]{1,0:T(8,128)(2,1)S(1)}, u32[]{:S(2)}, u32[]{:S(2)}) collective-permute-start(bf16[576,1152]{1,0:T(8,128)(2,1)S(1)} %constant_dynamic-slice_fusion), channel_id=1, source_target_pairs={{0,1},{1,0},{2,3},{3,2},{4,5},{5,4},{6,7},{7,6},{8,9},{9,8},{10,11... | collective-permute-start | bytes 3981320 | tf_op jit(solution)/shard_map/ppermute | solution.py:708
  142.9 21.4 %collective-permute-start.40 = (bf16[144,2304]{1,0:T(8,128)(2,1)S(1)}, bf16[144,2304]{1,0:T(8,128)(2,1)S(1)}, u32[]{:S(2)}, u32[]{:S(2)}) collective-permute-start(bf16[144,2304]{1,0:T(8,128)(2,1)S(1)} %collective-permute-done.28.refs_1_), channel_id=1, source_target_pairs={{0,2},{2,0},{4,6},{6,4},{8,10},{10,8},{12,14},{14,12},{16,18},{18,... | collective-permute-start | bytes 1990664 | tf_op jit(solution)/shard_map/ppermute | solution.py:700
  142.9 21.4 %collective-permute-start.38 = (bf16[144,2304]{1,0:T(8,128)(2,1)S(1)}, bf16[144,2304]{1,0:T(8,128)(2,1)}, u32[]{:S(2)}, u32[]{:S(2)}) collective-permute-start(bf16[144,2304]{1,0:T(8,128)(2,1)S(1)} %collective-permute-done.28.refs_1_), channel_id=1, source_target_pairs={{0,4},{2,6},{4,0},{6,2},{8,12},{10,14},{12,8},{14,10},{16,20},{18,... | collective-permute-start | bytes 1990664 | tf_op jit(solution)/shard_map/ppermute | solution.py:696
  164.3 338.5 %reduce-scatter.7.cloned.1.call-start = ((), (), s32[]{:S(2)}) async-start(), calls=%async_computation.4 | async-start | bytes 2820096
  164.4 32.6 %collective-permute-start.46 = (bf16[144,2304]{1,0:T(8,128)(2,1)}, bf16[144,2304]{1,0:T(8,128)(2,1)}, u32[]{:S(2)}, u32[]{:S(2)}) collective-permute-start(bf16[144,2304]{1,0:T(8,128)(2,1)} %collective-permute-done.38.refs_5_), channel_id=1, source_target_pairs={{0,2},{2,0},{4,6},{6,4},{8,10},{10,8},{12,14},{14,12},{16,18},{18,... | collective-permute-start | bytes 1990664 | tf_op jit(solution)/shard_map/ppermute | solution.py:700
  164.5 32.5 %collective-permute-start.44 = (bf16[144,2304]{1,0:T(8,128)(2,1)S(1)}, bf16[144,2304]{1,0:T(8,128)(2,1)}, u32[]{:S(2)}, u32[]{:S(2)}) collective-permute-start(bf16[144,2304]{1,0:T(8,128)(2,1)S(1)} %collective-permute-done.33.refs_2_), channel_id=1, source_target_pairs={{0,2},{2,0},{4,6},{6,4},{8,10},{10,8},{12,14},{14,12},{16,18},{18,... | collective-permute-start | bytes 1990664 | tf_op jit(solution)/shard_map/ppermute | solution.py:700
  165.0 32.0 %collective-permute-start.42 = (bf16[144,2304]{1,0:T(8,128)(2,1)S(1)}, bf16[144,2304]{1,0:T(8,128)(2,1)}, u32[]{:S(2)}, u32[]{:S(2)}) collective-permute-start(bf16[144,2304]{1,0:T(8,128)(2,1)S(1)} %collective-permute-done.33.refs_2_), channel_id=1, source_target_pairs={{0,4},{2,6},{4,0},{6,2},{8,12},{10,14},{12,8},{14,10},{16,20},{18,... | collective-permute-start | bytes 1990664 | tf_op jit(solution)/shard_map/ppermute | solution.py:696
  166.2 30.8 %collective-permute-start.45 = (bf16[144,2304]{1,0:T(8,128)(2,1)}, bf16[144,2304]{1,0:T(8,128)(2,1)}, u32[]{:S(2)}, u32[]{:S(2)}) collective-permute-start(bf16[144,2304]{1,0:T(8,128)(2,1)} %copy-done.8), channel_id=1, source_target_pairs={{0,2},{2,0},{4,6},{6,4},{8,10},{10,8},{12,14},{14,12},{16,18},{18,... | collective-permute-start | bytes 1990664 | tf_op jit(solution)/shard_map/ppermute | solution.py:700
  166.2 37.1 %collective-permute-start.43 = (bf16[144,2304]{1,0:T(8,128)(2,1)}, bf16[144,2304]{1,0:T(8,128)(2,1)}, u32[]{:S(2)}, u32[]{:S(2)}) collective-permute-start(bf16[144,2304]{1,0:T(8,128)(2,1)} %copy-done.8), channel_id=1, source_target_pairs={{0,4},{2,6},{4,0},{6,2},{8,12},{10,14},{12,8},{14,10},{16,20},{18,... | collective-permute-start | bytes 1990664 | tf_op jit(solution)/shard_map/ppermute | solution.py:696
  267.8 52.0 %collective-permute-start.49 = (bf16[2,2,4,144,1152]{4,3,2,1,0:T(8,128)(2,1)}, bf16[2,2,4,144,1152]{4,3,2,1,0:T(8,128)(2,1)}, u32[]{:S(2)}, u32[]{:S(2)}) collective-permute-start(bf16[2,2,4,144,1152]{4,3,2,1,0:T(8,128)(2,1)} %get-tuple-element.268), channel_id=1, source_target_pairs={{0,2},{2,0},{4,6},{6,4},{8,10},{10,8},{12,14},{14,12},{16,18},{18,... | collective-permute-start | bytes 15925256 | tf_op jit(solution)/shard_map/ppermute | solution.py:700
  326.8 86.1 %collective-permute-start.51 = (bf16[2,4,144,1152]{3,2,1,0:T(8,128)(2,1)}, bf16[2,4,144,1152]{3,2,1,0:T(8,128)(2,1)}, u32[]{:S(2)}, u32[]{:S(2)}) collective-permute-start(bf16[2,4,144,1152]{3,2,1,0:T(8,128)(2,1)} %get-tuple-element.387), channel_id=1, source_target_pairs={{0,1},{1,0},{2,3},{3,2},{4,5},{5,4},{6,7},{7,6},{8,9},{9,8},{10,11... | collective-permute-start | bytes 7962632 | tf_op jit(solution)/shard_map/ppermute | solution.py:708
  343.6 74.9 %collective-permute-start.52 = (bf16[4,72,4608]{2,1,0:T(8,128)(2,1)}, bf16[4,72,4608]{2,1,0:T(8,128)(2,1)}, u32[]{:S(2)}, u32[]{:S(2)}) collective-permute-start(bf16[4,72,4608]{2,1,0:T(8,128)(2,1)} %get-tuple-element.385), channel_id=1, source_target_pairs={{0,4},{2,6},{4,0},{6,2},{8,12},{10,14},{12,8},{14,10},{16,20},{18,... | collective-permute-start | bytes 7962632 | tf_op jit(solution)/shard_map/ppermute | solution.py:696
  353.8 168.3 %reduce-scatter.5.cloned.1.call-start = ((), (), s32[]{:S(2)}) async-start(), calls=%async_computation.3 | async-start | bytes 3317760 | tf_op jit(solution)/shard_map/reduce_scatter | solution.py:837
  422.5 23.2 %collective-permute-start.53 = (bf16[288,1152]{1,0:T(8,128)(2,1)S(1)}, bf16[288,1152]{1,0:T(8,128)(2,1)S(1)}, u32[]{:S(2)}, u32[]{:S(2)}) collective-permute-start(bf16[288,1152]{1,0:T(8,128)(2,1)S(1)} %slice.229), channel_id=1, source_target_pairs={{0,1},{1,0},{2,3},{3,2},{4,5},{5,4},{6,7},{7,6},{8,9},{9,8},{10,11... | collective-permute-start | bytes 1990664 | tf_op jit(solution)/shard_map/ppermute | solution.py:708
  422.6 23.1 %collective-permute-start.54 = (bf16[2,144,1152]{2,1,0:T(8,128)(2,1)}, bf16[2,144,1152]{2,1,0:T(8,128)(2,1)S(1)}, u32[]{:S(2)}, u32[]{:S(2)}) collective-permute-start(bf16[2,144,1152]{2,1,0:T(8,128)(2,1)} %get-tuple-element.303), channel_id=1, source_target_pairs={{0,4},{2,6},{4,0},{6,2},{8,12},{10,14},{12,8},{14,10},{16,20},{18,... | collective-permute-start | bytes 1990664 | tf_op jit(solution)/shard_map/ppermute | solution.py:696
  445.7 30.5 %collective-permute-start.55 = (bf16[2,4,72,3456]{3,2,1,0:T(8,128)(2,1)}, bf16[2,4,72,3456]{3,2,1,0:T(8,128)(2,1)}, u32[]{:S(2)}, u32[]{:S(2)}) collective-permute-start(bf16[2,4,72,3456]{3,2,1,0:T(8,128)(2,1)} %get-tuple-element.305), channel_id=1, source_target_pairs={{0,2},{2,0},{4,6},{6,4},{8,10},{10,8},{12,14},{14,12},{16,18},{18,... | collective-permute-start | bytes 11943944 | tf_op jit(solution)/shard_map/ppermute | solution.py:700
  463.8 39.1 %collective-permute-start.60 = (bf16[144,1152]{1,0:T(8,128)(2,1)S(1)}, bf16[144,1152]{1,0:T(8,128)(2,1)}, u32[]{:S(2)}, u32[]{:S(2)}) collective-permute-start(bf16[144,1152]{1,0:T(8,128)(2,1)S(1)} %get-tuple-element.404), channel_id=1, source_target_pairs={{0,8},{2,10},{4,12},{6,14},{8,16},{10,18},{12,20},{14,22},{16,24},... | collective-permute-start | bytes 995336 | tf_op jit(solution)/shard_map/ppermute | solution.py:704
  484.2 23.2 %collective-permute-start.57 = (bf16[72,3456]{1,0:T(8,128)(2,1)}, bf16[72,3456]{1,0:T(8,128)(2,1)}, u32[]{:S(2)}, u32[]{:S(2)}) collective-permute-start(bf16[72,3456]{1,0:T(8,128)(2,1)} %get-tuple-element.393), channel_id=1, source_target_pairs={{0,4},{2,6},{4,0},{6,2},{8,12},{10,14},{12,8},{14,10},{16,20},{18,... | collective-permute-start | bytes 1493000 | tf_op jit(solution)/shard_map/ppermute | solution.py:696
  507.3 26.0 %collective-permute-start.63 = (bf16[2,4,144,1152]{3,2,1,0:T(8,128)(2,1)}, bf16[2,4,144,1152]{3,2,1,0:T(8,128)(2,1)}, u32[]{:S(2)}, u32[]{:S(2)}) collective-permute-start(bf16[2,4,144,1152]{3,2,1,0:T(8,128)(2,1)} %copy-done.32), channel_id=1, source_target_pairs={{0,2},{2,0},{4,6},{6,4},{8,10},{10,8},{12,14},{14,12},{16,18},{18,... | collective-permute-start | bytes 7962632 | tf_op jit(solution)/shard_map/ppermute | solution.py:700
  520.7 28.4 %collective-permute-start.68 = (bf16[72,3456]{1,0:T(8,128)(2,1)S(1)}, bf16[72,3456]{1,0:T(8,128)(2,1)}, u32[]{:S(2)}, u32[]{:S(2)}) collective-permute-start(bf16[72,3456]{1,0:T(8,128)(2,1)S(1)} %get-tuple-element.334), channel_id=1, source_target_pairs={{0,4},{2,6},{4,0},{6,2},{8,12},{10,14},{12,8},{14,10},{16,20},{18,... | collective-permute-start | bytes 1493000 | tf_op jit(solution)/shard_map/ppermute | solution.py:696
  537.8 20.7 %collective-permute-start.71 = (bf16[72,4608]{1,0:T(8,128)(2,1)S(1)}, bf16[72,4608]{1,0:T(8,128)(2,1)S(1)}, u32[]{:S(2)}, u32[]{:S(2)}) collective-permute-start(bf16[72,4608]{1,0:T(8,128)(2,1)S(1)} %copy-done.53), channel_id=1, source_target_pairs={{0,1},{1,0},{2,3},{3,2},{4,5},{5,4},{6,7},{7,6},{8,9},{9,8},{10,11... | collective-permute-start | bytes 1990664 | tf_op jit(solution)/shard_map/ppermute | solution.py:708
  (131 other events, 1564.3 us)
Sparse Core Ops, SparseCore 0:
  164.5 90.0 all-gather.1
  353.9 68.6 reduce-scatter.6
  447.6 57.4 reduce-scatter.4
